TPU v7x, 128 devices: a whole 4x4x4 slice. The times are simulated.
128 devices in a mesh: dp: 16 (over x, y_hi, core), seq: 8 (over y_lo, z).
Axes of the slice: x: 4, y: 4 (y_hi: 2, y_lo: 2; y = y_hi * 2 + y_lo), z: 4, core: 2. Of those that a mesh axis runs over, the one named last changes fastest.
Arguments:
- latents: bfloat16 [16, 8, 256, 1152], P('dp', 'seq'), may hold values from -6 to 6
- cotangent: bfloat16 [16, 8, 256, 1152], P('dp', 'seq'), may hold values from -6 to 6
- modulation: float32 [16, 2, 3, 1152], P('dp'), may hold values from -3 to 3
- qk_gains: float32 [2, 2, 72], replicated, may hold values from 0.6 to 2
- spatial_qkv: bfloat16 [1152, 1728], replicated, may hold values from -0.1875 to 0.1875
- spatial_out: bfloat16 [576, 1152], replicated, may hold values from -0.25 to 0.25
- temporal_qkv: bfloat16 [1152, 1728], replicated, may hold values from -0.1875 to 0.1875
- temporal_out: bfloat16 [576, 1152], replicated, may hold values from -0.25 to 0.25
Outputs:
- block_output: bfloat16 [16, 8, 256, 1152], P('dp', 'seq')
- latents_grad: bfloat16 [16, 8, 256, 1152], P('dp', 'seq')
- spatial_qkv_grad: float32 [1152, 1728], P(('dp', 'seq'))
- spatial_out_grad: float32 [576, 1152], P(None, ('dp', 'seq'))
- temporal_qkv_grad: float32 [1152, 1728], P(('dp', 'seq'))
- temporal_out_grad: float32 [576, 1152], P(None, ('dp', 'seq'))
All inputs are finite; a program needn't handle non-finite values.
Results may differ from a plain program's by a relative error of at most 0.035.
Values may be sent and summed in bfloat16 or wider, within the bound.
No kernel may reach another device: no remote copies, remote signals or barrier semaphores. Data moves between devices by JAX's collectives and lax.ppermute only.
A program may use at most 192 MiB of HBM per device.

v0:
```python
import math

import jax
import jax.numpy as jnp
from jax import lax
from jax.experimental import pallas as pl
from jax.experimental.pallas import tpu as pltpu
from jax.sharding import PartitionSpec as P

T = 256
D = 1152
HEADS = 8
HEAD_DIM = 72
A = HEADS * HEAD_DIM
Q = 3 * A
A_PAD = 640
Q_PAD = 1792
COLUMNS = 2 * Q_PAD + 2 * A_PAD
LOCAL = 32
STRIP = 288
EPS = 1e-06
BF = jnp.bfloat16
F32 = jnp.float32
MESH = ("dp", "seq")
MIB = 1024 * 1024
PEERS = (0, 6, 5, 7, 4, 2, 1, 3)


def dot(left, right, over_left, over_right):
    return lax.dot_general(
        left, right, (((over_left,), (over_right,)), ((), ())), preferred_element_type=F32
    )


def call(body, outs, args, cost, scratch=(), limit=16, apart=(), aliases={}):
    shapes, specs = [], []
    for k, (shape, kind, *place) in enumerate(outs):
        if not place:
            shapes.append(pltpu.VMEM(shape, kind))
        elif place[0] == "hbm":
            shapes.append(pltpu.HBM(shape, kind))
        else:
            shapes.append(jax.ShapeDtypeStruct(shape, kind))
        specs.append(pl.BlockSpec(memory_space=pltpu.HBM if place == ["hbm"] else pltpu.VMEM))
    size = sum(x.size * x.dtype.itemsize for x in args)
    size += sum(math.prod(out[0]) * jnp.dtype(out[1]).itemsize for out in outs)
    args = [
        pltpu.with_memory_space_constraint(x, pltpu.HBM) if k in apart else x
        for k, x in enumerate(args)
    ]
    spaces = [pltpu.HBM if k in apart else pltpu.VMEM for k in range(len(args))]
    return pl.pallas_call(
        body,
        out_shape=tuple(shapes),
        in_specs=[pl.BlockSpec(memory_space=space) for space in spaces],
        out_specs=tuple(specs),
        scratch_shapes=list(scratch),
        input_output_aliases=aliases,
        cost_estimate=pl.CostEstimate(
            flops=int(cost * 1.1e9), bytes_accessed=size, transcendentals=0
        ),
        compiler_params=pltpu.CompilerParams(vmem_limit_bytes=limit * MIB),
    )(*args)


def in_order(*values):
    return lax.optimization_barrier(values)


def normalized(x32):
    mean = jnp.mean(x32, axis=-1, keepdims=True)
    centered = x32 - mean
    spread = lax.rsqrt(jnp.mean(centered * centered, axis=-1, keepdims=True) + EPS)
    return centered * spread, spread


def normalized_back(unit, spread, scale, grad):
    grad = grad * (1.0 + scale)
    inner = jnp.mean(grad * unit, axis=-1, keepdims=True)
    return spread * (grad - jnp.mean(grad, axis=-1, keepdims=True) - unit * inner)


def flip(source, target, blocks):
    for b in range(blocks):
        target[128 * b : 128 * b + 128, :] = source[:, 128 * b : 128 * b + 128].T


def flip_back(source, target, blocks):
    for b in range(blocks):
        target[:, 128 * b : 128 * b + 128] = source[128 * b : 128 * b + 128, :].T


def gain_columns(gains, block):
    row = lax.broadcasted_iota(jnp.int32, (HEAD_DIM, HEAD_DIM), 0)
    column = lax.broadcasted_iota(jnp.int32, (HEAD_DIM, HEAD_DIM), 1)
    return tuple(
        jnp.sum(jnp.where(row == column, gains[block, k : k + 1, :], 0.0), axis=1, keepdims=True)
        for k in range(2)
    )


def head_rows(which, h):
    start = which * A + h * HEAD_DIM
    return slice(start, start + HEAD_DIM)


def head_norm(rows, gain):
    root = lax.rsqrt(jnp.mean(rows * rows, axis=0, keepdims=True) + EPS)
    return root, (rows * root * gain).astype(BF)


def head_norm_back(rows, root, gain, grad):
    grad = grad.astype(BF).astype(F32) * gain
    inner = jnp.mean(rows * grad, axis=0, keepdims=True)
    return (root * grad - rows * (root * root * root * inner)).astype(BF).astype(F32)


def same_patch():
    key = lax.broadcasted_iota(jnp.int32, (T, T), 0)
    query = lax.broadcasted_iota(jnp.int32, (T, T), 1)
    return ((key ^ query) & (LOCAL - 1)) == 0


def heads_forward(qkv, pair, mask, probs, result):
    for h in range(HEADS):
        queries = head_norm(qkv[head_rows(0, h), :], pair[0])[1]
        keys = head_norm(qkv[head_rows(1, h), :], pair[1])[1]
        probs[h] = dot(keys, queries, 0, 0)
    for h in range(HEADS):
        scores = probs[h] * HEAD_DIM ** (-0.5)
        if mask is not None:
            scores = jnp.where(mask, scores, -1e30)
        expo = jnp.exp(scores - jnp.max(scores, axis=0, keepdims=True))
        probs[h] = expo * (1.0 / jnp.sum(expo, axis=0, keepdims=True))
    for h in range(HEADS):
        values = qkv[head_rows(2, h), :].astype(BF)
        result[head_rows(0, h), :] = dot(values, probs[h].astype(BF), 1, 0)


def heads_back(qkv, pair, probs, grads, out, work):
    for h in range(HEADS):
        grad = grads[head_rows(0, h), :].astype(BF)
        work[h] = dot(qkv[head_rows(2, h), :].astype(BF), grad, 0, 0).astype(BF)
        out[head_rows(2, h), :] = dot(grad, probs[h].astype(BF), 1, 1).astype(BF).astype(F32)
    for h in range(HEADS):
        prob, p_grad = probs[h], work[h].astype(F32)
        inner = jnp.sum(p_grad * prob, axis=0, keepdims=True)
        work[h] = (prob * (p_grad - inner) * HEAD_DIM ** (-0.5)).astype(BF)
    for h in range(HEADS):
        queries = head_norm(qkv[head_rows(0, h), :], pair[0])[1]
        keys = head_norm(qkv[head_rows(1, h), :], pair[1])[1]
        out[head_rows(0, h), :] = dot(keys, work[h], 1, 0)
        out[head_rows(1, h), :] = dot(queries, work[h], 1, 1)
    for h in range(HEADS):
        for which in range(2):
            rows = head_rows(which, h)
            root = head_norm(qkv[rows, :], pair[which])[0]
            out[rows, :] = head_norm_back(qkv[rows, :], root, pair[which], out[rows, :])


def order(core, chip):
    row = lax.broadcasted_iota(jnp.int32, (A, 1), 0)
    part = (row >= 192).astype(jnp.int32) + (row >= 384).astype(jnp.int32)
    rest = row - 192 * part
    first = (rest * 171) >> 12
    rest = rest - 24 * first
    second = (rest * 11) >> 5
    piece = 3 * part + rest - 3 * second
    place = []
    for axis in range(3):
        step = axis - part
        step = jnp.where(step < 0, step + 3, step)
        one = jnp.where(step == 0, first >> 2, jnp.where(step == 1, first >> 1, first)) & 1
        two = (second >> (2 - axis)) & 1
        near = jnp.where(core == 1, one, two) ^ ((chip[axis] ^ (chip[axis] >> 1)) & 1)
        far = jnp.where(core == 1, two, one) ^ (chip[axis] >> 1)
        place.append(2 * far + (near ^ far))
    x, y, z = place
    device = x * 32 + (y >> 1) * 16 + core * 8 + (y & 1) * 4 + z
    return 9 * device + piece


def position():
    dp, seq = lax.axis_index("dp"), lax.axis_index("seq")
    return dp & 1, (dp >> 2, ((dp >> 1) & 1) * 2 + (seq >> 2), seq & 3)


def picker(core, chip):
    feature = lax.broadcasted_iota(jnp.int32, (A, D), 1)
    return (feature == order(core, chip)).astype(F32).astype(BF)


def pick(hot, source):
    halves = [dot(hot[k : k + STRIP], source, 1, 1).astype(BF) for k in (0, STRIP)]
    return jnp.concatenate(halves, axis=0)


def local_rows(k):
    return pl.ds(pl.multiple_of((lax.axis_index("seq") ^ PEERS[k]) * LOCAL, LOCAL), LOCAL)


def forward_spatial(*refs):
    sources, refs = refs[:7], refs[7:]
    latents, cot, mod, gains, w_qkv, w_out_t, w_out = refs[:7]
    chunks, (both_mid, qkv_t, probs_t, normed, att, scaled_t, flat, tall, both, sems) = refs[7:15], refs[15:]
    loads = {
        k: pltpu.make_async_copy(sources[k], refs[k], sems.at[k]) for k in (0, 1, 2, 3, 5, 6)
    }
    pieces = [
        pltpu.make_async_copy(
            sources[4].at[pl.ds(STRIP * k, STRIP)], w_qkv.at[pl.ds(STRIP * k, STRIP)], sems.at[7 + k]
        )
        for k in range(Q // STRIP)
    ]
    for load in (loads[0], loads[2], loads[3], *pieces, loads[1], loads[5], loads[6]):
        load.start()
    for load in (loads[0], loads[2], loads[3]):
        load.wait()
    unit, _ = normalized(latents[...].astype(F32))
    norm = (unit * (1.0 + mod[1, 0:1, :]) + mod[0, 0:1, :]).astype(BF)
    normed[...] = norm
    for k, load in enumerate(pieces):
        load.wait()
        rows = slice(STRIP * k, STRIP * k + STRIP)
        qkv_t[rows, :] = dot(w_qkv[rows, :], norm, 1, 1).astype(BF).astype(F32)
    tall[A:, :] = jnp.zeros((A_PAD - A, T), F32)
    pair = gain_columns(gains, 0)
    heads_forward(qkv_t, pair, None, probs_t, tall)
    flip_back(tall, flat, A_PAD // 128)
    att[...] = flat[...].astype(BF)
    loads[1].wait()
    scaled = (mod[2, 1:2, :] * cot[...].astype(F32)).astype(BF)
    scaled_t[...] = scaled
    loads[5].wait()
    both[:, D:] = dot(scaled, w_out_t[...], 1, 1).astype(BF)
    loads[6].wait()
    result = dot(att[:, :A], w_out[...], 1, 0)
    mid = (latents[...].astype(F32) + mod[2, 0:1, :] * result).astype(BF)
    both_mid[...] = mid
    both[:, :D] = mid
    for k in range(8):
        chunks[k][...] = both[local_rows(k), :]


def temporal(*refs):
    mod, gains, w_qkv = refs[8:11]
    normed, qkv_grad, tall_qkv, tall_grad, wide, flat, tall, tall_att, both, probs_t, work = refs[19:]
    for k in range(8):
        both[LOCAL * k : LOCAL * k + LOCAL, :] = refs[k][...]
    unit, _ = normalized(both[:, :D].astype(F32))
    norm = (unit * (1.0 + mod[1, 1:2, :]) + mod[0, 1:2, :]).astype(BF)
    normed[...] = norm
    for k in range(Q // STRIP):
        rows = slice(STRIP * k, STRIP * k + STRIP)
        tall_qkv[rows, :] = dot(w_qkv[rows, :], norm, 1, 1).astype(BF).astype(F32)
    flat[:, A:] = jnp.zeros((T, A_PAD - A), F32)
    flat[:, :A] = both[:, D:].astype(F32)
    flip(flat, tall, A_PAD // 128)
    tall_att[A:, :] = jnp.zeros((A_PAD - A, T), F32)
    tall_grad[Q:, :] = jnp.zeros((Q_PAD - Q, T), F32)
    pair = gain_columns(gains, 1)
    heads_forward(tall_qkv, pair, same_patch(), probs_t, tall_att)
    heads_back(tall_qkv, pair, probs_t, tall, tall_grad, work)
    flip_back(tall_att, flat, A_PAD // 128)
    both[:, D:] = flat[:, :A].astype(BF)
    flip_back(tall_grad, wide, Q_PAD // 128)
    qkv_grad[...] = wide[...].astype(BF)
    both[:, :D] = dot(qkv_grad[:, :Q], w_qkv[...], 1, 0).astype(BF)
    for k in range(8):
        refs[11 + k][...] = both[LOCAL * k : LOCAL * k + LOCAL, :]


def pick_early(normed, scaled, w_far, own, other, mine, theirs, w_qkv, sem):
    load = pltpu.make_async_copy(w_far, w_qkv, sem)
    load.start()
    core, chip = position()
    own[...] = picker(core, chip)
    other[...] = picker(1 - core, chip)
    for k, source in enumerate((normed, scaled)):
        rows = slice(k * A, k * A + A)
        theirs[rows, :] = pick(other[...], source[...])
        mine[rows, :] = pick(own[...], source[...])
    load.wait()


def pick_later(source, own, other, mine, theirs):
    theirs[...] = pick(other[...], source[...])
    mine[...] = pick(own[...], source[...])


def enter_spatial_back(*refs):
    mid, cot, mod, w_out, mid_grad, scaled_s, att_grad, att_t, back = refs[8:]
    for k in range(8):
        back[local_rows(k), :] = refs[k][...]
    unit, spread = normalized(mid[...].astype(F32))
    grad = normalized_back(unit, spread, mod[1, 1:2, :], back[:, :D].astype(F32))
    total = (cot[...].astype(F32) + grad).astype(BF)
    mid_grad[...] = total
    scaled = (mod[2, 0:1, :] * total.astype(F32)).astype(BF)
    scaled_s[...] = scaled
    att_grad[:, A:] = jnp.zeros((T, A_PAD - A), F32)
    att_grad[:, :A] = dot(scaled, w_out[...], 1, 1).astype(BF).astype(F32)
    att_t[:, A:] = jnp.zeros((T, A_PAD - A), BF)
    att_t[:, :A] = back[:, D:]


def spatial_attention_back(att_grad, qkv_t, probs_t, gains, qkv_grad, tall_grad, wide, tall, work):
    flip(att_grad, tall, A_PAD // 128)
    tall_grad[Q:, :] = jnp.zeros((Q_PAD - Q, T), F32)
    heads_back(qkv_t, gain_columns(gains, 0), probs_t, tall, tall_grad, work)
    flip_back(tall_grad, wide, Q_PAD // 128)
    qkv_grad[...] = wide[...].astype(BF)


def leave_spatial_back(mid_grad, qkv_grad, latents, mod, w_qkv, latents_grad):
    norm_grad = dot(qkv_grad[:, :Q], w_qkv[...], 1, 0).astype(BF).astype(F32)
    unit, spread = normalized(latents[...].astype(F32))
    grad = normalized_back(unit, spread, mod[1, 0:1, :], norm_grad)
    latents_grad[...] = (mid_grad[...].astype(F32) + grad).astype(BF)


def project_output(mid, att_t, mod, w_out, output):
    result = dot(att_t[:, :A], w_out[...], 1, 0)
    output[...] = (mid[...].astype(F32) + mod[2, 1:2, :] * result).astype(BF)


def weight_rows(groups, start):
    def body(*refs):
        keep, sends = refs[-4], refs[-3:]
        fill(refs, keep, sends, start)

    def fill(refs, keep, sends, start):
        for (left, left_in, row), (right, right_in, column), width in groups:
            lefts = [refs[k][row : row + A, :] for k in (left, left_in)]
            rights = [refs[k][:, column : column + width] for k in (right, right_in)]
            tall_left = jnp.concatenate(lefts, axis=1)
            tall_right = jnp.concatenate(rights, axis=0)
            padded = -(-width // 128) * 128
            for at in range(0, width, 576):
                size = min(576, width - at)
                total = dot(tall_left, tall_right[:, at : at + size], 1, 0)
                for p in range(3):
                    rows = total[192 * p : 192 * p + 192]
                    columns = slice(start + at, start + at + size)
                    keep[p, :, columns] = rows[:96]
                    sends[p][:, columns] = rows[96:].astype(BF)
            if padded > width:
                gap = slice(start + width, start + padded)
                for p in range(3):
                    keep[p, :, gap] = jnp.zeros((96, padded - width), F32)
                    sends[p][:, gap] = jnp.zeros((96, padded - width), BF)
            start += padded

    return body


def first_halve(p):
    def body(keep, got, kept, send):
        total = keep[p] + got[...].astype(F32)
        half = kept.shape[0]
        kept[...] = total[:half]
        send[...] = total[half:].astype(BF)

    return body


def add_halve(keep, got, kept, send):
    half = kept.shape[0]
    total = keep[...] + got[...].astype(F32)
    kept[...] = total[:half]
    send[...] = total[half:].astype(BF)


def cut_pieces(*refs):
    own, sends = refs[6], refs[7:]
    width = refs[0].shape[1]
    for p in range(3):
        total = refs[p][...] + refs[3 + p][...].astype(F32)
        columns = slice(p * width, p * width + width)
        own[:, columns] = total[:3]
        for t in range(1, 8):
            sends[t - 1][:, columns] = total[3 * t : 3 * t + 3].astype(BF)


def last_add(*refs):
    width = refs[0].shape[1] // 3
    start = 0
    for out in refs[8:]:
        size = out.shape[1]
        for p in range(3):
            columns = slice(p * width + start, p * width + start + size)
            rows = refs[0][:, columns]
            for k in range(1, 8):
                rows = rows + refs[k][:, columns].astype(F32)
            out[3 * p : 3 * p + 3, :] = rows
        start += -(-size // 128) * 128


def pairs(change):
    found = []
    for device in range(128):
        dp, seq = divmod(device, 8)
        x, y, z, core = dp >> 2, ((dp >> 1) & 1) * 2 + (seq >> 2), seq & 3, dp & 1
        x, y, z, core = change(x, y, z, core)
        found.append((device, (x * 4 + (y >> 1) * 2 + core) * 8 + (y & 1) * 4 + z))
    return found


def to_other_core(value):
    return lax.ppermute(value, MESH, pairs(lambda x, y, z, c: (x, y, z, 1 - c)))


def along(value, axis):
    def change(x, y, z, core):
        place = [x, y, z]
        place[axis] ^= 1 if core == 1 else 3
        return (*place, core)

    return lax.ppermute(value, MESH, pairs(change))


def to_frame_holders(chunks):
    def step(k):
        return lax.ppermute(chunks[k], MESH, [(d, d ^ PEERS[k]) for d in range(128)])

    return [chunks[0]] + [step(k) for k in range(1, 8)]


def to_owners(pieces):
    def step(t):
        def change(x, y, z, core):
            flip_by = 3 if core == 1 else 1
            return x ^ flip_by * (t >> 2), y ^ flip_by * (t >> 1 & 1), z ^ flip_by * (t & 1), core

        return lax.ppermute(pieces[t - 1], MESH, pairs(change))

    return [step(t) for t in (1, 7, 6, 5, 3, 4, 2)]


def weight_partials(groups, args, before=()):
    cost = sum(group[-1] for group in groups) / 1000
    outs = [((3, 96, COLUMNS), F32)] + [((96, COLUMNS), BF)] * 3
    start = Q_PAD if before else 0
    aliases = {len(args) + k: k for k in range(len(before))}
    return call(weight_rows(groups, start), outs, (*args, *before), cost, aliases=aliases)


def shards(
    latents, cotangent, modulation, qk_gains, spatial_qkv, spatial_out, temporal_qkv, temporal_out
):
    wide, tall_grad = pltpu.VMEM((T, Q_PAD), F32), pltpu.VMEM((Q_PAD, T), F32)
    flat, tall = pltpu.VMEM((T, A_PAD), F32), pltpu.VMEM((A_PAD, T), F32)
    stage, work = pltpu.VMEM((T, D + A), BF), pltpu.VMEM((HEADS, T, T), BF)
    one_block, chunk = ((A, T), BF), ((LOCAL, D + A), BF)

    x, cot, mod, gains, w_qkv_s, w_out_t, w_out_s, *rest = call(
        forward_spatial,
        [
            ((T, D), BF), ((T, D), BF), ((3, 2, D), F32), ((2, 2, HEAD_DIM), F32),
            ((Q, D), BF), ((A, D), BF), ((A, D), BF), *[chunk] * 8,
            ((T, D), BF), ((Q, T), F32), ((HEADS, T, T), F32),
            ((T, D), BF), ((T, A_PAD), BF), ((T, D), BF),
        ],
        (
            latents.reshape(T, D), cotangent.reshape(T, D), modulation[0].transpose(1, 0, 2), qk_gains,
            spatial_qkv.T, temporal_out, spatial_out,
        ),
        10,
        (flat, tall, stage, pltpu.SemaphoreType.DMA((13,))),
        limit=18,
        apart=range(7),
    )
    mid, qkv_t, probs_t, normed_s, att_s, scaled_t = rest[8:]
    patch = to_frame_holders(rest[:8])
    att_s_in = to_other_core(att_s)
    own, other, early_mine, early_theirs, w_qkv_t = call(
        pick_early,
        [((A, D), BF), ((A, D), BF), ((2 * A, T), BF), ((2 * A, T), BF), ((Q, D), BF)],
        (normed_s, scaled_t, temporal_qkv.T),
        2.8,
        (pltpu.SemaphoreType.DMA(()),),
        apart=(2,),
    )
    *patch, early_mine, early_theirs, att_s_in = in_order(
        *patch, early_mine, early_theirs, att_s_in
    )
    early_in = to_other_core(early_theirs)

    *back, normed_t, qkv_grad_t = call(
        temporal,
        [*[chunk] * 8, ((T, D), BF), ((T, Q_PAD), BF)],
        (*patch, mod, gains, w_qkv_t),
        10,
        (
            pltpu.VMEM((Q, T), F32), tall_grad, wide, flat, tall, tall, stage,
            pltpu.VMEM((HEADS, T, T), F32), work,
        ),
        limit=24,
    )
    back = to_frame_holders(back)
    t_mine, t_theirs = call(pick_later, [one_block] * 2, (normed_t, own, other), 1)
    *back, t_theirs, early_theirs, qkv_grad_t = in_order(
        *back, t_theirs, early_theirs, qkv_grad_t
    )
    early_in = to_other_core(early_theirs)
    t_in, qkv_grad_t_in = to_other_core(t_theirs), to_other_core(qkv_grad_t)

    mid_grad, scaled_s, att_grad_s, att_t = call(
        enter_spatial_back,
        [((T, D), BF), ((T, D), BF), ((T, A_PAD), F32), ((T, A_PAD), BF)],
        (*back, mid, cot, mod, w_out_s),
        1.5,
        (stage,),
    )
    att_t_in = to_other_core(att_t)
    (qkv_grad_s,) = call(
        spatial_attention_back,
        [((T, Q_PAD), BF)],
        (att_grad_s, qkv_t, probs_t, gains),
        2.9,
        (tall_grad, wide, tall, work),
    )
    qkv_grad_s, scaled_s, t_in, qkv_grad_t_in, att_t_in = in_order(
        qkv_grad_s, scaled_s, t_in, qkv_grad_t_in, att_t_in
    )
    qkv_grad_s_in = to_other_core(qkv_grad_s)
    late_mine, late_theirs = call(pick_later, [one_block] * 2, (scaled_s, own, other), 1)
    late_in = to_other_core(late_theirs)
    partials = weight_partials(
        (((0, 1, 0), (2, 3, 0), Q),), (t_mine, t_in, qkv_grad_t, qkv_grad_t_in)
    )
    *partials, qkv_grad_s_in, late_in = in_order(*partials, qkv_grad_s_in, late_in)
    keep, *sends = weight_partials(
        (
            ((0, 1, 0), (2, 3, 0), Q), ((0, 1, A), (4, 5, 0), A), ((6, 7, 0), (8, 9, 0), A),
        ),
        (
            early_mine, early_in, qkv_grad_s, qkv_grad_s_in, att_t, att_t_in, late_mine, late_in,
            att_s, att_s_in,
        ),
        partials,
    )
    keep, att_t, mid_grad, *sends = in_order(keep, att_t, mid_grad, *sends)
    got = [along(sends[p], p) for p in range(3)]
    (output,) = call(project_output, [((T, D), BF, "any")], (mid, att_t, mod, w_out_t), 1.5)
    (latents_grad,) = call(
        leave_spatial_back, [((T, D), BF, "any")], (mid_grad, qkv_grad_s, x, mod, w_qkv_s), 2.7
    )
    keep, output, latents_grad = in_order(keep, output, latents_grad)

    kept = []
    for p in range(3):
        mine, send = call(
            first_halve(p), [((48, COLUMNS), F32), ((48, COLUMNS), BF)], (keep, got[p]), 0.2
        )
        kept.append(mine)
        got[p] = along(send, (p + 1) % 3)
    for p in range(3):
        kept[p], send = call(
            add_halve, [((24, COLUMNS), F32), ((24, COLUMNS), BF)], (kept[p], got[p]), 0.2
        )
        got[p] = along(send, (p + 2) % 3)
    own_piece, *pieces = call(
        cut_pieces, [((3, 3 * COLUMNS), F32)] + [((3, 3 * COLUMNS), BF)] * 7, (*kept, *got), 0.5
    )
    tq, sq, to, so = call(
        last_add,
        [((9, Q), F32, "any"), ((9, Q), F32, "any"), ((9, A), F32, "any"), ((9, A), F32, "any")],
        (own_piece, *to_owners(pieces)),
        1,
    )
    shape = (1, 1, T, D)
    return output.reshape(shape), latents_grad.reshape(shape), sq, so.T, tq, to.T


def solution(mesh):
    tokens = P("dp", "seq", None, None)
    rows, cols = P(("dp", "seq"), None), P(None, ("dp", "seq"))
    return jax.shard_map(
        shards,
        mesh=mesh,
        in_specs=(tokens, tokens, P("dp", None, None, None), P(), P(), P(), P(), P()),
        out_specs=(tokens, tokens, rows, cols, rows, cols),
        check_vma=False,
    )
```

profile of v0, /device:TPU:0, one launch (start us, length us, event | category | flops | bytes accessed | tf_op | source)
XLA Modules:
  0.0 114.6 jit_solution(8446897854310390901)
XLA Ops:
  0.6 7.7 %shard_map.127 = (bf16[256,1152]{1,0:T(8,128)(2,1)S(1)}, bf16[256,1152]{1,0:T(8,128)(2,1)S(1)}, f32[3,2,1152]{2,1,0:T(2,128)S(1)}, f32[2,2,72]{2,1,0:T(2,128)S(1...) custom-call(bf16[256,1152]{1,0:T(8,128)(2,1)} %bitcast.13, ...), custom_call_target="tpu_custom_call" | custom-call | flops 11000000512 | bytes 22536448 | tf_op jit(solution)/shard_map/pallas_call | solution.py:52
  8.3 5.0 %collective-permute-start = (bf16[32,1728]{1,0:T(8,128)(2,1)S(1)}, bf16[32,1728]{1,0:T(8,128)(2,1)S(1)}, u32[]{:S(2)}, u32[]{:S(2)}) collective-permute-start(bf16[32,1728]{1,0:T(8,128)(2,1)S(1)} %get-tuple-element.125), channel_id=1, source_target_pairs={{0,6},{1,7},{2,4},{3,5},{4,2},{5,3},{6,0},{7,1},{8,14},{9,15},{10,... | collective-permute-start | bytes 331784 | tf_op jit(solution)/shard_map/ppermute | solution.py:424
  13.4 0.9 collective-permute-start.1
  14.5 1.4 %collective-permute-start.3 = (bf16[32,1728]{1,0:T(8,128)(2,1)S(1)}, bf16[32,1728]{1,0:T(8,128)(2,1)S(1)}, u32[]{:S(2)}, u32[]{:S(2)}) collective-permute-start(bf16[32,1728]{1,0:T(8,128)(2,1)S(1)} %get-tuple-element.128), channel_id=1, source_target_pairs={{0,4},{1,5},{2,6},{3,7},{4,0},{5,1},{6,2},{7,3},{8,12},{9,13},{10,... | collective-permute-start | bytes 331784 | tf_op jit(solution)/shard_map/ppermute | solution.py:424
  15.9 1.1 collective-permute-done.refs_1_
  16.9 3.5 %collective-permute-start.4 = (bf16[32,1728]{1,0:T(8,128)(2,1)S(1)}, bf16[32,1728]{1,0:T(8,128)(2,1)S(1)}, u32[]{:S(2)}, u32[]{:S(2)}) collective-permute-start(bf16[32,1728]{1,0:T(8,128)(2,1)S(1)} %get-tuple-element.129), channel_id=1, source_target_pairs={{0,2},{1,3},{2,0},{3,1},{4,6},{5,7},{6,4},{7,5},{8,10},{9,11},{10,... | collective-permute-start | bytes 331784 | tf_op jit(solution)/shard_map/ppermute | solution.py:424
  20.4 1.0 collective-permute-start.5
  21.5 1.6 %collective-permute-done.2.refs_3_ = bf16[32,1728]{1,0:T(8,128)(2,1)S(1)} collective-permute-done((bf16[32,1728]{1,0:T(8,128)(2,1)S(1)}, bf16[32,1728]{1,0:T(8,128)(2,1)S(1)}, u32[]{:S(2)}, u32[]{:S(2)}) %collective-permute-start.2) | collective-permute-done | bytes 110624 | tf_op jit(solution)/shard_map/ppermute | solution.py:424
  23.1 2.4 %collective-permute-start.6 = (bf16[32,1728]{1,0:T(8,128)(2,1)S(1)}, bf16[32,1728]{1,0:T(8,128)(2,1)S(1)}, u32[]{:S(2)}, u32[]{:S(2)}) collective-permute-start(bf16[32,1728]{1,0:T(8,128)(2,1)S(1)} %get-tuple-element.131), channel_id=1, source_target_pairs={{0,3},{1,2},{2,1},{3,0},{4,7},{5,6},{6,5},{7,4},{8,11},{9,10},{10,... | collective-permute-start | bytes 331784 | tf_op jit(solution)/shard_map/ppermute | solution.py:424
  25.5 2.7 %shard_map.128 = (bf16[576,1152]{1,0:T(8,128)(2,1)S(1)}, bf16[576,1152]{1,0:T(8,128)(2,1)S(1)}, bf16[1152,256]{1,0:T(8,128)(2,1)S(1)}, bf16[1152,256]{1,0:T(8,128)(2,1)S(1)}, bf16[1728,1152]{1,0:T(8,128)(2,1)S(1)}) custom-call(bf16[256,1152]{1,0:T(8,128)(2,1)S(1)} %get-tuple-element.132.normed, bf16[256,1152]{1,0:T(8,128)(2,1)S(1)} %get-tuple-element.133.scaled, ...), custom_call_target="tpu_custom_call" | custom-call | flops 3080000000 | bytes 12976128 | tf_op jit(solution)/shard_map/pallas_call | solution.py:52
  28.2 0.9 collective-permute-done.6.refs_7_
  29.1 5.4 %shard_map.129 = (bf16[32,1728]{1,0:T(8,128)(2,1)S(1)}, bf16[32,1728]{1,0:T(8,128)(2,1)S(1)}, bf16[32,1728]{1,0:T(8,128)(2,1)S(1)}, bf16[32,1728]{1,0:T(8,128)(2...) custom-call(bf16[32,1728]{1,0:T(8,128)(2,1)S(1)} %get-tuple-element., ...), custom_call_target="tpu_custom_call" | custom-call | flops 11000000512 | bytes 7286912 | tf_op jit(solution)/shard_map/pallas_call | solution.py:52
  34.5 2.2 %collective-permute-start.8 = (bf16[32,1728]{1,0:T(8,128)(2,1)S(1)}, bf16[32,1728]{1,0:T(8,128)(2,1)S(1)}, u32[]{:S(2)}, u32[]{:S(2)}) collective-permute-start(bf16[32,1728]{1,0:T(8,128)(2,1)S(1)} %get-tuple-element.150), channel_id=1, source_target_pairs={{0,6},{1,7},{2,4},{3,5},{4,2},{5,3},{6,0},{7,1},{8,14},{9,15},{10,... | collective-permute-start | bytes 331784 | tf_op jit(solution)/shard_map/ppermute | solution.py:424
  36.7 2.0 %collective-permute-start.9 = (bf16[32,1728]{1,0:T(8,128)(2,1)S(1)}, bf16[32,1728]{1,0:T(8,128)(2,1)S(1)}, u32[]{:S(2)}, u32[]{:S(2)}) collective-permute-start(bf16[32,1728]{1,0:T(8,128)(2,1)S(1)} %get-tuple-element.151), channel_id=1, source_target_pairs={{0,5},{1,4},{2,7},{3,6},{4,1},{5,0},{6,3},{7,2},{8,13},{9,12},{10,... | collective-permute-start | bytes 331784 | tf_op jit(solution)/shard_map/ppermute | solution.py:424
  38.7 1.8 %collective-permute-start.10 = (bf16[32,1728]{1,0:T(8,128)(2,1)S(1)}, bf16[32,1728]{1,0:T(8,128)(2,1)S(1)}, u32[]{:S(2)}, u32[]{:S(2)}) collective-permute-start(bf16[32,1728]{1,0:T(8,128)(2,1)S(1)} %get-tuple-element.152), channel_id=1, source_target_pairs={{0,7},{1,6},{2,5},{3,4},{4,3},{5,2},{6,1},{7,0},{8,15},{9,14},{10,... | collective-permute-start | bytes 331784 | tf_op jit(solution)/shard_map/ppermute | solution.py:424
  40.5 0.5 collective-permute-start.11
  41.0 1.4 %collective-permute-start.12 = (bf16[32,1728]{1,0:T(8,128)(2,1)S(1)}, bf16[32,1728]{1,0:T(8,128)(2,1)S(1)}, u32[]{:S(2)}, u32[]{:S(2)}) collective-permute-start(bf16[32,1728]{1,0:T(8,128)(2,1)S(1)} %get-tuple-element.154), channel_id=1, source_target_pairs={{0,2},{1,3},{2,0},{3,1},{4,6},{5,7},{6,4},{7,5},{8,10},{9,11},{10,... | collective-permute-start | bytes 331784 | tf_op jit(solution)/shard_map/ppermute | solution.py:424
  42.5 0.9 collective-permute-done.8.refs_1_
  43.4 0.9 collective-permute-start.13
  44.3 1.1 collective-permute-start.14
  45.4 1.0 shard_map.130
  46.4 1.0 collective-permute-done.12.refs_5_
  47.4 0.9 collective-permute-done.13.refs_6_
  48.3 2.0 %collective-permute-done.14.refs_7_ = bf16[32,1728]{1,0:T(8,128)(2,1)S(1)} collective-permute-done((bf16[32,1728]{1,0:T(8,128)(2,1)S(1)}, bf16[32,1728]{1,0:T(8,128)(2,1)S(1)}, u32[]{:S(2)}, u32[]{:S(2)}) %collective-permute-start.14) | collective-permute-done | bytes 110624 | tf_op jit(solution)/shard_map/ppermute | solution.py:424
  50.3 1.4 %shard_map.131 = (bf16[256,1152]{1,0:T(8,128)(2,1)S(1)}, bf16[256,1152]{1,0:T(8,128)(2,1)S(1)}, f32[256,640]{1,0:T(8,128)S(1)}, bf16[256,640]{1,0:T(8,128)(2,1)S(1)}) custom-call(bf16[32,1728]{1,0:T(8,128)(2,1)S(1)} %get-tuple-element.164.refs_0_, bf16[32,1728]{1,0:T(8,128)(2,1)S(1)} %collective-permute-done.8.refs_1_, ...), custom_call_target="tpu_custom_call" | custom-call | flops 1650000000 | bytes 5581824 | tf_op jit(solution)/shard_map/pallas_call | solution.py:52
  51.7 0.6 collective-permute-start.18
  52.3 0.3 collective-permute-start.16
  52.6 1.9 %shard_map.132.refs_2_.qkv_grad = bf16[256,1792]{1,0:T(8,128)(2,1)S(1)} custom-call(f32[256,640]{1,0:T(8,128)S(1)} %get-tuple-element.175.att_grad, f32[1728,256]{1,0:T(8,128)S(1)} %get-tuple-element.176.qkv_t, f32[8,256,256]{2,1,0:T(8,128)S(1)} %get-tuple-element.177.probs_t, f32[2,2,72]{2,1,0:T(2,128)S(1)} %get-tuple-element.147.refs_9_.gains), custom_call_target="tpu_custom_call" | custom-call | flops 3190000128 | bytes 5440640 | tf_op jit(solution)/shard_map/pallas_call | solution.py:52
  54.6 0.3 collective-permute-start.19
  54.8 0.3 collective-permute-start.15
  55.1 0.9 shard_map.134
  56.1 0.3 collective-permute-start.20
  56.4 1.6 %shard_map.133 = (f32[3,96,4864]{2,1,0:T(8,128)S(1)}, bf16[96,4864]{1,0:T(8,128)(2,1)S(1)}, bf16[96,4864]{1,0:T(8,128)(2,1)S(1)}, bf16[96,4864]{1,0:T(8,128)(2,1)S(1)}) custom-call(bf16[576,256]{1,0:T(8,128)(2,1)S(1)} %get-tuple-element.183.refs_0_, bf16[576,256]{1,0:T(8,128)(2,1)S(1)} %collective-permute-done.16.refs_1_, ...), custom_call_target="tpu_custom_call" | custom-call | flops 1900800000 | bytes 10829824 | tf_op jit(solution)/shard_map/pallas_call | solution.py:52
  57.9 0.4 collective-permute-done.20.refs_7_
  58.4 2.5 %shard_map.135 = (f32[3,96,4864]{2,1,0:T(8,128)S(1)}, bf16[96,4864]{1,0:T(8,128)(2,1)S(1)}, bf16[96,4864]{1,0:T(8,128)(2,1)S(1)}, bf16[96,4864]{1,0:T(8,128)(2,1)S(1)}) custom-call(bf16[1152,256]{1,0:T(8,128)(2,1)S(1)} %get-tuple-element.137.refs_0_, ...), custom_call_target="tpu_custom_call", output_to_operand_aliasing={{0}: (10, {}), {1}: (11, {}), {2}: (12, {}), {3}: (13, {})} | custom-call | flops 3168000000 | bytes 21725184 | tf_op jit(solution)/shard_map/pallas_call | solution.py:52
  60.9 2.8 %collective-permute-start.21 = (bf16[96,4864]{1,0:T(8,128)(2,1)S(1)}, bf16[96,4864]{1,0:T(8,128)(2,1)S(1)}, u32[]{:S(2)}, u32[]{:S(2)}) collective-permute-start(bf16[96,4864]{1,0:T(8,128)(2,1)S(1)} %get-tuple-element.215), channel_id=1, source_target_pairs={{0,96},{1,97},{2,98},{3,99},{4,100},{5,101},{6,102},{7,103},{8,40}... | collective-permute-start | bytes 2801672 | tf_op jit(solution)/shard_map/ppermute | solution.py:419
  63.7 3.1 %collective-permute-start.23 = (bf16[96,4864]{1,0:T(8,128)(2,1)S(1)}, bf16[96,4864]{1,0:T(8,128)(2,1)S(1)}, u32[]{:S(2)}, u32[]{:S(2)}) collective-permute-start(bf16[96,4864]{1,0:T(8,128)(2,1)S(1)} %get-tuple-element.219), channel_id=1, source_target_pairs={{0,20},{1,21},{2,22},{3,23},{4,16},{5,17},{6,18},{7,19},{8,12},{9,... | collective-permute-start | bytes 2801672 | tf_op jit(solution)/shard_map/ppermute | solution.py:419
  66.8 0.7 collective-permute-start.25
  67.5 1.5 %shard_map.136 = bf16[256,1152]{1,0:T(8,128)(2,1)} custom-call(bf16[256,1152]{1,0:T(8,128)(2,1)S(1)} %get-tuple-element.172.refs_8_.mid, bf16[256,640]{1,0:T(8,128)(2,1)S(1)} %get-tuple-element.207.refs_4_.att_t, f32[3,2,1152]{2,1,0:T(2,128)S(1)} %get-tuple-element.146.refs_8_.refs_10_.mod, bf16[576,1152]{1,0:T(8,128)(2,1)S(1)} %get-tuple-element.208.w_out), custom_call_target="tpu_custom_call" | custom-call | flops 1650000000 | bytes 2862080 | tf_op jit(solution)/shard_map/pallas_call | solution.py:52
  69.0 2.6 %shard_map.137 = bf16[256,1152]{1,0:T(8,128)(2,1)} custom-call(bf16[256,1152]{1,0:T(8,128)(2,1)S(1)} %get-tuple-element.209.mid_grad, bf16[256,1792]{1,0:T(8,128)(2,1)S(1)} %shard_map.132.refs_2_.qkv_grad, bf16[256,1152]{1,0:T(8,128)(2,1)S(1)} %get-tuple-element.210.latents, f32[3,2,1152]{2,1,0:T(2,128)S(1)} %get-tuple-element.146.refs_8_.refs_10_.mod, ...), custom_call_target="tpu_custom_call" | custom-call | flops 2969999872 | bytes 6695936 | tf_op jit(solution)/shard_map/pallas_call | solution.py:52
  71.6 4.2 %collective-permute-done.21.got = bf16[96,4864]{1,0:T(8,128)(2,1)S(1)} collective-permute-done((bf16[96,4864]{1,0:T(8,128)(2,1)S(1)}, bf16[96,4864]{1,0:T(8,128)(2,1)S(1)}, u32[]{:S(2)}, u32[]{:S(2)}) %collective-permute-start.21) | collective-permute-done | bytes 933920 | tf_op jit(solution)/shard_map/ppermute | solution.py:419
  75.7 0.2 shard_map.138
  76.0 3.2 %collective-permute-start.22 = (bf16[48,4864]{1,0:T(8,128)(2,1)S(1)}, bf16[48,4864]{1,0:T(8,128)(2,1)S(1)}, u32[]{:S(2)}, u32[]{:S(2)}) collective-permute-start(bf16[48,4864]{1,0:T(8,128)(2,1)S(1)} %get-tuple-element.217), channel_id=1, source_target_pairs={{0,20},{1,21},{2,22},{3,23},{4,16},{5,17},{6,18},{7,19},{8,12},{9,... | collective-permute-start | bytes 1400840 | tf_op jit(solution)/shard_map/ppermute | solution.py:419
  79.2 0.2 shard_map.140
  79.4 0.8 collective-permute-start.24
  80.2 1.4 %collective-permute-done.25.got = bf16[96,4864]{1,0:T(8,128)(2,1)S(1)} collective-permute-done((bf16[96,4864]{1,0:T(8,128)(2,1)S(1)}, bf16[96,4864]{1,0:T(8,128)(2,1)S(1)}, u32[]{:S(2)}, u32[]{:S(2)}) %collective-permute-start.25) | collective-permute-done | bytes 933920 | tf_op jit(solution)/shard_map/ppermute | solution.py:419
  81.6 0.2 shard_map.142
  81.8 1.4 %collective-permute-start.26 = (bf16[48,4864]{1,0:T(8,128)(2,1)S(1)}, bf16[48,4864]{1,0:T(8,128)(2,1)S(1)}, u32[]{:S(2)}, u32[]{:S(2)}) collective-permute-start(bf16[48,4864]{1,0:T(8,128)(2,1)S(1)} %get-tuple-element.225), channel_id=1, source_target_pairs={{0,96},{1,97},{2,98},{3,99},{4,100},{5,101},{6,102},{7,103},{8,40}... | collective-permute-start | bytes 1400840 | tf_op jit(solution)/shard_map/ppermute | solution.py:419
  83.2 2.6 %collective-permute-done.22.got = bf16[48,4864]{1,0:T(8,128)(2,1)S(1)} collective-permute-done((bf16[48,4864]{1,0:T(8,128)(2,1)S(1)}, bf16[48,4864]{1,0:T(8,128)(2,1)S(1)}, u32[]{:S(2)}, u32[]{:S(2)}) %collective-permute-start.22) | collective-permute-done | bytes 466976 | tf_op jit(solution)/shard_map/ppermute | solution.py:419
  85.9 1.2 %collective-permute-start.27 = (bf16[24,4864]{1,0:T(8,128)(2,1)S(1)}, bf16[24,4864]{1,0:T(8,128)(2,1)S(1)}, u32[]{:S(2)}, u32[]{:S(2)}) collective-permute-start(bf16[24,4864]{1,0:T(8,128)(2,1)S(1)} %get-tuple-element.227), channel_id=1, source_target_pairs={{0,3},{1,2},{2,1},{3,0},{4,7},{5,6},{6,5},{7,4},{8,9},{9,8},{10,11... | collective-permute-start | bytes 700424 | tf_op jit(solution)/shard_map/ppermute | solution.py:419
  87.1 2.1 %collective-permute-done.24.got = bf16[48,4864]{1,0:T(8,128)(2,1)S(1)} collective-permute-done((bf16[48,4864]{1,0:T(8,128)(2,1)S(1)}, bf16[48,4864]{1,0:T(8,128)(2,1)S(1)}, u32[]{:S(2)}, u32[]{:S(2)}) %collective-permute-start.24) | collective-permute-done | bytes 466976 | tf_op jit(solution)/shard_map/ppermute | solution.py:419
  89.3 2.8 %collective-permute-start.28 = (bf16[24,4864]{1,0:T(8,128)(2,1)S(1)}, bf16[24,4864]{1,0:T(8,128)(2,1)S(1)}, u32[]{:S(2)}, u32[]{:S(2)}) collective-permute-start(bf16[24,4864]{1,0:T(8,128)(2,1)S(1)} %get-tuple-element.228), channel_id=1, source_target_pairs={{0,96},{1,97},{2,98},{3,99},{4,100},{5,101},{6,102},{7,103},{8,40}... | collective-permute-start | bytes 700424 | tf_op jit(solution)/shard_map/ppermute | solution.py:419
  92.3 0.9 collective-permute-start.29
  93.3 3.4 %collective-permute-done.28.refs_4_ = bf16[24,4864]{1,0:T(8,128)(2,1)S(1)} collective-permute-done((bf16[24,4864]{1,0:T(8,128)(2,1)S(1)}, bf16[24,4864]{1,0:T(8,128)(2,1)S(1)}, u32[]{:S(2)}, u32[]{:S(2)}) %collective-permute-start.28) | collective-permute-done | bytes 233504 | tf_op jit(solution)/shard_map/ppermute | solution.py:419
  96.7 4.5 %collective-permute-done.29.refs_5_ = bf16[24,4864]{1,0:T(8,128)(2,1)S(1)} collective-permute-done((bf16[24,4864]{1,0:T(8,128)(2,1)S(1)}, bf16[24,4864]{1,0:T(8,128)(2,1)S(1)}, u32[]{:S(2)}, u32[]{:S(2)}) %collective-permute-start.29) | collective-permute-done | bytes 233504 | tf_op jit(solution)/shard_map/ppermute | solution.py:419
  101.1 0.4 shard_map.144
  101.7 4.3 %collective-permute-start.32 = (bf16[3,14592]{1,0:T(4,128)(2,1)S(1)}, bf16[3,14592]{1,0:T(4,128)(2,1)S(1)}, u32[]{:S(2)}, u32[]{:S(2)}) collective-permute-start(bf16[3,14592]{1,0:T(4,128)(2,1)S(1)} %get-tuple-element.233), channel_id=1, source_target_pairs={{0,36},{1,37},{2,38},{3,39},{4,32},{5,33},{6,34},{7,35},{8,124},{9... | collective-permute-start | bytes 262664 | tf_op jit(solution)/shard_map/ppermute | solution.py:435
  106.0 1.5 %collective-permute-start.34 = (bf16[3,14592]{1,0:T(4,128)(2,1)S(1)}, bf16[3,14592]{1,0:T(4,128)(2,1)S(1)}, u32[]{:S(2)}, u32[]{:S(2)}) collective-permute-start(bf16[3,14592]{1,0:T(4,128)(2,1)S(1)} %get-tuple-element.235), channel_id=1, source_target_pairs={{0,5},{1,4},{2,7},{3,6},{4,1},{5,0},{6,3},{7,2},{8,31},{9,30},{10,... | collective-permute-start | bytes 262664 | tf_op jit(solution)/shard_map/ppermute | solution.py:435
  107.5 0.3 collective-permute-start.35
  107.8 0.5 collective-permute-done.31.refs_2_
  108.3 2.6 %collective-permute-start.36 = (bf16[3,14592]{1,0:T(4,128)(2,1)S(1)}, bf16[3,14592]{1,0:T(4,128)(2,1)S(1)}, u32[]{:S(2)}, u32[]{:S(2)}) collective-permute-start(bf16[3,14592]{1,0:T(4,128)(2,1)S(1)} %get-tuple-element.237), channel_id=1, source_target_pairs={{0,4},{1,5},{2,6},{3,7},{4,0},{5,1},{6,2},{7,3},{8,28},{9,29},{10,... | collective-permute-start | bytes 262664 | tf_op jit(solution)/shard_map/ppermute | solution.py:435
  111.0 2.0 %collective-permute-done.33.refs_4_ = bf16[3,14592]{1,0:T(4,128)(2,1)S(1)} collective-permute-done((bf16[3,14592]{1,0:T(4,128)(2,1)S(1)}, bf16[3,14592]{1,0:T(4,128)(2,1)S(1)}, u32[]{:S(2)}, u32[]{:S(2)}) %collective-permute-start.33) | collective-permute-done | bytes 87584 | tf_op jit(solution)/shard_map/ppermute | solution.py:435
  113.0 0.8 collective-permute-done.36.refs_7_
  113.8 0.8 shard_map.145
  (29 shorter events, 0.8 us)
Async XLA Ops:
  8.3 8.6 %collective-permute-start = (bf16[32,1728]{1,0:T(8,128)(2,1)S(1)}, bf16[32,1728]{1,0:T(8,128)(2,1)S(1)}, u32[]{:S(2)}, u32[]{:S(2)}) collective-permute-start(bf16[32,1728]{1,0:T(8,128)(2,1)S(1)} %get-tuple-element.125), channel_id=1, source_target_pairs={{0,6},{1,7},{2,4},{3,5},{4,2},{5,3},{6,0},{7,1},{8,14},{9,15},{10,... | collective-permute-start | bytes 331784 | tf_op jit(solution)/shard_map/ppermute | solution.py:424
  13.4 7.0 %collective-permute-start.1 = (bf16[32,1728]{1,0:T(8,128)(2,1)S(1)}, bf16[32,1728]{1,0:T(8,128)(2,1)S(1)}, u32[]{:S(2)}, u32[]{:S(2)}) collective-permute-start(bf16[32,1728]{1,0:T(8,128)(2,1)S(1)} %get-tuple-element.126), channel_id=1, source_target_pairs={{0,5},{1,4},{2,7},{3,6},{4,1},{5,0},{6,3},{7,2},{8,13},{9,12},{10,... | collective-permute-start | bytes 331784 | tf_op jit(solution)/shard_map/ppermute | solution.py:424
  14.3 8.8 %collective-permute-start.2 = (bf16[32,1728]{1,0:T(8,128)(2,1)S(1)}, bf16[32,1728]{1,0:T(8,128)(2,1)S(1)}, u32[]{:S(2)}, u32[]{:S(2)}) collective-permute-start(bf16[32,1728]{1,0:T(8,128)(2,1)S(1)} %get-tuple-element.127), channel_id=1, source_target_pairs={{0,7},{1,6},{2,5},{3,4},{4,3},{5,2},{6,1},{7,0},{8,15},{9,14},{10,... | collective-permute-start | bytes 331784 | tf_op jit(solution)/shard_map/ppermute | solution.py:424
  14.5 14.6 %collective-permute-start.7 = (bf16[256,640]{1,0:T(8,128)(2,1)S(1)}, bf16[256,640]{1,0:T(8,128)(2,1)S(1)}, u32[]{:S(2)}, u32[]{:S(2)}) collective-permute-start(bf16[256,640]{1,0:T(8,128)(2,1)S(1)} %get-tuple-element.136.refs_8_), channel_id=1, source_target_pairs={{0,8},{1,9},{2,10},{3,11},{4,12},{5,13},{6,14},{7,15},{8,0},{9,1},... | collective-permute-start | bytes 983048 | tf_op jit(solution)/shard_map/ppermute | solution.py:410
  14.5 13.7 %collective-permute-start.3 = (bf16[32,1728]{1,0:T(8,128)(2,1)S(1)}, bf16[32,1728]{1,0:T(8,128)(2,1)S(1)}, u32[]{:S(2)}, u32[]{:S(2)}) collective-permute-start(bf16[32,1728]{1,0:T(8,128)(2,1)S(1)} %get-tuple-element.128), channel_id=1, source_target_pairs={{0,4},{1,5},{2,6},{3,7},{4,0},{5,1},{6,2},{7,3},{8,12},{9,13},{10,... | collective-permute-start | bytes 331784 | tf_op jit(solution)/shard_map/ppermute | solution.py:424
  16.9 11.3 %collective-permute-start.4 = (bf16[32,1728]{1,0:T(8,128)(2,1)S(1)}, bf16[32,1728]{1,0:T(8,128)(2,1)S(1)}, u32[]{:S(2)}, u32[]{:S(2)}) collective-permute-start(bf16[32,1728]{1,0:T(8,128)(2,1)S(1)} %get-tuple-element.129), channel_id=1, source_target_pairs={{0,2},{1,3},{2,0},{3,1},{4,6},{5,7},{6,4},{7,5},{8,10},{9,11},{10,... | collective-permute-start | bytes 331784 | tf_op jit(solution)/shard_map/ppermute | solution.py:424
  20.4 7.8 %collective-permute-start.5 = (bf16[32,1728]{1,0:T(8,128)(2,1)S(1)}, bf16[32,1728]{1,0:T(8,128)(2,1)S(1)}, u32[]{:S(2)}, u32[]{:S(2)}) collective-permute-start(bf16[32,1728]{1,0:T(8,128)(2,1)S(1)} %get-tuple-element.130), channel_id=1, source_target_pairs={{0,1},{1,0},{2,3},{3,2},{4,5},{5,4},{6,7},{7,6},{8,9},{9,8},{10,11... | collective-permute-start | bytes 331784 | tf_op jit(solution)/shard_map/ppermute | solution.py:424
  23.1 6.0 %collective-permute-start.6 = (bf16[32,1728]{1,0:T(8,128)(2,1)S(1)}, bf16[32,1728]{1,0:T(8,128)(2,1)S(1)}, u32[]{:S(2)}, u32[]{:S(2)}) collective-permute-start(bf16[32,1728]{1,0:T(8,128)(2,1)S(1)} %get-tuple-element.131), channel_id=1, source_target_pairs={{0,3},{1,2},{2,1},{3,0},{4,7},{5,6},{6,5},{7,4},{8,11},{9,10},{10,... | collective-permute-start | bytes 331784 | tf_op jit(solution)/shard_map/ppermute | solution.py:424
  34.5 8.9 %collective-permute-start.8 = (bf16[32,1728]{1,0:T(8,128)(2,1)S(1)}, bf16[32,1728]{1,0:T(8,128)(2,1)S(1)}, u32[]{:S(2)}, u32[]{:S(2)}) collective-permute-start(bf16[32,1728]{1,0:T(8,128)(2,1)S(1)} %get-tuple-element.150), channel_id=1, source_target_pairs={{0,6},{1,7},{2,4},{3,5},{4,2},{5,3},{6,0},{7,1},{8,14},{9,15},{10,... | collective-permute-start | bytes 331784 | tf_op jit(solution)/shard_map/ppermute | solution.py:424
  36.7 7.6 %collective-permute-start.9 = (bf16[32,1728]{1,0:T(8,128)(2,1)S(1)}, bf16[32,1728]{1,0:T(8,128)(2,1)S(1)}, u32[]{:S(2)}, u32[]{:S(2)}) collective-permute-start(bf16[32,1728]{1,0:T(8,128)(2,1)S(1)} %get-tuple-element.151), channel_id=1, source_target_pairs={{0,5},{1,4},{2,7},{3,6},{4,1},{5,0},{6,3},{7,2},{8,13},{9,12},{10,... | collective-permute-start | bytes 331784 | tf_op jit(solution)/shard_map/ppermute | solution.py:424
  38.7 7.6 %collective-permute-start.10 = (bf16[32,1728]{1,0:T(8,128)(2,1)S(1)}, bf16[32,1728]{1,0:T(8,128)(2,1)S(1)}, u32[]{:S(2)}, u32[]{:S(2)}) collective-permute-start(bf16[32,1728]{1,0:T(8,128)(2,1)S(1)} %get-tuple-element.152), channel_id=1, source_target_pairs={{0,7},{1,6},{2,5},{3,4},{4,3},{5,2},{6,1},{7,0},{8,15},{9,14},{10,... | collective-permute-start | bytes 331784 | tf_op jit(solution)/shard_map/ppermute | solution.py:424
  40.5 5.9 %collective-permute-start.11 = (bf16[32,1728]{1,0:T(8,128)(2,1)S(1)}, bf16[32,1728]{1,0:T(8,128)(2,1)S(1)}, u32[]{:S(2)}, u32[]{:S(2)}) collective-permute-start(bf16[32,1728]{1,0:T(8,128)(2,1)S(1)} %get-tuple-element.153), channel_id=1, source_target_pairs={{0,4},{1,5},{2,6},{3,7},{4,0},{5,1},{6,2},{7,3},{8,12},{9,13},{10,... | collective-permute-start | bytes 331784 | tf_op jit(solution)/shard_map/ppermute | solution.py:424
  41.0 6.4 %collective-permute-start.12 = (bf16[32,1728]{1,0:T(8,128)(2,1)S(1)}, bf16[32,1728]{1,0:T(8,128)(2,1)S(1)}, u32[]{:S(2)}, u32[]{:S(2)}) collective-permute-start(bf16[32,1728]{1,0:T(8,128)(2,1)S(1)} %get-tuple-element.154), channel_id=1, source_target_pairs={{0,2},{1,3},{2,0},{3,1},{4,6},{5,7},{6,4},{7,5},{8,10},{9,11},{10,... | collective-permute-start | bytes 331784 | tf_op jit(solution)/shard_map/ppermute | solution.py:424
  43.4 4.9 %collective-permute-start.13 = (bf16[32,1728]{1,0:T(8,128)(2,1)S(1)}, bf16[32,1728]{1,0:T(8,128)(2,1)S(1)}, u32[]{:S(2)}, u32[]{:S(2)}) collective-permute-start(bf16[32,1728]{1,0:T(8,128)(2,1)S(1)} %get-tuple-element.155), channel_id=1, source_target_pairs={{0,1},{1,0},{2,3},{3,2},{4,5},{5,4},{6,7},{7,6},{8,9},{9,8},{10,11... | collective-permute-start | bytes 331784 | tf_op jit(solution)/shard_map/ppermute | solution.py:424
  44.3 6.0 %collective-permute-start.14 = (bf16[32,1728]{1,0:T(8,128)(2,1)S(1)}, bf16[32,1728]{1,0:T(8,128)(2,1)S(1)}, u32[]{:S(2)}, u32[]{:S(2)}) collective-permute-start(bf16[32,1728]{1,0:T(8,128)(2,1)S(1)} %get-tuple-element.156), channel_id=1, source_target_pairs={{0,3},{1,2},{2,1},{3,0},{4,7},{5,6},{6,5},{7,4},{8,11},{9,10},{10,... | collective-permute-start | bytes 331784 | tf_op jit(solution)/shard_map/ppermute | solution.py:424
  50.3 4.3 %collective-permute-start.17 = (bf16[256,1792]{1,0:T(8,128)(2,1)S(1)}, bf16[256,1792]{1,0:T(8,128)(2,1)S(1)}, u32[]{:S(2)}, u32[]{:S(2)}) collective-permute-start(bf16[256,1792]{1,0:T(8,128)(2,1)S(1)} %get-tuple-element.180.refs_2_), channel_id=1, source_target_pairs={{0,8},{1,9},{2,10},{3,11},{4,12},{5,13},{6,14},{7,15},{8,0},{9,1},... | collective-permute-start | bytes 2752520 | tf_op jit(solution)/shard_map/ppermute | solution.py:410
  51.7 2.9 %collective-permute-start.18 = (bf16[256,640]{1,0:T(8,128)(2,1)S(1)}, bf16[256,640]{1,0:T(8,128)(2,1)S(1)}, u32[]{:S(2)}, u32[]{:S(2)}) collective-permute-start(bf16[256,640]{1,0:T(8,128)(2,1)S(1)} %get-tuple-element.207.refs_4_.att_t), channel_id=1, source_target_pairs={{0,8},{1,9},{2,10},{3,11},{4,12},{5,13},{6,14},{7,15},{8,0},{9,1},... | collective-permute-start | bytes 983048 | tf_op jit(solution)/shard_map/ppermute | solution.py:410
  52.3 2.3 %collective-permute-start.16 = (bf16[576,256]{1,0:T(8,128)(2,1)S(1)}, bf16[576,256]{1,0:T(8,128)(2,1)S(1)}, u32[]{:S(2)}, u32[]{:S(2)}) collective-permute-start(bf16[576,256]{1,0:T(8,128)(2,1)S(1)} %get-tuple-element.179), channel_id=1, source_target_pairs={{0,8},{1,9},{2,10},{3,11},{4,12},{5,13},{6,14},{7,15},{8,0},{9,1},... | collective-permute-start | bytes 884744 | tf_op jit(solution)/shard_map/ppermute | solution.py:410
  54.6 3.8 %collective-permute-start.19 = (bf16[256,1792]{1,0:T(8,128)(2,1)S(1)}, bf16[256,1792]{1,0:T(8,128)(2,1)S(1)}, u32[]{:S(2)}, u32[]{:S(2)}) collective-permute-start(bf16[256,1792]{1,0:T(8,128)(2,1)S(1)} %shard_map.132.refs_2_.qkv_grad), channel_id=1, source_target_pairs={{0,8},{1,9},{2,10},{3,11},{4,12},{5,13},{6,14},{7,15},{8,0},{9,1},... | collective-permute-start | bytes 2752520 | tf_op jit(solution)/shard_map/ppermute | solution.py:410
  54.8 3.5 %collective-permute-start.15 = (bf16[1152,256]{1,0:T(8,128)(2,1)S(1)}, bf16[1152,256]{1,0:T(8,128)(2,1)S(1)}, u32[]{:S(2)}, u32[]{:S(2)}) collective-permute-start(bf16[1152,256]{1,0:T(8,128)(2,1)S(1)} %get-tuple-element.163), channel_id=1, source_target_pairs={{0,8},{1,9},{2,10},{3,11},{4,12},{5,13},{6,14},{7,15},{8,0},{9,1},... | collective-permute-start | bytes 1769480 | tf_op jit(solution)/shard_map/ppermute | solution.py:410
  56.1 2.3 %collective-permute-start.20 = (bf16[576,256]{1,0:T(8,128)(2,1)S(1)}, bf16[576,256]{1,0:T(8,128)(2,1)S(1)}, u32[]{:S(2)}, u32[]{:S(2)}) collective-permute-start(bf16[576,256]{1,0:T(8,128)(2,1)S(1)} %get-tuple-element.191), channel_id=1, source_target_pairs={{0,8},{1,9},{2,10},{3,11},{4,12},{5,13},{6,14},{7,15},{8,0},{9,1},... | collective-permute-start | bytes 884744 | tf_op jit(solution)/shard_map/ppermute | solution.py:410
  60.9 14.9 %collective-permute-start.21 = (bf16[96,4864]{1,0:T(8,128)(2,1)S(1)}, bf16[96,4864]{1,0:T(8,128)(2,1)S(1)}, u32[]{:S(2)}, u32[]{:S(2)}) collective-permute-start(bf16[96,4864]{1,0:T(8,128)(2,1)S(1)} %get-tuple-element.215), channel_id=1, source_target_pairs={{0,96},{1,97},{2,98},{3,99},{4,100},{5,101},{6,102},{7,103},{8,40}... | collective-permute-start | bytes 2801672 | tf_op jit(solution)/shard_map/ppermute | solution.py:419
  63.7 15.4 %collective-permute-start.23 = (bf16[96,4864]{1,0:T(8,128)(2,1)S(1)}, bf16[96,4864]{1,0:T(8,128)(2,1)S(1)}, u32[]{:S(2)}, u32[]{:S(2)}) collective-permute-start(bf16[96,4864]{1,0:T(8,128)(2,1)S(1)} %get-tuple-element.219), channel_id=1, source_target_pairs={{0,20},{1,21},{2,22},{3,23},{4,16},{5,17},{6,18},{7,19},{8,12},{9,... | collective-permute-start | bytes 2801672 | tf_op jit(solution)/shard_map/ppermute | solution.py:419
  66.8 14.8 %collective-permute-start.25 = (bf16[96,4864]{1,0:T(8,128)(2,1)S(1)}, bf16[96,4864]{1,0:T(8,128)(2,1)S(1)}, u32[]{:S(2)}, u32[]{:S(2)}) collective-permute-start(bf16[96,4864]{1,0:T(8,128)(2,1)S(1)} %get-tuple-element.223), channel_id=1, source_target_pairs={{0,3},{1,2},{2,1},{3,0},{4,7},{5,6},{6,5},{7,4},{8,9},{9,8},{10,11... | collective-permute-start | bytes 2801672 | tf_op jit(solution)/shard_map/ppermute | solution.py:419
  76.0 9.9 %collective-permute-start.22 = (bf16[48,4864]{1,0:T(8,128)(2,1)S(1)}, bf16[48,4864]{1,0:T(8,128)(2,1)S(1)}, u32[]{:S(2)}, u32[]{:S(2)}) collective-permute-start(bf16[48,4864]{1,0:T(8,128)(2,1)S(1)} %get-tuple-element.217), channel_id=1, source_target_pairs={{0,20},{1,21},{2,22},{3,23},{4,16},{5,17},{6,18},{7,19},{8,12},{9,... | collective-permute-start | bytes 1400840 | tf_op jit(solution)/shard_map/ppermute | solution.py:419
  79.4 9.9 %collective-permute-start.24 = (bf16[48,4864]{1,0:T(8,128)(2,1)S(1)}, bf16[48,4864]{1,0:T(8,128)(2,1)S(1)}, u32[]{:S(2)}, u32[]{:S(2)}) collective-permute-start(bf16[48,4864]{1,0:T(8,128)(2,1)S(1)} %get-tuple-element.221), channel_id=1, source_target_pairs={{0,3},{1,2},{2,1},{3,0},{4,7},{5,6},{6,5},{7,4},{8,9},{9,8},{10,11... | collective-permute-start | bytes 1400840 | tf_op jit(solution)/shard_map/ppermute | solution.py:419
  81.8 10.3 %collective-permute-start.26 = (bf16[48,4864]{1,0:T(8,128)(2,1)S(1)}, bf16[48,4864]{1,0:T(8,128)(2,1)S(1)}, u32[]{:S(2)}, u32[]{:S(2)}) collective-permute-start(bf16[48,4864]{1,0:T(8,128)(2,1)S(1)} %get-tuple-element.225), channel_id=1, source_target_pairs={{0,96},{1,97},{2,98},{3,99},{4,100},{5,101},{6,102},{7,103},{8,40}... | collective-permute-start | bytes 1400840 | tf_op jit(solution)/shard_map/ppermute | solution.py:419
  85.9 7.4 %collective-permute-start.27 = (bf16[24,4864]{1,0:T(8,128)(2,1)S(1)}, bf16[24,4864]{1,0:T(8,128)(2,1)S(1)}, u32[]{:S(2)}, u32[]{:S(2)}) collective-permute-start(bf16[24,4864]{1,0:T(8,128)(2,1)S(1)} %get-tuple-element.227), channel_id=1, source_target_pairs={{0,3},{1,2},{2,1},{3,0},{4,7},{5,6},{6,5},{7,4},{8,9},{9,8},{10,11... | collective-permute-start | bytes 700424 | tf_op jit(solution)/shard_map/ppermute | solution.py:419
  89.3 7.4 %collective-permute-start.28 = (bf16[24,4864]{1,0:T(8,128)(2,1)S(1)}, bf16[24,4864]{1,0:T(8,128)(2,1)S(1)}, u32[]{:S(2)}, u32[]{:S(2)}) collective-permute-start(bf16[24,4864]{1,0:T(8,128)(2,1)S(1)} %get-tuple-element.228), channel_id=1, source_target_pairs={{0,96},{1,97},{2,98},{3,99},{4,100},{5,101},{6,102},{7,103},{8,40}... | collective-permute-start | bytes 700424 | tf_op jit(solution)/shard_map/ppermute | solution.py:419
  92.3 8.9 %collective-permute-start.29 = (bf16[24,4864]{1,0:T(8,128)(2,1)S(1)}, bf16[24,4864]{1,0:T(8,128)(2,1)S(1)}, u32[]{:S(2)}, u32[]{:S(2)}) collective-permute-start(bf16[24,4864]{1,0:T(8,128)(2,1)S(1)} %get-tuple-element.229), channel_id=1, source_target_pairs={{0,20},{1,21},{2,22},{3,23},{4,16},{5,17},{6,18},{7,19},{8,12},{9,... | collective-permute-start | bytes 700424 | tf_op jit(solution)/shard_map/ppermute | solution.py:419
  101.6 5.9 %collective-permute-start.30 = (bf16[3,14592]{1,0:T(4,128)(2,1)S(1)}, bf16[3,14592]{1,0:T(4,128)(2,1)S(1)}, u32[]{:S(2)}, u32[]{:S(2)}) collective-permute-start(bf16[3,14592]{1,0:T(4,128)(2,1)S(1)} %get-tuple-element.231), channel_id=1, source_target_pairs={{0,1},{1,0},{2,3},{3,2},{4,5},{5,4},{6,7},{7,6},{8,11},{9,10},{10,... | collective-permute-start | bytes 262664 | tf_op jit(solution)/shard_map/ppermute | solution.py:435
  101.6 6.7 %collective-permute-start.31 = (bf16[3,14592]{1,0:T(4,128)(2,1)S(1)}, bf16[3,14592]{1,0:T(4,128)(2,1)S(1)}, u32[]{:S(2)}, u32[]{:S(2)}) collective-permute-start(bf16[3,14592]{1,0:T(4,128)(2,1)S(1)} %get-tuple-element.232), channel_id=1, source_target_pairs={{0,37},{1,36},{2,39},{3,38},{4,33},{5,32},{6,35},{7,34},{8,127},{9... | collective-permute-start | bytes 262664 | tf_op jit(solution)/shard_map/ppermute | solution.py:435
  101.7 9.2 %collective-permute-start.32 = (bf16[3,14592]{1,0:T(4,128)(2,1)S(1)}, bf16[3,14592]{1,0:T(4,128)(2,1)S(1)}, u32[]{:S(2)}, u32[]{:S(2)}) collective-permute-start(bf16[3,14592]{1,0:T(4,128)(2,1)S(1)} %get-tuple-element.233), channel_id=1, source_target_pairs={{0,36},{1,37},{2,38},{3,39},{4,32},{5,33},{6,34},{7,35},{8,124},{9... | collective-permute-start | bytes 262664 | tf_op jit(solution)/shard_map/ppermute | solution.py:435
  106.0 7.0 %collective-permute-start.33 = (bf16[3,14592]{1,0:T(4,128)(2,1)S(1)}, bf16[3,14592]{1,0:T(4,128)(2,1)S(1)}, u32[]{:S(2)}, u32[]{:S(2)}) collective-permute-start(bf16[3,14592]{1,0:T(4,128)(2,1)S(1)} %get-tuple-element.234), channel_id=1, source_target_pairs={{0,33},{1,32},{2,35},{3,34},{4,37},{5,36},{6,39},{7,38},{8,107},{9... | collective-permute-start | bytes 262664 | tf_op jit(solution)/shard_map/ppermute | solution.py:435
  106.0 7.0 %collective-permute-start.34 = (bf16[3,14592]{1,0:T(4,128)(2,1)S(1)}, bf16[3,14592]{1,0:T(4,128)(2,1)S(1)}, u32[]{:S(2)}, u32[]{:S(2)}) collective-permute-start(bf16[3,14592]{1,0:T(4,128)(2,1)S(1)} %get-tuple-element.235), channel_id=1, source_target_pairs={{0,5},{1,4},{2,7},{3,6},{4,1},{5,0},{6,3},{7,2},{8,31},{9,30},{10,... | collective-permute-start | bytes 262664 | tf_op jit(solution)/shard_map/ppermute | solution.py:435
  107.5 5.5 %collective-permute-start.35 = (bf16[3,14592]{1,0:T(4,128)(2,1)S(1)}, bf16[3,14592]{1,0:T(4,128)(2,1)S(1)}, u32[]{:S(2)}, u32[]{:S(2)}) collective-permute-start(bf16[3,14592]{1,0:T(4,128)(2,1)S(1)} %get-tuple-element.236), channel_id=1, source_target_pairs={{0,32},{1,33},{2,34},{3,35},{4,36},{5,37},{6,38},{7,39},{8,104},{9... | collective-permute-start | bytes 262664 | tf_op jit(solution)/shard_map/ppermute | solution.py:435
  108.3 5.4 %collective-permute-start.36 = (bf16[3,14592]{1,0:T(4,128)(2,1)S(1)}, bf16[3,14592]{1,0:T(4,128)(2,1)S(1)}, u32[]{:S(2)}, u32[]{:S(2)}) collective-permute-start(bf16[3,14592]{1,0:T(4,128)(2,1)S(1)} %get-tuple-element.237), channel_id=1, source_target_pairs={{0,4},{1,5},{2,6},{3,7},{4,0},{5,1},{6,2},{7,3},{8,28},{9,29},{10,... | collective-permute-start | bytes 262664 | tf_op jit(solution)/shard_map/ppermute | solution.py:435
where the time goes:
time: 115 us
  starting transfers between devices  52.1 us (45%)
  Pallas kernels  31.2 us (27%)
  waiting for transfers between devices  30.4 us (26%)
    pallas_call x19, Pallas kernels, call(): pl.pallas_call(body, out_shape=tuple(shapes), in_specs=[pl.BlockSpec(memo...  31.2 us
    ppermute x14, starting transfers between devices, step(): lax.ppermute(chunks[k], MESH, [(d, d ^ PEERS[k]) for d in range(128)])  24.5 us
    ppermute x9, waiting for transfers between devices, along(): return lax.ppermute(value, MESH, pairs(change))  18.2 us
    ppermute x9, starting transfers between devices, along(): return lax.ppermute(value, MESH, pairs(change))  17 us
    ppermute x7, starting transfers between devices, step(): return lax.ppermute(pieces[t - 1], MESH, pairs(change))  8.88 us
    ppermute x14, waiting for transfers between devices, step(): lax.ppermute(chunks[k], MESH, [(d, d ^ PEERS[k]) for d in range(128)])  8.43 us
    ppermute x7, waiting for transfers between devices, step(): return lax.ppermute(pieces[t - 1], MESH, pairs(change))  3.32 us
  transfers between devices with their start and end apart: 37, of which 18 were waited for; matrix products, arithmetic and copies ran while one was open for 0% of the time, Pallas kernels for 13%

commit v1 on v0

--- a/solution.py
+++ b/solution.py
@@ -15,7 +15,7 @@
 Q = 3 * A
 A_PAD = 640
 Q_PAD = 1792
-COLUMNS = 2 * Q_PAD + 2 * A_PAD
+COLUMNS = 2 * Q + 2 * A
 LOCAL = 32
 STRIP = 288
 EPS = 1e-06
@@ -289,7 +289,7 @@
 
 
 def enter_spatial_back(*refs):
-    mid, cot, mod, w_out, mid_grad, scaled_s, att_grad, att_t, back = refs[8:]
+    mid, cot, mod, w_out, own, other, mid_grad, att_grad, att_t, mine, theirs, back = refs[8:]
     for k in range(8):
         back[local_rows(k), :] = refs[k][...]
     unit, spread = normalized(mid[...].astype(F32))
@@ -297,7 +297,8 @@
     total = (cot[...].astype(F32) + grad).astype(BF)
     mid_grad[...] = total
     scaled = (mod[2, 0:1, :] * total.astype(F32)).astype(BF)
-    scaled_s[...] = scaled
+    theirs[...] = pick(other[...], scaled)
+    mine[...] = pick(own[...], scaled)
     att_grad[:, A:] = jnp.zeros((T, A_PAD - A), F32)
     att_grad[:, :A] = dot(scaled, w_out[...], 1, 1).astype(BF).astype(F32)
     att_t[:, A:] = jnp.zeros((T, A_PAD - A), BF)
@@ -324,18 +325,14 @@
     output[...] = (mid[...].astype(F32) + mod[2, 1:2, :] * result).astype(BF)
 
 
-def weight_rows(groups, start):
+def weight_rows(groups):
     def body(*refs):
         keep, sends = refs[-4], refs[-3:]
-        fill(refs, keep, sends, start)
-
-    def fill(refs, keep, sends, start):
-        for (left, left_in, row), (right, right_in, column), width in groups:
+        for (left, left_in, row), (right, right_in, column), width, start in groups:
             lefts = [refs[k][row : row + A, :] for k in (left, left_in)]
             rights = [refs[k][:, column : column + width] for k in (right, right_in)]
             tall_left = jnp.concatenate(lefts, axis=1)
             tall_right = jnp.concatenate(rights, axis=0)
-            padded = -(-width // 128) * 128
             for at in range(0, width, 576):
                 size = min(576, width - at)
                 total = dot(tall_left, tall_right[:, at : at + size], 1, 0)
@@ -344,20 +341,14 @@
                     columns = slice(start + at, start + at + size)
                     keep[p, :, columns] = rows[:96]
                     sends[p][:, columns] = rows[96:].astype(BF)
-            if padded > width:
-                gap = slice(start + width, start + padded)
-                for p in range(3):
-                    keep[p, :, gap] = jnp.zeros((96, padded - width), F32)
-                    sends[p][:, gap] = jnp.zeros((96, padded - width), BF)
-            start += padded
 
     return body
 
 
 def first_halve(p):
     def body(keep, got, kept, send):
+        half = kept.shape[0]
         total = keep[p] + got[...].astype(F32)
-        half = kept.shape[0]
         kept[...] = total[:half]
         send[...] = total[half:].astype(BF)
 
@@ -393,7 +384,7 @@
             for k in range(1, 8):
                 rows = rows + refs[k][:, columns].astype(F32)
             out[3 * p : 3 * p + 3, :] = rows
-        start += -(-size // 128) * 128
+        start += size
 
 
 def pairs(change):
@@ -438,11 +429,10 @@
 
 
 def weight_partials(groups, args, before=()):
-    cost = sum(group[-1] for group in groups) / 1000
+    cost = sum(group[2] for group in groups) / 1100
     outs = [((3, 96, COLUMNS), F32)] + [((96, COLUMNS), BF)] * 3
-    start = Q_PAD if before else 0
     aliases = {len(args) + k: k for k in range(len(before))}
-    return call(weight_rows(groups, start), outs, (*args, *before), cost, aliases=aliases)
+    return call(weight_rows(groups), outs, (*args, *before), cost, aliases=aliases)
 
 
 def shards(
@@ -505,39 +495,39 @@
     early_in = to_other_core(early_theirs)
     t_in, qkv_grad_t_in = to_other_core(t_theirs), to_other_core(qkv_grad_t)
 
-    mid_grad, scaled_s, att_grad_s, att_t = call(
+    mid_grad, att_grad_s, att_t, late_mine, late_theirs = call(
         enter_spatial_back,
-        [((T, D), BF), ((T, D), BF), ((T, A_PAD), F32), ((T, A_PAD), BF)],
-        (*back, mid, cot, mod, w_out_s),
-        1.5,
+        [((T, D), BF), ((T, A_PAD), F32), ((T, A_PAD), BF), one_block, one_block],
+        (*back, mid, cot, mod, w_out_s, own, other),
+        2.4,
         (stage,),
     )
-    att_t_in = to_other_core(att_t)
+    att_t_in, late_in = to_other_core(att_t), to_other_core(late_theirs)
     (qkv_grad_s,) = call(
         spatial_attention_back,
         [((T, Q_PAD), BF)],
         (att_grad_s, qkv_t, probs_t, gains),
-        2.9,
+        2,
         (tall_grad, wide, tall, work),
     )
-    qkv_grad_s, scaled_s, t_in, qkv_grad_t_in, att_t_in = in_order(
-        qkv_grad_s, scaled_s, t_in, qkv_grad_t_in, att_t_in
+    qkv_grad_s, late_in, t_in, qkv_grad_t_in, att_t_in, early_in = in_order(
+        qkv_grad_s, late_in, t_in, qkv_grad_t_in, att_t_in, early_in
     )
     qkv_grad_s_in = to_other_core(qkv_grad_s)
-    late_mine, late_theirs = call(pick_later, [one_block] * 2, (scaled_s, own, other), 1)
-    late_in = to_other_core(late_theirs)
     partials = weight_partials(
-        (((0, 1, 0), (2, 3, 0), Q),), (t_mine, t_in, qkv_grad_t, qkv_grad_t_in)
-    )
-    *partials, qkv_grad_s_in, late_in = in_order(*partials, qkv_grad_s_in, late_in)
-    keep, *sends = weight_partials(
         (
-            ((0, 1, 0), (2, 3, 0), Q), ((0, 1, A), (4, 5, 0), A), ((6, 7, 0), (8, 9, 0), A),
+            ((0, 1, 0), (2, 3, 0), Q, 0), ((4, 5, A), (6, 7, 0), A, Q),
+            ((8, 9, 0), (10, 11, 0), A, 2 * Q + A),
         ),
         (
-            early_mine, early_in, qkv_grad_s, qkv_grad_s_in, att_t, att_t_in, late_mine, late_in,
-            att_s, att_s_in,
+            t_mine, t_in, qkv_grad_t, qkv_grad_t_in, early_mine, early_in, att_t, att_t_in,
+            late_mine, late_in, att_s, att_s_in,
         ),
+    )
+    *partials, qkv_grad_s_in = in_order(*partials, qkv_grad_s_in)
+    keep, *sends = weight_partials(
+        (((0, 1, 0), (2, 3, 0), Q, Q + A),),
+        (early_mine, early_in, qkv_grad_s, qkv_grad_s_in),
         partials,
     )
     keep, att_t, mid_grad, *sends = in_order(keep, att_t, mid_grad, *sends)
@@ -547,7 +537,6 @@
         leave_spatial_back, [((T, D), BF, "any")], (mid_grad, qkv_grad_s, x, mod, w_qkv_s), 2.7
     )
     keep, output, latents_grad = in_order(keep, output, latents_grad)
-
     kept = []
     for p in range(3):
         mine, send = call(
@@ -563,9 +552,9 @@
     own_piece, *pieces = call(
         cut_pieces, [((3, 3 * COLUMNS), F32)] + [((3, 3 * COLUMNS), BF)] * 7, (*kept, *got), 0.5
     )
-    tq, sq, to, so = call(
+    tq, to, sq, so = call(
         last_add,
-        [((9, Q), F32, "any"), ((9, Q), F32, "any"), ((9, A), F32, "any"), ((9, A), F32, "any")],
+        [((9, Q), F32, "any"), ((9, A), F32, "any"), ((9, Q), F32, "any"), ((9, A), F32, "any")],
         (own_piece, *to_owners(pieces)),
         1,
     )

time: 115 us -> 113 us (0.983)
  waiting for transfers between devices: 30.4 us -> 28.7 us
    ppermute x9, waiting for transfers between devices: 18.2 us -> 17 us  [along(): return lax.ppermute(value, MESH, pairs(change))]
    pallas_call x19 -> x18, Pallas kernels: 31.2 us -> 31 us  [call(): pl.pallas_call(body, out_shape=tuple(shapes), in_specs=[pl.BlockSpec(memo...]
  transfers between devices with their start and end apart: 37 -> 37, of which waited for: 18 -> 17; matrix products, arithmetic and copies ran while one was open for 0% -> 0% of each run, Pallas kernels for 13% -> 13%
where the time goes in v1:
time: 113 us
  starting transfers between devices  52.3 us (46%)
  Pallas kernels  31 us (27%)
  waiting for transfers between devices  28.7 us (25%)
    pallas_call x18, Pallas kernels, call(): pl.pallas_call(body, out_shape=tuple(shapes), in_specs=[pl.BlockSpec(memo...  31 us
    ppermute x14, starting transfers between devices, step(): lax.ppermute(chunks[k], MESH, [(d, d ^ PEERS[k]) for d in range(128)])  24.5 us
    ppermute x9, starting transfers between devices, along(): return lax.ppermute(value, MESH, pairs(change))  17.2 us
    ppermute x9, waiting for transfers between devices, along(): return lax.ppermute(value, MESH, pairs(change))  17 us
    ppermute x7, starting transfers between devices, step(): return lax.ppermute(pieces[t - 1], MESH, pairs(change))  8.94 us
    ppermute x14, waiting for transfers between devices, step(): lax.ppermute(chunks[k], MESH, [(d, d ^ PEERS[k]) for d in range(128)])  8.42 us
    ppermute x7, waiting for transfers between devices, step(): return lax.ppermute(pieces[t - 1], MESH, pairs(change))  3.19 us
  transfers between devices with their start and end apart: 37, of which 17 were waited for; matrix products, arithmetic and copies ran while one was open for 0% of the time, Pallas kernels for 13%

profile of v1, /device:TPU:0, one launch (start us, length us, event | category | flops | bytes accessed | tf_op | source)
XLA Modules:
  0.0 112.9 jit_solution(1700656266797193430)
XLA Ops:
  0.6 7.7 %shard_map.127 = (bf16[256,1152]{1,0:T(8,128)(2,1)S(1)}, bf16[256,1152]{1,0:T(8,128)(2,1)S(1)}, f32[3,2,1152]{2,1,0:T(2,128)S(1)}, f32[2,2,72]{2,1,0:T(2,128)S(1...) custom-call(bf16[256,1152]{1,0:T(8,128)(2,1)} %bitcast.13, ...), custom_call_target="tpu_custom_call" | custom-call | flops 11000000512 | bytes 22536448 | tf_op jit(solution)/shard_map/pallas_call | solution.py:52
  8.3 5.0 %collective-permute-start = (bf16[32,1728]{1,0:T(8,128)(2,1)S(1)}, bf16[32,1728]{1,0:T(8,128)(2,1)S(1)}, u32[]{:S(2)}, u32[]{:S(2)}) collective-permute-start(bf16[32,1728]{1,0:T(8,128)(2,1)S(1)} %get-tuple-element.124), channel_id=1, source_target_pairs={{0,6},{1,7},{2,4},{3,5},{4,2},{5,3},{6,0},{7,1},{8,14},{9,15},{10,... | collective-permute-start | bytes 331784 | tf_op jit(solution)/shard_map/ppermute | solution.py:415
  13.4 0.9 collective-permute-start.1
  14.3 0.2 collective-permute-start.2
  14.5 1.4 %collective-permute-start.3 = (bf16[32,1728]{1,0:T(8,128)(2,1)S(1)}, bf16[32,1728]{1,0:T(8,128)(2,1)S(1)}, u32[]{:S(2)}, u32[]{:S(2)}) collective-permute-start(bf16[32,1728]{1,0:T(8,128)(2,1)S(1)} %get-tuple-element.127), channel_id=1, source_target_pairs={{0,4},{1,5},{2,6},{3,7},{4,0},{5,1},{6,2},{7,3},{8,12},{9,13},{10,... | collective-permute-start | bytes 331784 | tf_op jit(solution)/shard_map/ppermute | solution.py:415
  15.9 1.1 collective-permute-done.refs_1_
  16.9 3.5 %collective-permute-start.4 = (bf16[32,1728]{1,0:T(8,128)(2,1)S(1)}, bf16[32,1728]{1,0:T(8,128)(2,1)S(1)}, u32[]{:S(2)}, u32[]{:S(2)}) collective-permute-start(bf16[32,1728]{1,0:T(8,128)(2,1)S(1)} %get-tuple-element.128), channel_id=1, source_target_pairs={{0,2},{1,3},{2,0},{3,1},{4,6},{5,7},{6,4},{7,5},{8,10},{9,11},{10,... | collective-permute-start | bytes 331784 | tf_op jit(solution)/shard_map/ppermute | solution.py:415
  20.4 1.1 collective-permute-start.5
  21.5 1.6 %collective-permute-done.2.refs_3_ = bf16[32,1728]{1,0:T(8,128)(2,1)S(1)} collective-permute-done((bf16[32,1728]{1,0:T(8,128)(2,1)S(1)}, bf16[32,1728]{1,0:T(8,128)(2,1)S(1)}, u32[]{:S(2)}, u32[]{:S(2)}) %collective-permute-start.2) | collective-permute-done | bytes 110624 | tf_op jit(solution)/shard_map/ppermute | solution.py:415
  23.1 2.4 %collective-permute-start.6 = (bf16[32,1728]{1,0:T(8,128)(2,1)S(1)}, bf16[32,1728]{1,0:T(8,128)(2,1)S(1)}, u32[]{:S(2)}, u32[]{:S(2)}) collective-permute-start(bf16[32,1728]{1,0:T(8,128)(2,1)S(1)} %get-tuple-element.130), channel_id=1, source_target_pairs={{0,3},{1,2},{2,1},{3,0},{4,7},{5,6},{6,5},{7,4},{8,11},{9,10},{10,... | collective-permute-start | bytes 331784 | tf_op jit(solution)/shard_map/ppermute | solution.py:415
  25.5 2.7 %shard_map.128 = (bf16[576,1152]{1,0:T(8,128)(2,1)S(1)}, bf16[576,1152]{1,0:T(8,128)(2,1)S(1)}, bf16[1152,256]{1,0:T(8,128)(2,1)S(1)}, bf16[1152,256]{1,0:T(8,128)(2,1)S(1)}, bf16[1728,1152]{1,0:T(8,128)(2,1)S(1)}) custom-call(bf16[256,1152]{1,0:T(8,128)(2,1)S(1)} %get-tuple-element.131.normed, bf16[256,1152]{1,0:T(8,128)(2,1)S(1)} %get-tuple-element.132.scaled, ...), custom_call_target="tpu_custom_call" | custom-call | flops 3080000000 | bytes 12976128 | tf_op jit(solution)/shard_map/pallas_call | solution.py:52
  28.2 0.9 collective-permute-done.6.refs_7_
  29.1 5.4 %shard_map.129 = (bf16[32,1728]{1,0:T(8,128)(2,1)S(1)}, bf16[32,1728]{1,0:T(8,128)(2,1)S(1)}, bf16[32,1728]{1,0:T(8,128)(2,1)S(1)}, bf16[32,1728]{1,0:T(8,128)(2...) custom-call(bf16[32,1728]{1,0:T(8,128)(2,1)S(1)} %get-tuple-element., ...), custom_call_target="tpu_custom_call" | custom-call | flops 11000000512 | bytes 7286912 | tf_op jit(solution)/shard_map/pallas_call | solution.py:52
  34.5 2.2 %collective-permute-start.8 = (bf16[32,1728]{1,0:T(8,128)(2,1)S(1)}, bf16[32,1728]{1,0:T(8,128)(2,1)S(1)}, u32[]{:S(2)}, u32[]{:S(2)}) collective-permute-start(bf16[32,1728]{1,0:T(8,128)(2,1)S(1)} %get-tuple-element.149), channel_id=1, source_target_pairs={{0,6},{1,7},{2,4},{3,5},{4,2},{5,3},{6,0},{7,1},{8,14},{9,15},{10,... | collective-permute-start | bytes 331784 | tf_op jit(solution)/shard_map/ppermute | solution.py:415
  36.7 2.0 %collective-permute-start.9 = (bf16[32,1728]{1,0:T(8,128)(2,1)S(1)}, bf16[32,1728]{1,0:T(8,128)(2,1)S(1)}, u32[]{:S(2)}, u32[]{:S(2)}) collective-permute-start(bf16[32,1728]{1,0:T(8,128)(2,1)S(1)} %get-tuple-element.150), channel_id=1, source_target_pairs={{0,5},{1,4},{2,7},{3,6},{4,1},{5,0},{6,3},{7,2},{8,13},{9,12},{10,... | collective-permute-start | bytes 331784 | tf_op jit(solution)/shard_map/ppermute | solution.py:415
  38.7 1.8 %collective-permute-start.10 = (bf16[32,1728]{1,0:T(8,128)(2,1)S(1)}, bf16[32,1728]{1,0:T(8,128)(2,1)S(1)}, u32[]{:S(2)}, u32[]{:S(2)}) collective-permute-start(bf16[32,1728]{1,0:T(8,128)(2,1)S(1)} %get-tuple-element.151), channel_id=1, source_target_pairs={{0,7},{1,6},{2,5},{3,4},{4,3},{5,2},{6,1},{7,0},{8,15},{9,14},{10,... | collective-permute-start | bytes 331784 | tf_op jit(solution)/shard_map/ppermute | solution.py:415
  40.5 0.5 collective-permute-start.11
  41.0 1.4 %collective-permute-start.12 = (bf16[32,1728]{1,0:T(8,128)(2,1)S(1)}, bf16[32,1728]{1,0:T(8,128)(2,1)S(1)}, u32[]{:S(2)}, u32[]{:S(2)}) collective-permute-start(bf16[32,1728]{1,0:T(8,128)(2,1)S(1)} %get-tuple-element.153), channel_id=1, source_target_pairs={{0,2},{1,3},{2,0},{3,1},{4,6},{5,7},{6,4},{7,5},{8,10},{9,11},{10,... | collective-permute-start | bytes 331784 | tf_op jit(solution)/shard_map/ppermute | solution.py:415
  42.5 0.9 collective-permute-done.8.refs_1_
  43.4 0.9 collective-permute-start.13
  44.3 1.1 collective-permute-start.14
  45.4 1.0 shard_map.130
  46.4 1.0 collective-permute-done.12.refs_5_
  47.4 0.9 collective-permute-done.13.refs_6_
  48.3 2.0 %collective-permute-done.14.refs_7_ = bf16[32,1728]{1,0:T(8,128)(2,1)S(1)} collective-permute-done((bf16[32,1728]{1,0:T(8,128)(2,1)S(1)}, bf16[32,1728]{1,0:T(8,128)(2,1)S(1)}, u32[]{:S(2)}, u32[]{:S(2)}) %collective-permute-start.14) | collective-permute-done | bytes 110624 | tf_op jit(solution)/shard_map/ppermute | solution.py:415
  50.3 0.5 collective-permute-start.19
  50.8 2.2 %shard_map.131 = (bf16[256,1152]{1,0:T(8,128)(2,1)S(1)}, f32[256,640]{1,0:T(8,128)S(1)}, bf16[256,640]{1,0:T(8,128)(2,1)S(1)}, bf16[576,256]{1,0:T(8,128)(2,1)S(1)}, bf16[576,256]{1,0:T(8,128)(2,1)S(1)}) custom-call(bf16[32,1728]{1,0:T(8,128)(2,1)S(1)} %get-tuple-element.162.refs_0_, bf16[32,1728]{1,0:T(8,128)(2,1)S(1)} %collective-permute-done.8.refs_1_, ...), custom_call_target="tpu_custom_call" | custom-call | flops 2640000000 | bytes 8236032 | tf_op jit(solution)/shard_map/pallas_call | solution.py:52
  53.1 0.5 collective-permute-start.15
  53.6 0.1 collective-permute-start.16
  53.7 1.9 %shard_map.132.refs_2_.qkv_grad = bf16[256,1792]{1,0:T(8,128)(2,1)S(1)} custom-call(f32[256,640]{1,0:T(8,128)S(1)} %get-tuple-element.173.att_grad, f32[1728,256]{1,0:T(8,128)S(1)} %get-tuple-element.174.qkv_t, f32[8,256,256]{2,1,0:T(8,128)S(1)} %get-tuple-element.175.probs_t, f32[2,2,72]{2,1,0:T(2,128)S(1)} %get-tuple-element.146.refs_9_.gains), custom_call_target="tpu_custom_call" | custom-call | flops 2200000000 | bytes 5440640 | tf_op jit(solution)/shard_map/pallas_call | solution.py:52
  55.7 0.5 collective-permute-start.20
  56.2 2.6 %shard_map.133 = (f32[3,96,4608]{2,1,0:T(8,128)S(1)}, bf16[96,4608]{1,0:T(8,128)(2,1)S(1)}, bf16[96,4608]{1,0:T(8,128)(2,1)S(1)}, bf16[96,4608]{1,0:T(8,128)(2,1)S(1)}) custom-call(bf16[576,256]{1,0:T(8,128)(2,1)S(1)} %get-tuple-element.183.refs_0_, bf16[576,256]{1,0:T(8,128)(2,1)S(1)} %collective-permute-done.16.refs_1_, ...), custom_call_target="tpu_custom_call" | custom-call | flops 2880000000 | bytes 13467648 | tf_op jit(solution)/shard_map/pallas_call | solution.py:52
  58.8 1.6 %shard_map.134 = (f32[3,96,4608]{2,1,0:T(8,128)S(1)}, bf16[96,4608]{1,0:T(8,128)(2,1)S(1)}, bf16[96,4608]{1,0:T(8,128)(2,1)S(1)}, bf16[96,4608]{1,0:T(8,128)(2,1)S(1)}) custom-call(bf16[1152,256]{1,0:T(8,128)(2,1)S(1)} %get-tuple-element.136.refs_4_.refs_0_, ...), custom_call_target="tpu_custom_call", output_to_operand_aliasing={{0}: (4, {}), {1}: (5, {}), {2}: (6, {}), {3}: (7, {})} | custom-call | flops 1728000000 | bytes 18939904 | tf_op jit(solution)/shard_map/pallas_call | solution.py:52
  60.4 2.8 %collective-permute-start.21 = (bf16[96,4608]{1,0:T(8,128)(2,1)S(1)}, bf16[96,4608]{1,0:T(8,128)(2,1)S(1)}, u32[]{:S(2)}, u32[]{:S(2)}) collective-permute-start(bf16[96,4608]{1,0:T(8,128)(2,1)S(1)} %get-tuple-element.213), channel_id=1, source_target_pairs={{0,96},{1,97},{2,98},{3,99},{4,100},{5,101},{6,102},{7,103},{8,40}... | collective-permute-start | bytes 2654216 | tf_op jit(solution)/shard_map/ppermute | solution.py:410
  63.2 3.1 %collective-permute-start.23 = (bf16[96,4608]{1,0:T(8,128)(2,1)S(1)}, bf16[96,4608]{1,0:T(8,128)(2,1)S(1)}, u32[]{:S(2)}, u32[]{:S(2)}) collective-permute-start(bf16[96,4608]{1,0:T(8,128)(2,1)S(1)} %get-tuple-element.217), channel_id=1, source_target_pairs={{0,20},{1,21},{2,22},{3,23},{4,16},{5,17},{6,18},{7,19},{8,12},{9,... | collective-permute-start | bytes 2654216 | tf_op jit(solution)/shard_map/ppermute | solution.py:410
  66.4 0.7 collective-permute-start.25
  67.1 1.5 %shard_map.135 = bf16[256,1152]{1,0:T(8,128)(2,1)} custom-call(bf16[256,1152]{1,0:T(8,128)(2,1)S(1)} %get-tuple-element.170.refs_8_.mid, bf16[256,640]{1,0:T(8,128)(2,1)S(1)} %get-tuple-element.205.refs_6_.att_t, f32[3,2,1152]{2,1,0:T(2,128)S(1)} %get-tuple-element.145.refs_8_.refs_10_.mod, bf16[576,1152]{1,0:T(8,128)(2,1)S(1)} %get-tuple-element.206.w_out), custom_call_target="tpu_custom_call" | custom-call | flops 1650000000 | bytes 2862080 | tf_op jit(solution)/shard_map/pallas_call | solution.py:52
  68.5 2.7 %shard_map.136 = bf16[256,1152]{1,0:T(8,128)(2,1)} custom-call(bf16[256,1152]{1,0:T(8,128)(2,1)S(1)} %get-tuple-element.207.mid_grad, bf16[256,1792]{1,0:T(8,128)(2,1)S(1)} %shard_map.132.refs_2_.qkv_grad, bf16[256,1152]{1,0:T(8,128)(2,1)S(1)} %get-tuple-element.208.latents, f32[3,2,1152]{2,1,0:T(2,128)S(1)} %get-tuple-element.145.refs_8_.refs_10_.mod, ...), custom_call_target="tpu_custom_call" | custom-call | flops 2969999872 | bytes 6695936 | tf_op jit(solution)/shard_map/pallas_call | solution.py:52
  71.2 3.5 %collective-permute-done.21.got = bf16[96,4608]{1,0:T(8,128)(2,1)S(1)} collective-permute-done((bf16[96,4608]{1,0:T(8,128)(2,1)S(1)}, bf16[96,4608]{1,0:T(8,128)(2,1)S(1)}, u32[]{:S(2)}, u32[]{:S(2)}) %collective-permute-start.21) | collective-permute-done | bytes 884768 | tf_op jit(solution)/shard_map/ppermute | solution.py:410
  74.7 0.1 shard_map.137
  74.9 3.4 %collective-permute-start.22 = (bf16[48,4608]{1,0:T(8,128)(2,1)S(1)}, bf16[48,4608]{1,0:T(8,128)(2,1)S(1)}, u32[]{:S(2)}, u32[]{:S(2)}) collective-permute-start(bf16[48,4608]{1,0:T(8,128)(2,1)S(1)} %get-tuple-element.215), channel_id=1, source_target_pairs={{0,20},{1,21},{2,22},{3,23},{4,16},{5,17},{6,18},{7,19},{8,12},{9,... | collective-permute-start | bytes 1327112 | tf_op jit(solution)/shard_map/ppermute | solution.py:410
  78.3 0.1 shard_map.139
  78.5 0.8 collective-permute-start.24
  79.3 1.3 %collective-permute-done.25.got = bf16[96,4608]{1,0:T(8,128)(2,1)S(1)} collective-permute-done((bf16[96,4608]{1,0:T(8,128)(2,1)S(1)}, bf16[96,4608]{1,0:T(8,128)(2,1)S(1)}, u32[]{:S(2)}, u32[]{:S(2)}) %collective-permute-start.25) | collective-permute-done | bytes 884768 | tf_op jit(solution)/shard_map/ppermute | solution.py:410
  80.6 0.1 shard_map.141
  80.8 1.5 %collective-permute-start.26 = (bf16[48,4608]{1,0:T(8,128)(2,1)S(1)}, bf16[48,4608]{1,0:T(8,128)(2,1)S(1)}, u32[]{:S(2)}, u32[]{:S(2)}) collective-permute-start(bf16[48,4608]{1,0:T(8,128)(2,1)S(1)} %get-tuple-element.223), channel_id=1, source_target_pairs={{0,96},{1,97},{2,98},{3,99},{4,100},{5,101},{6,102},{7,103},{8,40}... | collective-permute-start | bytes 1327112 | tf_op jit(solution)/shard_map/ppermute | solution.py:410
  82.3 2.5 %collective-permute-done.22.got = bf16[48,4608]{1,0:T(8,128)(2,1)S(1)} collective-permute-done((bf16[48,4608]{1,0:T(8,128)(2,1)S(1)}, bf16[48,4608]{1,0:T(8,128)(2,1)S(1)}, u32[]{:S(2)}, u32[]{:S(2)}) %collective-permute-start.22) | collective-permute-done | bytes 442400 | tf_op jit(solution)/shard_map/ppermute | solution.py:410
  84.8 1.2 %collective-permute-start.27 = (bf16[24,4608]{1,0:T(8,128)(2,1)S(1)}, bf16[24,4608]{1,0:T(8,128)(2,1)S(1)}, u32[]{:S(2)}, u32[]{:S(2)}) collective-permute-start(bf16[24,4608]{1,0:T(8,128)(2,1)S(1)} %get-tuple-element.225), channel_id=1, source_target_pairs={{0,3},{1,2},{2,1},{3,0},{4,7},{5,6},{6,5},{7,4},{8,9},{9,8},{10,11... | collective-permute-start | bytes 663560 | tf_op jit(solution)/shard_map/ppermute | solution.py:410
  86.0 2.1 %collective-permute-done.24.got = bf16[48,4608]{1,0:T(8,128)(2,1)S(1)} collective-permute-done((bf16[48,4608]{1,0:T(8,128)(2,1)S(1)}, bf16[48,4608]{1,0:T(8,128)(2,1)S(1)}, u32[]{:S(2)}, u32[]{:S(2)}) %collective-permute-start.24) | collective-permute-done | bytes 442400 | tf_op jit(solution)/shard_map/ppermute | solution.py:410
  88.2 2.8 %collective-permute-start.28 = (bf16[24,4608]{1,0:T(8,128)(2,1)S(1)}, bf16[24,4608]{1,0:T(8,128)(2,1)S(1)}, u32[]{:S(2)}, u32[]{:S(2)}) collective-permute-start(bf16[24,4608]{1,0:T(8,128)(2,1)S(1)} %get-tuple-element.226), channel_id=1, source_target_pairs={{0,96},{1,97},{2,98},{3,99},{4,100},{5,101},{6,102},{7,103},{8,40}... | collective-permute-start | bytes 663560 | tf_op jit(solution)/shard_map/ppermute | solution.py:410
  91.0 0.1 shard_map.142
  91.1 0.7 collective-permute-start.29
  91.9 0.2 collective-permute-done.27.refs_3_
  92.0 3.3 %collective-permute-done.28.refs_4_ = bf16[24,4608]{1,0:T(8,128)(2,1)S(1)} collective-permute-done((bf16[24,4608]{1,0:T(8,128)(2,1)S(1)}, bf16[24,4608]{1,0:T(8,128)(2,1)S(1)}, u32[]{:S(2)}, u32[]{:S(2)}) %collective-permute-start.28) | collective-permute-done | bytes 221216 | tf_op jit(solution)/shard_map/ppermute | solution.py:410
  95.4 4.1 %collective-permute-done.29.refs_5_ = bf16[24,4608]{1,0:T(8,128)(2,1)S(1)} collective-permute-done((bf16[24,4608]{1,0:T(8,128)(2,1)S(1)}, bf16[24,4608]{1,0:T(8,128)(2,1)S(1)}, u32[]{:S(2)}, u32[]{:S(2)}) %collective-permute-start.29) | collective-permute-done | bytes 221216 | tf_op jit(solution)/shard_map/ppermute | solution.py:410
  99.5 0.4 shard_map.143
  100.1 4.3 %collective-permute-start.32 = (bf16[3,13824]{1,0:T(4,128)(2,1)S(1)}, bf16[3,13824]{1,0:T(4,128)(2,1)S(1)}, u32[]{:S(2)}, u32[]{:S(2)}) collective-permute-start(bf16[3,13824]{1,0:T(4,128)(2,1)S(1)} %get-tuple-element.231), channel_id=1, source_target_pairs={{0,36},{1,37},{2,38},{3,39},{4,32},{5,33},{6,34},{7,35},{8,124},{9... | collective-permute-start | bytes 248840 | tf_op jit(solution)/shard_map/ppermute | solution.py:426
  104.4 1.5 %collective-permute-start.34 = (bf16[3,13824]{1,0:T(4,128)(2,1)S(1)}, bf16[3,13824]{1,0:T(4,128)(2,1)S(1)}, u32[]{:S(2)}, u32[]{:S(2)}) collective-permute-start(bf16[3,13824]{1,0:T(4,128)(2,1)S(1)} %get-tuple-element.233), channel_id=1, source_target_pairs={{0,5},{1,4},{2,7},{3,6},{4,1},{5,0},{6,3},{7,2},{8,31},{9,30},{10,... | collective-permute-start | bytes 248840 | tf_op jit(solution)/shard_map/ppermute | solution.py:426
  105.8 0.3 collective-permute-start.35
  106.2 0.5 collective-permute-done.31.refs_2_
  106.6 2.7 %collective-permute-start.36 = (bf16[3,13824]{1,0:T(4,128)(2,1)S(1)}, bf16[3,13824]{1,0:T(4,128)(2,1)S(1)}, u32[]{:S(2)}, u32[]{:S(2)}) collective-permute-start(bf16[3,13824]{1,0:T(4,128)(2,1)S(1)} %get-tuple-element.235), channel_id=1, source_target_pairs={{0,4},{1,5},{2,6},{3,7},{4,0},{5,1},{6,2},{7,3},{8,28},{9,29},{10,... | collective-permute-start | bytes 248840 | tf_op jit(solution)/shard_map/ppermute | solution.py:426
  109.3 1.9 %collective-permute-done.33.refs_4_ = bf16[3,13824]{1,0:T(4,128)(2,1)S(1)} collective-permute-done((bf16[3,13824]{1,0:T(4,128)(2,1)S(1)}, bf16[3,13824]{1,0:T(4,128)(2,1)S(1)}, u32[]{:S(2)}, u32[]{:S(2)}) %collective-permute-start.33) | collective-permute-done | bytes 82976 | tf_op jit(solution)/shard_map/ppermute | solution.py:426
  111.2 0.8 collective-permute-done.36.refs_7_
  112.1 0.8 shard_map.144
  (28 shorter events, 0.5 us)
Async XLA Ops:
  8.3 8.6 %collective-permute-start = (bf16[32,1728]{1,0:T(8,128)(2,1)S(1)}, bf16[32,1728]{1,0:T(8,128)(2,1)S(1)}, u32[]{:S(2)}, u32[]{:S(2)}) collective-permute-start(bf16[32,1728]{1,0:T(8,128)(2,1)S(1)} %get-tuple-element.124), channel_id=1, source_target_pairs={{0,6},{1,7},{2,4},{3,5},{4,2},{5,3},{6,0},{7,1},{8,14},{9,15},{10,... | collective-permute-start | bytes 331784 | tf_op jit(solution)/shard_map/ppermute | solution.py:415
  13.4 7.0 %collective-permute-start.1 = (bf16[32,1728]{1,0:T(8,128)(2,1)S(1)}, bf16[32,1728]{1,0:T(8,128)(2,1)S(1)}, u32[]{:S(2)}, u32[]{:S(2)}) collective-permute-start(bf16[32,1728]{1,0:T(8,128)(2,1)S(1)} %get-tuple-element.125), channel_id=1, source_target_pairs={{0,5},{1,4},{2,7},{3,6},{4,1},{5,0},{6,3},{7,2},{8,13},{9,12},{10,... | collective-permute-start | bytes 331784 | tf_op jit(solution)/shard_map/ppermute | solution.py:415
  14.3 8.8 %collective-permute-start.2 = (bf16[32,1728]{1,0:T(8,128)(2,1)S(1)}, bf16[32,1728]{1,0:T(8,128)(2,1)S(1)}, u32[]{:S(2)}, u32[]{:S(2)}) collective-permute-start(bf16[32,1728]{1,0:T(8,128)(2,1)S(1)} %get-tuple-element.126), channel_id=1, source_target_pairs={{0,7},{1,6},{2,5},{3,4},{4,3},{5,2},{6,1},{7,0},{8,15},{9,14},{10,... | collective-permute-start | bytes 331784 | tf_op jit(solution)/shard_map/ppermute | solution.py:415
  14.5 14.6 %collective-permute-start.7 = (bf16[256,640]{1,0:T(8,128)(2,1)S(1)}, bf16[256,640]{1,0:T(8,128)(2,1)S(1)}, u32[]{:S(2)}, u32[]{:S(2)}) collective-permute-start(bf16[256,640]{1,0:T(8,128)(2,1)S(1)} %get-tuple-element.135.refs_10_), channel_id=1, source_target_pairs={{0,8},{1,9},{2,10},{3,11},{4,12},{5,13},{6,14},{7,15},{8,0},{9,1},... | collective-permute-start | bytes 983048 | tf_op jit(solution)/shard_map/ppermute | solution.py:401
  14.5 13.7 %collective-permute-start.3 = (bf16[32,1728]{1,0:T(8,128)(2,1)S(1)}, bf16[32,1728]{1,0:T(8,128)(2,1)S(1)}, u32[]{:S(2)}, u32[]{:S(2)}) collective-permute-start(bf16[32,1728]{1,0:T(8,128)(2,1)S(1)} %get-tuple-element.127), channel_id=1, source_target_pairs={{0,4},{1,5},{2,6},{3,7},{4,0},{5,1},{6,2},{7,3},{8,12},{9,13},{10,... | collective-permute-start | bytes 331784 | tf_op jit(solution)/shard_map/ppermute | solution.py:415
  16.9 11.3 %collective-permute-start.4 = (bf16[32,1728]{1,0:T(8,128)(2,1)S(1)}, bf16[32,1728]{1,0:T(8,128)(2,1)S(1)}, u32[]{:S(2)}, u32[]{:S(2)}) collective-permute-start(bf16[32,1728]{1,0:T(8,128)(2,1)S(1)} %get-tuple-element.128), channel_id=1, source_target_pairs={{0,2},{1,3},{2,0},{3,1},{4,6},{5,7},{6,4},{7,5},{8,10},{9,11},{10,... | collective-permute-start | bytes 331784 | tf_op jit(solution)/shard_map/ppermute | solution.py:415
  20.4 7.8 %collective-permute-start.5 = (bf16[32,1728]{1,0:T(8,128)(2,1)S(1)}, bf16[32,1728]{1,0:T(8,128)(2,1)S(1)}, u32[]{:S(2)}, u32[]{:S(2)}) collective-permute-start(bf16[32,1728]{1,0:T(8,128)(2,1)S(1)} %get-tuple-element.129), channel_id=1, source_target_pairs={{0,1},{1,0},{2,3},{3,2},{4,5},{5,4},{6,7},{7,6},{8,9},{9,8},{10,11... | collective-permute-start | bytes 331784 | tf_op jit(solution)/shard_map/ppermute | solution.py:415
  23.1 6.0 %collective-permute-start.6 = (bf16[32,1728]{1,0:T(8,128)(2,1)S(1)}, bf16[32,1728]{1,0:T(8,128)(2,1)S(1)}, u32[]{:S(2)}, u32[]{:S(2)}) collective-permute-start(bf16[32,1728]{1,0:T(8,128)(2,1)S(1)} %get-tuple-element.130), channel_id=1, source_target_pairs={{0,3},{1,2},{2,1},{3,0},{4,7},{5,6},{6,5},{7,4},{8,11},{9,10},{10,... | collective-permute-start | bytes 331784 | tf_op jit(solution)/shard_map/ppermute | solution.py:415
  34.5 8.9 %collective-permute-start.8 = (bf16[32,1728]{1,0:T(8,128)(2,1)S(1)}, bf16[32,1728]{1,0:T(8,128)(2,1)S(1)}, u32[]{:S(2)}, u32[]{:S(2)}) collective-permute-start(bf16[32,1728]{1,0:T(8,128)(2,1)S(1)} %get-tuple-element.149), channel_id=1, source_target_pairs={{0,6},{1,7},{2,4},{3,5},{4,2},{5,3},{6,0},{7,1},{8,14},{9,15},{10,... | collective-permute-start | bytes 331784 | tf_op jit(solution)/shard_map/ppermute | solution.py:415
  36.7 7.6 %collective-permute-start.9 = (bf16[32,1728]{1,0:T(8,128)(2,1)S(1)}, bf16[32,1728]{1,0:T(8,128)(2,1)S(1)}, u32[]{:S(2)}, u32[]{:S(2)}) collective-permute-start(bf16[32,1728]{1,0:T(8,128)(2,1)S(1)} %get-tuple-element.150), channel_id=1, source_target_pairs={{0,5},{1,4},{2,7},{3,6},{4,1},{5,0},{6,3},{7,2},{8,13},{9,12},{10,... | collective-permute-start | bytes 331784 | tf_op jit(solution)/shard_map/ppermute | solution.py:415
  38.7 7.7 %collective-permute-start.10 = (bf16[32,1728]{1,0:T(8,128)(2,1)S(1)}, bf16[32,1728]{1,0:T(8,128)(2,1)S(1)}, u32[]{:S(2)}, u32[]{:S(2)}) collective-permute-start(bf16[32,1728]{1,0:T(8,128)(2,1)S(1)} %get-tuple-element.151), channel_id=1, source_target_pairs={{0,7},{1,6},{2,5},{3,4},{4,3},{5,2},{6,1},{7,0},{8,15},{9,14},{10,... | collective-permute-start | bytes 331784 | tf_op jit(solution)/shard_map/ppermute | solution.py:415
  40.5 5.9 %collective-permute-start.11 = (bf16[32,1728]{1,0:T(8,128)(2,1)S(1)}, bf16[32,1728]{1,0:T(8,128)(2,1)S(1)}, u32[]{:S(2)}, u32[]{:S(2)}) collective-permute-start(bf16[32,1728]{1,0:T(8,128)(2,1)S(1)} %get-tuple-element.152), channel_id=1, source_target_pairs={{0,4},{1,5},{2,6},{3,7},{4,0},{5,1},{6,2},{7,3},{8,12},{9,13},{10,... | collective-permute-start | bytes 331784 | tf_op jit(solution)/shard_map/ppermute | solution.py:415
  41.0 6.4 %collective-permute-start.12 = (bf16[32,1728]{1,0:T(8,128)(2,1)S(1)}, bf16[32,1728]{1,0:T(8,128)(2,1)S(1)}, u32[]{:S(2)}, u32[]{:S(2)}) collective-permute-start(bf16[32,1728]{1,0:T(8,128)(2,1)S(1)} %get-tuple-element.153), channel_id=1, source_target_pairs={{0,2},{1,3},{2,0},{3,1},{4,6},{5,7},{6,4},{7,5},{8,10},{9,11},{10,... | collective-permute-start | bytes 331784 | tf_op jit(solution)/shard_map/ppermute | solution.py:415
  43.4 4.9 %collective-permute-start.13 = (bf16[32,1728]{1,0:T(8,128)(2,1)S(1)}, bf16[32,1728]{1,0:T(8,128)(2,1)S(1)}, u32[]{:S(2)}, u32[]{:S(2)}) collective-permute-start(bf16[32,1728]{1,0:T(8,128)(2,1)S(1)} %get-tuple-element.154), channel_id=1, source_target_pairs={{0,1},{1,0},{2,3},{3,2},{4,5},{5,4},{6,7},{7,6},{8,9},{9,8},{10,11... | collective-permute-start | bytes 331784 | tf_op jit(solution)/shard_map/ppermute | solution.py:415
  44.3 6.0 %collective-permute-start.14 = (bf16[32,1728]{1,0:T(8,128)(2,1)S(1)}, bf16[32,1728]{1,0:T(8,128)(2,1)S(1)}, u32[]{:S(2)}, u32[]{:S(2)}) collective-permute-start(bf16[32,1728]{1,0:T(8,128)(2,1)S(1)} %get-tuple-element.155), channel_id=1, source_target_pairs={{0,3},{1,2},{2,1},{3,0},{4,7},{5,6},{6,5},{7,4},{8,11},{9,10},{10,... | collective-permute-start | bytes 331784 | tf_op jit(solution)/shard_map/ppermute | solution.py:415
  50.3 5.4 %collective-permute-start.17 = (bf16[256,1792]{1,0:T(8,128)(2,1)S(1)}, bf16[256,1792]{1,0:T(8,128)(2,1)S(1)}, u32[]{:S(2)}, u32[]{:S(2)}) collective-permute-start(bf16[256,1792]{1,0:T(8,128)(2,1)S(1)} %get-tuple-element.178.refs_2_), channel_id=1, source_target_pairs={{0,8},{1,9},{2,10},{3,11},{4,12},{5,13},{6,14},{7,15},{8,0},{9,1},... | collective-permute-start | bytes 2752520 | tf_op jit(solution)/shard_map/ppermute | solution.py:401
  50.3 5.4 %collective-permute-start.19 = (bf16[1152,256]{1,0:T(8,128)(2,1)S(1)}, bf16[1152,256]{1,0:T(8,128)(2,1)S(1)}, u32[]{:S(2)}, u32[]{:S(2)}) collective-permute-start(bf16[1152,256]{1,0:T(8,128)(2,1)S(1)} %get-tuple-element.180), channel_id=1, source_target_pairs={{0,8},{1,9},{2,10},{3,11},{4,12},{5,13},{6,14},{7,15},{8,0},{9,1},... | collective-permute-start | bytes 1769480 | tf_op jit(solution)/shard_map/ppermute | solution.py:401
  53.0 2.7 %collective-permute-start.18 = (bf16[256,640]{1,0:T(8,128)(2,1)S(1)}, bf16[256,640]{1,0:T(8,128)(2,1)S(1)}, u32[]{:S(2)}, u32[]{:S(2)}) collective-permute-start(bf16[256,640]{1,0:T(8,128)(2,1)S(1)} %get-tuple-element.205.refs_6_.att_t), channel_id=1, source_target_pairs={{0,8},{1,9},{2,10},{3,11},{4,12},{5,13},{6,14},{7,15},{8,0},{9,1},... | collective-permute-start | bytes 983048 | tf_op jit(solution)/shard_map/ppermute | solution.py:401
  53.1 2.5 %collective-permute-start.15 = (bf16[576,256]{1,0:T(8,128)(2,1)S(1)}, bf16[576,256]{1,0:T(8,128)(2,1)S(1)}, u32[]{:S(2)}, u32[]{:S(2)}) collective-permute-start(bf16[576,256]{1,0:T(8,128)(2,1)S(1)} %get-tuple-element.176), channel_id=1, source_target_pairs={{0,8},{1,9},{2,10},{3,11},{4,12},{5,13},{6,14},{7,15},{8,0},{9,1},... | collective-permute-start | bytes 884744 | tf_op jit(solution)/shard_map/ppermute | solution.py:401
  53.6 2.1 %collective-permute-start.16 = (bf16[576,256]{1,0:T(8,128)(2,1)S(1)}, bf16[576,256]{1,0:T(8,128)(2,1)S(1)}, u32[]{:S(2)}, u32[]{:S(2)}) collective-permute-start(bf16[576,256]{1,0:T(8,128)(2,1)S(1)} %get-tuple-element.177), channel_id=1, source_target_pairs={{0,8},{1,9},{2,10},{3,11},{4,12},{5,13},{6,14},{7,15},{8,0},{9,1},... | collective-permute-start | bytes 884744 | tf_op jit(solution)/shard_map/ppermute | solution.py:401
  55.7 3.1 %collective-permute-start.20 = (bf16[256,1792]{1,0:T(8,128)(2,1)S(1)}, bf16[256,1792]{1,0:T(8,128)(2,1)S(1)}, u32[]{:S(2)}, u32[]{:S(2)}) collective-permute-start(bf16[256,1792]{1,0:T(8,128)(2,1)S(1)} %shard_map.132.refs_2_.qkv_grad), channel_id=1, source_target_pairs={{0,8},{1,9},{2,10},{3,11},{4,12},{5,13},{6,14},{7,15},{8,0},{9,1},... | collective-permute-start | bytes 2752520 | tf_op jit(solution)/shard_map/ppermute | solution.py:401
  60.4 14.3 %collective-permute-start.21 = (bf16[96,4608]{1,0:T(8,128)(2,1)S(1)}, bf16[96,4608]{1,0:T(8,128)(2,1)S(1)}, u32[]{:S(2)}, u32[]{:S(2)}) collective-permute-start(bf16[96,4608]{1,0:T(8,128)(2,1)S(1)} %get-tuple-element.213), channel_id=1, source_target_pairs={{0,96},{1,97},{2,98},{3,99},{4,100},{5,101},{6,102},{7,103},{8,40}... | collective-permute-start | bytes 2654216 | tf_op jit(solution)/shard_map/ppermute | solution.py:410
  63.2 15.1 %collective-permute-start.23 = (bf16[96,4608]{1,0:T(8,128)(2,1)S(1)}, bf16[96,4608]{1,0:T(8,128)(2,1)S(1)}, u32[]{:S(2)}, u32[]{:S(2)}) collective-permute-start(bf16[96,4608]{1,0:T(8,128)(2,1)S(1)} %get-tuple-element.217), channel_id=1, source_target_pairs={{0,20},{1,21},{2,22},{3,23},{4,16},{5,17},{6,18},{7,19},{8,12},{9,... | collective-permute-start | bytes 2654216 | tf_op jit(solution)/shard_map/ppermute | solution.py:410
  66.4 14.3 %collective-permute-start.25 = (bf16[96,4608]{1,0:T(8,128)(2,1)S(1)}, bf16[96,4608]{1,0:T(8,128)(2,1)S(1)}, u32[]{:S(2)}, u32[]{:S(2)}) collective-permute-start(bf16[96,4608]{1,0:T(8,128)(2,1)S(1)} %get-tuple-element.221), channel_id=1, source_target_pairs={{0,3},{1,2},{2,1},{3,0},{4,7},{5,6},{6,5},{7,4},{8,9},{9,8},{10,11... | collective-permute-start | bytes 2654216 | tf_op jit(solution)/shard_map/ppermute | solution.py:410
  74.9 9.9 %collective-permute-start.22 = (bf16[48,4608]{1,0:T(8,128)(2,1)S(1)}, bf16[48,4608]{1,0:T(8,128)(2,1)S(1)}, u32[]{:S(2)}, u32[]{:S(2)}) collective-permute-start(bf16[48,4608]{1,0:T(8,128)(2,1)S(1)} %get-tuple-element.215), channel_id=1, source_target_pairs={{0,20},{1,21},{2,22},{3,23},{4,16},{5,17},{6,18},{7,19},{8,12},{9,... | collective-permute-start | bytes 1327112 | tf_op jit(solution)/shard_map/ppermute | solution.py:410
  78.5 9.6 %collective-permute-start.24 = (bf16[48,4608]{1,0:T(8,128)(2,1)S(1)}, bf16[48,4608]{1,0:T(8,128)(2,1)S(1)}, u32[]{:S(2)}, u32[]{:S(2)}) collective-permute-start(bf16[48,4608]{1,0:T(8,128)(2,1)S(1)} %get-tuple-element.219), channel_id=1, source_target_pairs={{0,3},{1,2},{2,1},{3,0},{4,7},{5,6},{6,5},{7,4},{8,9},{9,8},{10,11... | collective-permute-start | bytes 1327112 | tf_op jit(solution)/shard_map/ppermute | solution.py:410
  80.8 10.2 %collective-permute-start.26 = (bf16[48,4608]{1,0:T(8,128)(2,1)S(1)}, bf16[48,4608]{1,0:T(8,128)(2,1)S(1)}, u32[]{:S(2)}, u32[]{:S(2)}) collective-permute-start(bf16[48,4608]{1,0:T(8,128)(2,1)S(1)} %get-tuple-element.223), channel_id=1, source_target_pairs={{0,96},{1,97},{2,98},{3,99},{4,100},{5,101},{6,102},{7,103},{8,40}... | collective-permute-start | bytes 1327112 | tf_op jit(solution)/shard_map/ppermute | solution.py:410
  84.8 7.2 %collective-permute-start.27 = (bf16[24,4608]{1,0:T(8,128)(2,1)S(1)}, bf16[24,4608]{1,0:T(8,128)(2,1)S(1)}, u32[]{:S(2)}, u32[]{:S(2)}) collective-permute-start(bf16[24,4608]{1,0:T(8,128)(2,1)S(1)} %get-tuple-element.225), channel_id=1, source_target_pairs={{0,3},{1,2},{2,1},{3,0},{4,7},{5,6},{6,5},{7,4},{8,9},{9,8},{10,11... | collective-permute-start | bytes 663560 | tf_op jit(solution)/shard_map/ppermute | solution.py:410
  88.2 7.2 %collective-permute-start.28 = (bf16[24,4608]{1,0:T(8,128)(2,1)S(1)}, bf16[24,4608]{1,0:T(8,128)(2,1)S(1)}, u32[]{:S(2)}, u32[]{:S(2)}) collective-permute-start(bf16[24,4608]{1,0:T(8,128)(2,1)S(1)} %get-tuple-element.226), channel_id=1, source_target_pairs={{0,96},{1,97},{2,98},{3,99},{4,100},{5,101},{6,102},{7,103},{8,40}... | collective-permute-start | bytes 663560 | tf_op jit(solution)/shard_map/ppermute | solution.py:410
  91.1 8.4 %collective-permute-start.29 = (bf16[24,4608]{1,0:T(8,128)(2,1)S(1)}, bf16[24,4608]{1,0:T(8,128)(2,1)S(1)}, u32[]{:S(2)}, u32[]{:S(2)}) collective-permute-start(bf16[24,4608]{1,0:T(8,128)(2,1)S(1)} %get-tuple-element.227), channel_id=1, source_target_pairs={{0,20},{1,21},{2,22},{3,23},{4,16},{5,17},{6,18},{7,19},{8,12},{9,... | collective-permute-start | bytes 663560 | tf_op jit(solution)/shard_map/ppermute | solution.py:410
  99.9 5.9 %collective-permute-start.30 = (bf16[3,13824]{1,0:T(4,128)(2,1)S(1)}, bf16[3,13824]{1,0:T(4,128)(2,1)S(1)}, u32[]{:S(2)}, u32[]{:S(2)}) collective-permute-start(bf16[3,13824]{1,0:T(4,128)(2,1)S(1)} %get-tuple-element.229), channel_id=1, source_target_pairs={{0,1},{1,0},{2,3},{3,2},{4,5},{5,4},{6,7},{7,6},{8,11},{9,10},{10,... | collective-permute-start | bytes 248840 | tf_op jit(solution)/shard_map/ppermute | solution.py:426
  100.0 6.6 %collective-permute-start.31 = (bf16[3,13824]{1,0:T(4,128)(2,1)S(1)}, bf16[3,13824]{1,0:T(4,128)(2,1)S(1)}, u32[]{:S(2)}, u32[]{:S(2)}) collective-permute-start(bf16[3,13824]{1,0:T(4,128)(2,1)S(1)} %get-tuple-element.230), channel_id=1, source_target_pairs={{0,37},{1,36},{2,39},{3,38},{4,33},{5,32},{6,35},{7,34},{8,127},{9... | collective-permute-start | bytes 248840 | tf_op jit(solution)/shard_map/ppermute | solution.py:426
  100.1 9.2 %collective-permute-start.32 = (bf16[3,13824]{1,0:T(4,128)(2,1)S(1)}, bf16[3,13824]{1,0:T(4,128)(2,1)S(1)}, u32[]{:S(2)}, u32[]{:S(2)}) collective-permute-start(bf16[3,13824]{1,0:T(4,128)(2,1)S(1)} %get-tuple-element.231), channel_id=1, source_target_pairs={{0,36},{1,37},{2,38},{3,39},{4,32},{5,33},{6,34},{7,35},{8,124},{9... | collective-permute-start | bytes 248840 | tf_op jit(solution)/shard_map/ppermute | solution.py:426
  104.4 6.8 %collective-permute-start.33 = (bf16[3,13824]{1,0:T(4,128)(2,1)S(1)}, bf16[3,13824]{1,0:T(4,128)(2,1)S(1)}, u32[]{:S(2)}, u32[]{:S(2)}) collective-permute-start(bf16[3,13824]{1,0:T(4,128)(2,1)S(1)} %get-tuple-element.232), channel_id=1, source_target_pairs={{0,33},{1,32},{2,35},{3,34},{4,37},{5,36},{6,39},{7,38},{8,107},{9... | collective-permute-start | bytes 248840 | tf_op jit(solution)/shard_map/ppermute | solution.py:426
  104.4 6.8 %collective-permute-start.34 = (bf16[3,13824]{1,0:T(4,128)(2,1)S(1)}, bf16[3,13824]{1,0:T(4,128)(2,1)S(1)}, u32[]{:S(2)}, u32[]{:S(2)}) collective-permute-start(bf16[3,13824]{1,0:T(4,128)(2,1)S(1)} %get-tuple-element.233), channel_id=1, source_target_pairs={{0,5},{1,4},{2,7},{3,6},{4,1},{5,0},{6,3},{7,2},{8,31},{9,30},{10,... | collective-permute-start | bytes 248840 | tf_op jit(solution)/shard_map/ppermute | solution.py:426
  105.8 5.4 %collective-permute-start.35 = (bf16[3,13824]{1,0:T(4,128)(2,1)S(1)}, bf16[3,13824]{1,0:T(4,128)(2,1)S(1)}, u32[]{:S(2)}, u32[]{:S(2)}) collective-permute-start(bf16[3,13824]{1,0:T(4,128)(2,1)S(1)} %get-tuple-element.234), channel_id=1, source_target_pairs={{0,32},{1,33},{2,34},{3,35},{4,36},{5,37},{6,38},{7,39},{8,104},{9... | collective-permute-start | bytes 248840 | tf_op jit(solution)/shard_map/ppermute | solution.py:426
  106.6 5.4 %collective-permute-start.36 = (bf16[3,13824]{1,0:T(4,128)(2,1)S(1)}, bf16[3,13824]{1,0:T(4,128)(2,1)S(1)}, u32[]{:S(2)}, u32[]{:S(2)}) collective-permute-start(bf16[3,13824]{1,0:T(4,128)(2,1)S(1)} %get-tuple-element.235), channel_id=1, source_target_pairs={{0,4},{1,5},{2,6},{3,7},{4,0},{5,1},{6,2},{7,3},{8,28},{9,29},{10,... | collective-permute-start | bytes 248840 | tf_op jit(solution)/shard_map/ppermute | solution.py:426

commit v2 on v1

--- a/solution.py
+++ b/solution.py
@@ -425,7 +425,7 @@
 
         return lax.ppermute(pieces[t - 1], MESH, pairs(change))
 
-    return [step(t) for t in (1, 7, 6, 5, 3, 4, 2)]
+    return [step(t) for t in (4, 2, 1, 6, 5, 3, 7)]
 
 
 def weight_partials(groups, args, before=()):
@@ -462,7 +462,6 @@
     )
     mid, qkv_t, probs_t, normed_s, att_s, scaled_t = rest[8:]
     patch = to_frame_holders(rest[:8])
-    att_s_in = to_other_core(att_s)
     own, other, early_mine, early_theirs, w_qkv_t = call(
         pick_early,
         [((A, D), BF), ((A, D), BF), ((2 * A, T), BF), ((2 * A, T), BF), ((Q, D), BF)],
@@ -471,9 +470,7 @@
         (pltpu.SemaphoreType.DMA(()),),
         apart=(2,),
     )
-    *patch, early_mine, early_theirs, att_s_in = in_order(
-        *patch, early_mine, early_theirs, att_s_in
-    )
+    *patch, early_mine, early_theirs = in_order(*patch, early_mine, early_theirs)
     early_in = to_other_core(early_theirs)
 
     *back, normed_t, qkv_grad_t = call(
@@ -489,9 +486,10 @@
     )
     back = to_frame_holders(back)
     t_mine, t_theirs = call(pick_later, [one_block] * 2, (normed_t, own, other), 1)
-    *back, t_theirs, early_theirs, qkv_grad_t = in_order(
-        *back, t_theirs, early_theirs, qkv_grad_t
-    )
+    *back, t_theirs, early_theirs, qkv_grad_t, att_s = in_order(
+        *back, t_theirs, early_theirs, qkv_grad_t, att_s
+    )
+    att_s_in = to_other_core(att_s)
     early_in = to_other_core(early_theirs)
     t_in, qkv_grad_t_in = to_other_core(t_theirs), to_other_core(qkv_grad_t)
 
@@ -510,8 +508,8 @@
         2,
         (tall_grad, wide, tall, work),
     )
-    qkv_grad_s, late_in, t_in, qkv_grad_t_in, att_t_in, early_in = in_order(
-        qkv_grad_s, late_in, t_in, qkv_grad_t_in, att_t_in, early_in
+    qkv_grad_s, late_in, t_in, qkv_grad_t_in, att_t_in, early_in, att_s_in = in_order(
+        qkv_grad_s, late_in, t_in, qkv_grad_t_in, att_t_in, early_in, att_s_in
     )
     qkv_grad_s_in = to_other_core(qkv_grad_s)
     partials = weight_partials(

time: 113 us -> 112 us (level)
  waiting for transfers between devices: 28.7 us -> 22.3 us
  starting transfers between devices: 52.3 us -> 56.9 us
    ppermute x9, waiting for transfers between devices: 17 us -> 10.5 us  [along(): return lax.ppermute(value, MESH, pairs(change))]
    ppermute x9, starting transfers between devices: 17.2 us -> 22.8 us  [along(): return lax.ppermute(value, MESH, pairs(change))]
    ppermute x14, starting transfers between devices: 24.5 us -> 22.7 us  [step(): lax.ppermute(chunks[k], MESH, [(d, d ^ PEERS[k]) for d in range(128)])]
  transfers between devices with their start and end apart: 37 -> 37, of which waited for: 17 -> 18; matrix products, arithmetic and copies ran while one was open for 0% -> 0% of each run, Pallas kernels for 13% -> 14%
where the time goes in v2:
time: 112 us; the launch traced here: 111 us
  starting transfers between devices  56.9 us (51%)
  Pallas kernels  31 us (28%)
  waiting for transfers between devices  22.3 us (20%)
    pallas_call x18, Pallas kernels, call(): pl.pallas_call(body, out_shape=tuple(shapes), in_specs=[pl.BlockSpec(memo...  31 us
    ppermute x9, starting transfers between devices, along(): return lax.ppermute(value, MESH, pairs(change))  22.8 us
    ppermute x14, starting transfers between devices, step(): lax.ppermute(chunks[k], MESH, [(d, d ^ PEERS[k]) for d in range(128)])  22.7 us
    ppermute x9, waiting for transfers between devices, along(): return lax.ppermute(value, MESH, pairs(change))  10.5 us
    ppermute x7, starting transfers between devices, step(): return lax.ppermute(pieces[t - 1], MESH, pairs(change))  9.39 us
    ppermute x14, waiting for transfers between devices, step(): lax.ppermute(chunks[k], MESH, [(d, d ^ PEERS[k]) for d in range(128)])  8.42 us
    ppermute x7, waiting for transfers between devices, step(): return lax.ppermute(pieces[t - 1], MESH, pairs(change))  2.73 us
  transfers between devices with their start and end apart: 37, of which 18 were waited for; matrix products, arithmetic and copies ran while one was open for 0% of the time, Pallas kernels for 14%

profile of v2, /device:TPU:0, one launch (start us, length us, event | category | flops | bytes accessed | tf_op | source)
XLA Modules:
  0.0 111.0 jit_solution(1287341628123517500)
XLA Ops:
  0.6 7.7 %shard_map.127 = (bf16[256,1152]{1,0:T(8,128)(2,1)S(1)}, bf16[256,1152]{1,0:T(8,128)(2,1)S(1)}, f32[3,2,1152]{2,1,0:T(2,128)S(1)}, f32[2,2,72]{2,1,0:T(2,128)S(1...) custom-call(bf16[256,1152]{1,0:T(8,128)(2,1)} %bitcast.13, ...), custom_call_target="tpu_custom_call" | custom-call | flops 11000000512 | bytes 22536448 | tf_op jit(solution)/shard_map/pallas_call | solution.py:52
  8.3 5.0 %collective-permute-start = (bf16[32,1728]{1,0:T(8,128)(2,1)S(1)}, bf16[32,1728]{1,0:T(8,128)(2,1)S(1)}, u32[]{:S(2)}, u32[]{:S(2)}) collective-permute-start(bf16[32,1728]{1,0:T(8,128)(2,1)S(1)} %get-tuple-element.125), channel_id=1, source_target_pairs={{0,6},{1,7},{2,4},{3,5},{4,2},{5,3},{6,0},{7,1},{8,14},{9,15},{10,... | collective-permute-start | bytes 331784 | tf_op jit(solution)/shard_map/ppermute | solution.py:415
  13.4 0.9 collective-permute-start.1
  14.3 0.2 collective-permute-start.2
  14.5 1.4 %collective-permute-start.3 = (bf16[32,1728]{1,0:T(8,128)(2,1)S(1)}, bf16[32,1728]{1,0:T(8,128)(2,1)S(1)}, u32[]{:S(2)}, u32[]{:S(2)}) collective-permute-start(bf16[32,1728]{1,0:T(8,128)(2,1)S(1)} %get-tuple-element.128), channel_id=1, source_target_pairs={{0,4},{1,5},{2,6},{3,7},{4,0},{5,1},{6,2},{7,3},{8,12},{9,13},{10,... | collective-permute-start | bytes 331784 | tf_op jit(solution)/shard_map/ppermute | solution.py:415
  15.9 3.0 %collective-permute-start.4 = (bf16[32,1728]{1,0:T(8,128)(2,1)S(1)}, bf16[32,1728]{1,0:T(8,128)(2,1)S(1)}, u32[]{:S(2)}, u32[]{:S(2)}) collective-permute-start(bf16[32,1728]{1,0:T(8,128)(2,1)S(1)} %get-tuple-element.129), channel_id=1, source_target_pairs={{0,2},{1,3},{2,0},{3,1},{4,6},{5,7},{6,4},{7,5},{8,10},{9,11},{10,... | collective-permute-start | bytes 331784 | tf_op jit(solution)/shard_map/ppermute | solution.py:415
  18.8 1.0 collective-permute-start.5
  19.9 0.5 collective-permute-done.1.refs_2_
  20.4 0.6 collective-permute-start.6
  21.0 2.7 %shard_map.128 = (bf16[576,1152]{1,0:T(8,128)(2,1)S(1)}, bf16[576,1152]{1,0:T(8,128)(2,1)S(1)}, bf16[1152,256]{1,0:T(8,128)(2,1)S(1)}, bf16[1152,256]{1,0:T(8,128)(2,1)S(1)}, bf16[1728,1152]{1,0:T(8,128)(2,1)S(1)}) custom-call(bf16[256,1152]{1,0:T(8,128)(2,1)S(1)} %get-tuple-element.132.normed, bf16[256,1152]{1,0:T(8,128)(2,1)S(1)} %get-tuple-element.133.scaled, ...), custom_call_target="tpu_custom_call" | custom-call | flops 3080000000 | bytes 12976128 | tf_op jit(solution)/shard_map/pallas_call | solution.py:52
  23.7 0.4 collective-permute-done.3.refs_4_
  24.1 0.7 collective-permute-done.5.refs_6_
  24.8 1.6 %collective-permute-done.6.refs_7_ = bf16[32,1728]{1,0:T(8,128)(2,1)S(1)} collective-permute-done((bf16[32,1728]{1,0:T(8,128)(2,1)S(1)}, bf16[32,1728]{1,0:T(8,128)(2,1)S(1)}, u32[]{:S(2)}, u32[]{:S(2)}) %collective-permute-start.6) | collective-permute-done | bytes 110624 | tf_op jit(solution)/shard_map/ppermute | solution.py:415
  26.4 5.4 %shard_map.129 = (bf16[32,1728]{1,0:T(8,128)(2,1)S(1)}, bf16[32,1728]{1,0:T(8,128)(2,1)S(1)}, bf16[32,1728]{1,0:T(8,128)(2,1)S(1)}, bf16[32,1728]{1,0:T(8,128)(2...) custom-call(bf16[32,1728]{1,0:T(8,128)(2,1)S(1)} %get-tuple-element., ...), custom_call_target="tpu_custom_call" | custom-call | flops 11000000512 | bytes 7286912 | tf_op jit(solution)/shard_map/pallas_call | solution.py:52
  31.8 3.2 %collective-permute-start.7 = (bf16[32,1728]{1,0:T(8,128)(2,1)S(1)}, bf16[32,1728]{1,0:T(8,128)(2,1)S(1)}, u32[]{:S(2)}, u32[]{:S(2)}) collective-permute-start(bf16[32,1728]{1,0:T(8,128)(2,1)S(1)} %get-tuple-element.149), channel_id=1, source_target_pairs={{0,6},{1,7},{2,4},{3,5},{4,2},{5,3},{6,0},{7,1},{8,14},{9,15},{10,... | collective-permute-start | bytes 331784 | tf_op jit(solution)/shard_map/ppermute | solution.py:415
  34.9 1.1 collective-permute-start.8
  36.0 2.2 %collective-permute-start.9 = (bf16[32,1728]{1,0:T(8,128)(2,1)S(1)}, bf16[32,1728]{1,0:T(8,128)(2,1)S(1)}, u32[]{:S(2)}, u32[]{:S(2)}) collective-permute-start(bf16[32,1728]{1,0:T(8,128)(2,1)S(1)} %get-tuple-element.151), channel_id=1, source_target_pairs={{0,7},{1,6},{2,5},{3,4},{4,3},{5,2},{6,1},{7,0},{8,15},{9,14},{10,... | collective-permute-start | bytes 331784 | tf_op jit(solution)/shard_map/ppermute | solution.py:415
  38.3 2.2 %collective-permute-start.11 = (bf16[32,1728]{1,0:T(8,128)(2,1)S(1)}, bf16[32,1728]{1,0:T(8,128)(2,1)S(1)}, u32[]{:S(2)}, u32[]{:S(2)}) collective-permute-start(bf16[32,1728]{1,0:T(8,128)(2,1)S(1)} %get-tuple-element.153), channel_id=1, source_target_pairs={{0,2},{1,3},{2,0},{3,1},{4,6},{5,7},{6,4},{7,5},{8,10},{9,11},{10,... | collective-permute-start | bytes 331784 | tf_op jit(solution)/shard_map/ppermute | solution.py:415
  40.5 1.0 collective-permute-start.12
  41.6 0.9 collective-permute-done.8.refs_2_
  42.4 0.8 collective-permute-start.13
  43.2 0.9 shard_map.130
  44.2 0.4 collective-permute-done.9.refs_3_
  44.6 1.4 %collective-permute-done.10.refs_4_ = bf16[32,1728]{1,0:T(8,128)(2,1)S(1)} collective-permute-done((bf16[32,1728]{1,0:T(8,128)(2,1)S(1)}, bf16[32,1728]{1,0:T(8,128)(2,1)S(1)}, u32[]{:S(2)}, u32[]{:S(2)}) %collective-permute-start.10) | collective-permute-done | bytes 110624 | tf_op jit(solution)/shard_map/ppermute | solution.py:415
  46.0 0.7 collective-permute-done.12.refs_6_
  46.7 1.8 %collective-permute-done.13.refs_7_ = bf16[32,1728]{1,0:T(8,128)(2,1)S(1)} collective-permute-done((bf16[32,1728]{1,0:T(8,128)(2,1)S(1)}, bf16[32,1728]{1,0:T(8,128)(2,1)S(1)}, u32[]{:S(2)}, u32[]{:S(2)}) %collective-permute-start.13) | collective-permute-done | bytes 110624 | tf_op jit(solution)/shard_map/ppermute | solution.py:415
  48.5 2.2 %shard_map.131 = (bf16[256,1152]{1,0:T(8,128)(2,1)S(1)}, f32[256,640]{1,0:T(8,128)S(1)}, bf16[256,640]{1,0:T(8,128)(2,1)S(1)}, bf16[576,256]{1,0:T(8,128)(2,1)S(1)}, bf16[576,256]{1,0:T(8,128)(2,1)S(1)}) custom-call(bf16[32,1728]{1,0:T(8,128)(2,1)S(1)} %get-tuple-element.163.refs_0_, bf16[32,1728]{1,0:T(8,128)(2,1)S(1)} %collective-permute-done.7.refs_1_, ...), custom_call_target="tpu_custom_call" | custom-call | flops 2640000000 | bytes 8236032 | tf_op jit(solution)/shard_map/pallas_call | solution.py:52
  50.7 0.8 collective-permute-start.14
  51.6 0.4 collective-permute-start.17
  52.0 0.1 collective-permute-start.19
  52.1 0.6 collective-permute-done.14.refs_9_
  52.7 0.4 collective-permute-start.15
  53.1 2.0 %shard_map.132.refs_2_.qkv_grad = bf16[256,1792]{1,0:T(8,128)(2,1)S(1)} custom-call(f32[256,640]{1,0:T(8,128)S(1)} %get-tuple-element.174.att_grad, f32[1728,256]{1,0:T(8,128)S(1)} %get-tuple-element.175.qkv_t, f32[8,256,256]{2,1,0:T(8,128)S(1)} %get-tuple-element.176.probs_t, f32[2,2,72]{2,1,0:T(2,128)S(1)} %get-tuple-element.146.refs_9_.gains), custom_call_target="tpu_custom_call" | custom-call | flops 2200000000 | bytes 5440640 | tf_op jit(solution)/shard_map/pallas_call | solution.py:52
  55.1 0.3 collective-permute-start.20
  55.4 2.6 %shard_map.133 = (f32[3,96,4608]{2,1,0:T(8,128)S(1)}, bf16[96,4608]{1,0:T(8,128)(2,1)S(1)}, bf16[96,4608]{1,0:T(8,128)(2,1)S(1)}, bf16[96,4608]{1,0:T(8,128)(2,1)S(1)}) custom-call(bf16[576,256]{1,0:T(8,128)(2,1)S(1)} %get-tuple-element.185.refs_0_, bf16[576,256]{1,0:T(8,128)(2,1)S(1)} %collective-permute-done.15.refs_1_, ...), custom_call_target="tpu_custom_call" | custom-call | flops 2880000000 | bytes 13467648 | tf_op jit(solution)/shard_map/pallas_call | solution.py:52
  58.0 1.6 %shard_map.134 = (f32[3,96,4608]{2,1,0:T(8,128)S(1)}, bf16[96,4608]{1,0:T(8,128)(2,1)S(1)}, bf16[96,4608]{1,0:T(8,128)(2,1)S(1)}, bf16[96,4608]{1,0:T(8,128)(2,1)S(1)}) custom-call(bf16[1152,256]{1,0:T(8,128)(2,1)S(1)} %get-tuple-element.136.refs_4_.refs_0_, ...), custom_call_target="tpu_custom_call", output_to_operand_aliasing={{0}: (4, {}), {1}: (5, {}), {2}: (6, {}), {3}: (7, {})} | custom-call | flops 1728000000 | bytes 18939904 | tf_op jit(solution)/shard_map/pallas_call | solution.py:52
  59.6 2.8 %collective-permute-start.21 = (bf16[96,4608]{1,0:T(8,128)(2,1)S(1)}, bf16[96,4608]{1,0:T(8,128)(2,1)S(1)}, u32[]{:S(2)}, u32[]{:S(2)}) collective-permute-start(bf16[96,4608]{1,0:T(8,128)(2,1)S(1)} %get-tuple-element.215), channel_id=1, source_target_pairs={{0,96},{1,97},{2,98},{3,99},{4,100},{5,101},{6,102},{7,103},{8,40}... | collective-permute-start | bytes 2654216 | tf_op jit(solution)/shard_map/ppermute | solution.py:410
  62.4 2.8 %collective-permute-start.23 = (bf16[96,4608]{1,0:T(8,128)(2,1)S(1)}, bf16[96,4608]{1,0:T(8,128)(2,1)S(1)}, u32[]{:S(2)}, u32[]{:S(2)}) collective-permute-start(bf16[96,4608]{1,0:T(8,128)(2,1)S(1)} %get-tuple-element.219), channel_id=1, source_target_pairs={{0,20},{1,21},{2,22},{3,23},{4,16},{5,17},{6,18},{7,19},{8,12},{9,... | collective-permute-start | bytes 2654216 | tf_op jit(solution)/shard_map/ppermute | solution.py:410
  65.3 2.1 %collective-permute-start.25 = (bf16[96,4608]{1,0:T(8,128)(2,1)S(1)}, bf16[96,4608]{1,0:T(8,128)(2,1)S(1)}, u32[]{:S(2)}, u32[]{:S(2)}) collective-permute-start(bf16[96,4608]{1,0:T(8,128)(2,1)S(1)} %get-tuple-element.223), channel_id=1, source_target_pairs={{0,3},{1,2},{2,1},{3,0},{4,7},{5,6},{6,5},{7,4},{8,9},{9,8},{10,11... | collective-permute-start | bytes 2654216 | tf_op jit(solution)/shard_map/ppermute | solution.py:410
  67.3 1.5 %shard_map.135 = bf16[256,1152]{1,0:T(8,128)(2,1)} custom-call(bf16[256,1152]{1,0:T(8,128)(2,1)S(1)} %get-tuple-element.171.refs_8_.mid, bf16[256,640]{1,0:T(8,128)(2,1)S(1)} %get-tuple-element.207.refs_6_.att_t, f32[3,2,1152]{2,1,0:T(2,128)S(1)} %get-tuple-element.145.refs_8_.refs_10_.mod, bf16[576,1152]{1,0:T(8,128)(2,1)S(1)} %get-tuple-element.208.w_out), custom_call_target="tpu_custom_call" | custom-call | flops 1650000000 | bytes 2862080 | tf_op jit(solution)/shard_map/pallas_call | solution.py:52
  68.8 2.7 %shard_map.136 = bf16[256,1152]{1,0:T(8,128)(2,1)} custom-call(bf16[256,1152]{1,0:T(8,128)(2,1)S(1)} %get-tuple-element.209.mid_grad, bf16[256,1792]{1,0:T(8,128)(2,1)S(1)} %shard_map.132.refs_2_.qkv_grad, bf16[256,1152]{1,0:T(8,128)(2,1)S(1)} %get-tuple-element.210.latents, f32[3,2,1152]{2,1,0:T(2,128)S(1)} %get-tuple-element.145.refs_8_.refs_10_.mod, ...), custom_call_target="tpu_custom_call" | custom-call | flops 2969999872 | bytes 6695936 | tf_op jit(solution)/shard_map/pallas_call | solution.py:52
  71.4 2.5 %collective-permute-done.21.got = bf16[96,4608]{1,0:T(8,128)(2,1)S(1)} collective-permute-done((bf16[96,4608]{1,0:T(8,128)(2,1)S(1)}, bf16[96,4608]{1,0:T(8,128)(2,1)S(1)}, u32[]{:S(2)}, u32[]{:S(2)}) %collective-permute-start.21) | collective-permute-done | bytes 884768 | tf_op jit(solution)/shard_map/ppermute | solution.py:410
  73.9 0.1 shard_map.137
  74.1 2.9 %collective-permute-start.22 = (bf16[48,4608]{1,0:T(8,128)(2,1)S(1)}, bf16[48,4608]{1,0:T(8,128)(2,1)S(1)}, u32[]{:S(2)}, u32[]{:S(2)}) collective-permute-start(bf16[48,4608]{1,0:T(8,128)(2,1)S(1)} %get-tuple-element.217), channel_id=1, source_target_pairs={{0,20},{1,21},{2,22},{3,23},{4,16},{5,17},{6,18},{7,19},{8,12},{9,... | collective-permute-start | bytes 1327112 | tf_op jit(solution)/shard_map/ppermute | solution.py:410
  77.0 0.1 shard_map.139
  77.1 2.1 %collective-permute-start.24 = (bf16[48,4608]{1,0:T(8,128)(2,1)S(1)}, bf16[48,4608]{1,0:T(8,128)(2,1)S(1)}, u32[]{:S(2)}, u32[]{:S(2)}) collective-permute-start(bf16[48,4608]{1,0:T(8,128)(2,1)S(1)} %get-tuple-element.221), channel_id=1, source_target_pairs={{0,3},{1,2},{2,1},{3,0},{4,7},{5,6},{6,5},{7,4},{8,9},{9,8},{10,11... | collective-permute-start | bytes 1327112 | tf_op jit(solution)/shard_map/ppermute | solution.py:410
  79.3 0.2 collective-permute-done.25.got
  79.5 0.1 shard_map.141
  79.7 2.6 %collective-permute-start.26 = (bf16[48,4608]{1,0:T(8,128)(2,1)S(1)}, bf16[48,4608]{1,0:T(8,128)(2,1)S(1)}, u32[]{:S(2)}, u32[]{:S(2)}) collective-permute-start(bf16[48,4608]{1,0:T(8,128)(2,1)S(1)} %get-tuple-element.225), channel_id=1, source_target_pairs={{0,96},{1,97},{2,98},{3,99},{4,100},{5,101},{6,102},{7,103},{8,40}... | collective-permute-start | bytes 1327112 | tf_op jit(solution)/shard_map/ppermute | solution.py:410
  82.3 1.4 %collective-permute-done.22.got = bf16[48,4608]{1,0:T(8,128)(2,1)S(1)} collective-permute-done((bf16[48,4608]{1,0:T(8,128)(2,1)S(1)}, bf16[48,4608]{1,0:T(8,128)(2,1)S(1)}, u32[]{:S(2)}, u32[]{:S(2)}) %collective-permute-start.22) | collective-permute-done | bytes 442400 | tf_op jit(solution)/shard_map/ppermute | solution.py:410
  83.7 2.2 %collective-permute-start.27 = (bf16[24,4608]{1,0:T(8,128)(2,1)S(1)}, bf16[24,4608]{1,0:T(8,128)(2,1)S(1)}, u32[]{:S(2)}, u32[]{:S(2)}) collective-permute-start(bf16[24,4608]{1,0:T(8,128)(2,1)S(1)} %get-tuple-element.227), channel_id=1, source_target_pairs={{0,3},{1,2},{2,1},{3,0},{4,7},{5,6},{6,5},{7,4},{8,9},{9,8},{10,11... | collective-permute-start | bytes 663560 | tf_op jit(solution)/shard_map/ppermute | solution.py:410
  86.0 0.7 collective-permute-done.24.got
  86.8 3.1 %collective-permute-start.28 = (bf16[24,4608]{1,0:T(8,128)(2,1)S(1)}, bf16[24,4608]{1,0:T(8,128)(2,1)S(1)}, u32[]{:S(2)}, u32[]{:S(2)}) collective-permute-start(bf16[24,4608]{1,0:T(8,128)(2,1)S(1)} %get-tuple-element.228), channel_id=1, source_target_pairs={{0,96},{1,97},{2,98},{3,99},{4,100},{5,101},{6,102},{7,103},{8,40}... | collective-permute-start | bytes 663560 | tf_op jit(solution)/shard_map/ppermute | solution.py:410
  89.9 0.1 shard_map.142
  90.0 2.1 %collective-permute-start.29 = (bf16[24,4608]{1,0:T(8,128)(2,1)S(1)}, bf16[24,4608]{1,0:T(8,128)(2,1)S(1)}, u32[]{:S(2)}, u32[]{:S(2)}) collective-permute-start(bf16[24,4608]{1,0:T(8,128)(2,1)S(1)} %get-tuple-element.229), channel_id=1, source_target_pairs={{0,20},{1,21},{2,22},{3,23},{4,16},{5,17},{6,18},{7,19},{8,12},{9,... | collective-permute-start | bytes 663560 | tf_op jit(solution)/shard_map/ppermute | solution.py:410
  92.1 3.4 %collective-permute-done.28.refs_4_ = bf16[24,4608]{1,0:T(8,128)(2,1)S(1)} collective-permute-done((bf16[24,4608]{1,0:T(8,128)(2,1)S(1)}, bf16[24,4608]{1,0:T(8,128)(2,1)S(1)}, u32[]{:S(2)}, u32[]{:S(2)}) %collective-permute-start.28) | collective-permute-done | bytes 221216 | tf_op jit(solution)/shard_map/ppermute | solution.py:410
  95.5 2.2 %collective-permute-done.29.refs_5_ = bf16[24,4608]{1,0:T(8,128)(2,1)S(1)} collective-permute-done((bf16[24,4608]{1,0:T(8,128)(2,1)S(1)}, bf16[24,4608]{1,0:T(8,128)(2,1)S(1)}, u32[]{:S(2)}, u32[]{:S(2)}) %collective-permute-start.29) | collective-permute-done | bytes 221216 | tf_op jit(solution)/shard_map/ppermute | solution.py:410
  97.7 0.4 shard_map.143
  98.4 3.3 %collective-permute-start.33 = (bf16[3,13824]{1,0:T(4,128)(2,1)S(1)}, bf16[3,13824]{1,0:T(4,128)(2,1)S(1)}, u32[]{:S(2)}, u32[]{:S(2)}) collective-permute-start(bf16[3,13824]{1,0:T(4,128)(2,1)S(1)} %get-tuple-element.234), channel_id=1, source_target_pairs={{0,36},{1,37},{2,38},{3,39},{4,32},{5,33},{6,34},{7,35},{8,124},{9... | collective-permute-start | bytes 248840 | tf_op jit(solution)/shard_map/ppermute | solution.py:426
  101.6 1.6 %collective-permute-start.34 = (bf16[3,13824]{1,0:T(4,128)(2,1)S(1)}, bf16[3,13824]{1,0:T(4,128)(2,1)S(1)}, u32[]{:S(2)}, u32[]{:S(2)}) collective-permute-start(bf16[3,13824]{1,0:T(4,128)(2,1)S(1)} %get-tuple-element.235), channel_id=1, source_target_pairs={{0,33},{1,32},{2,35},{3,34},{4,37},{5,36},{6,39},{7,38},{8,107},{9... | collective-permute-start | bytes 248840 | tf_op jit(solution)/shard_map/ppermute | solution.py:426
  103.2 4.3 %collective-permute-start.36 = (bf16[3,13824]{1,0:T(4,128)(2,1)S(1)}, bf16[3,13824]{1,0:T(4,128)(2,1)S(1)}, u32[]{:S(2)}, u32[]{:S(2)}) collective-permute-start(bf16[3,13824]{1,0:T(4,128)(2,1)S(1)} %get-tuple-element.237), channel_id=1, source_target_pairs={{0,37},{1,36},{2,39},{3,38},{4,33},{5,32},{6,35},{7,34},{8,127},{9... | collective-permute-start | bytes 248840 | tf_op jit(solution)/shard_map/ppermute | solution.py:426
  107.5 1.3 %collective-permute-done.35.refs_6_ = bf16[3,13824]{1,0:T(4,128)(2,1)S(1)} collective-permute-done((bf16[3,13824]{1,0:T(4,128)(2,1)S(1)}, bf16[3,13824]{1,0:T(4,128)(2,1)S(1)}, u32[]{:S(2)}, u32[]{:S(2)}) %collective-permute-start.35) | collective-permute-done | bytes 82976 | tf_op jit(solution)/shard_map/ppermute | solution.py:426
  108.9 1.4 %collective-permute-done.36.refs_7_ = bf16[3,13824]{1,0:T(4,128)(2,1)S(1)} collective-permute-done((bf16[3,13824]{1,0:T(4,128)(2,1)S(1)}, bf16[3,13824]{1,0:T(4,128)(2,1)S(1)}, u32[]{:S(2)}, u32[]{:S(2)}) %collective-permute-start.36) | collective-permute-done | bytes 82976 | tf_op jit(solution)/shard_map/ppermute | solution.py:426
  110.2 0.8 shard_map.144
  (28 shorter events, 0.6 us)
Async XLA Ops:
  8.3 10.5 %collective-permute-start = (bf16[32,1728]{1,0:T(8,128)(2,1)S(1)}, bf16[32,1728]{1,0:T(8,128)(2,1)S(1)}, u32[]{:S(2)}, u32[]{:S(2)}) collective-permute-start(bf16[32,1728]{1,0:T(8,128)(2,1)S(1)} %get-tuple-element.125), channel_id=1, source_target_pairs={{0,6},{1,7},{2,4},{3,5},{4,2},{5,3},{6,0},{7,1},{8,14},{9,15},{10,... | collective-permute-start | bytes 331784 | tf_op jit(solution)/shard_map/ppermute | solution.py:415
  13.4 7.0 %collective-permute-start.1 = (bf16[32,1728]{1,0:T(8,128)(2,1)S(1)}, bf16[32,1728]{1,0:T(8,128)(2,1)S(1)}, u32[]{:S(2)}, u32[]{:S(2)}) collective-permute-start(bf16[32,1728]{1,0:T(8,128)(2,1)S(1)} %get-tuple-element.126), channel_id=1, source_target_pairs={{0,5},{1,4},{2,7},{3,6},{4,1},{5,0},{6,3},{7,2},{8,13},{9,12},{10,... | collective-permute-start | bytes 331784 | tf_op jit(solution)/shard_map/ppermute | solution.py:415
  14.3 9.4 %collective-permute-start.2 = (bf16[32,1728]{1,0:T(8,128)(2,1)S(1)}, bf16[32,1728]{1,0:T(8,128)(2,1)S(1)}, u32[]{:S(2)}, u32[]{:S(2)}) collective-permute-start(bf16[32,1728]{1,0:T(8,128)(2,1)S(1)} %get-tuple-element.127), channel_id=1, source_target_pairs={{0,7},{1,6},{2,5},{3,4},{4,3},{5,2},{6,1},{7,0},{8,15},{9,14},{10,... | collective-permute-start | bytes 331784 | tf_op jit(solution)/shard_map/ppermute | solution.py:415
  14.5 9.6 %collective-permute-start.3 = (bf16[32,1728]{1,0:T(8,128)(2,1)S(1)}, bf16[32,1728]{1,0:T(8,128)(2,1)S(1)}, u32[]{:S(2)}, u32[]{:S(2)}) collective-permute-start(bf16[32,1728]{1,0:T(8,128)(2,1)S(1)} %get-tuple-element.128), channel_id=1, source_target_pairs={{0,4},{1,5},{2,6},{3,7},{4,0},{5,1},{6,2},{7,3},{8,12},{9,13},{10,... | collective-permute-start | bytes 331784 | tf_op jit(solution)/shard_map/ppermute | solution.py:415
  15.9 8.2 %collective-permute-start.4 = (bf16[32,1728]{1,0:T(8,128)(2,1)S(1)}, bf16[32,1728]{1,0:T(8,128)(2,1)S(1)}, u32[]{:S(2)}, u32[]{:S(2)}) collective-permute-start(bf16[32,1728]{1,0:T(8,128)(2,1)S(1)} %get-tuple-element.129), channel_id=1, source_target_pairs={{0,2},{1,3},{2,0},{3,1},{4,6},{5,7},{6,4},{7,5},{8,10},{9,11},{10,... | collective-permute-start | bytes 331784 | tf_op jit(solution)/shard_map/ppermute | solution.py:415
  18.8 5.9 %collective-permute-start.5 = (bf16[32,1728]{1,0:T(8,128)(2,1)S(1)}, bf16[32,1728]{1,0:T(8,128)(2,1)S(1)}, u32[]{:S(2)}, u32[]{:S(2)}) collective-permute-start(bf16[32,1728]{1,0:T(8,128)(2,1)S(1)} %get-tuple-element.130), channel_id=1, source_target_pairs={{0,1},{1,0},{2,3},{3,2},{4,5},{5,4},{6,7},{7,6},{8,9},{9,8},{10,11... | collective-permute-start | bytes 331784 | tf_op jit(solution)/shard_map/ppermute | solution.py:415
  20.4 6.0 %collective-permute-start.6 = (bf16[32,1728]{1,0:T(8,128)(2,1)S(1)}, bf16[32,1728]{1,0:T(8,128)(2,1)S(1)}, u32[]{:S(2)}, u32[]{:S(2)}) collective-permute-start(bf16[32,1728]{1,0:T(8,128)(2,1)S(1)} %get-tuple-element.131), channel_id=1, source_target_pairs={{0,3},{1,2},{2,1},{3,0},{4,7},{5,6},{6,5},{7,4},{8,11},{9,10},{10,... | collective-permute-start | bytes 331784 | tf_op jit(solution)/shard_map/ppermute | solution.py:415
  31.8 8.8 %collective-permute-start.7 = (bf16[32,1728]{1,0:T(8,128)(2,1)S(1)}, bf16[32,1728]{1,0:T(8,128)(2,1)S(1)}, u32[]{:S(2)}, u32[]{:S(2)}) collective-permute-start(bf16[32,1728]{1,0:T(8,128)(2,1)S(1)} %get-tuple-element.149), channel_id=1, source_target_pairs={{0,6},{1,7},{2,4},{3,5},{4,2},{5,3},{6,0},{7,1},{8,14},{9,15},{10,... | collective-permute-start | bytes 331784 | tf_op jit(solution)/shard_map/ppermute | solution.py:415
  34.9 7.5 %collective-permute-start.8 = (bf16[32,1728]{1,0:T(8,128)(2,1)S(1)}, bf16[32,1728]{1,0:T(8,128)(2,1)S(1)}, u32[]{:S(2)}, u32[]{:S(2)}) collective-permute-start(bf16[32,1728]{1,0:T(8,128)(2,1)S(1)} %get-tuple-element.150), channel_id=1, source_target_pairs={{0,5},{1,4},{2,7},{3,6},{4,1},{5,0},{6,3},{7,2},{8,13},{9,12},{10,... | collective-permute-start | bytes 331784 | tf_op jit(solution)/shard_map/ppermute | solution.py:415
  36.0 8.5 %collective-permute-start.9 = (bf16[32,1728]{1,0:T(8,128)(2,1)S(1)}, bf16[32,1728]{1,0:T(8,128)(2,1)S(1)}, u32[]{:S(2)}, u32[]{:S(2)}) collective-permute-start(bf16[32,1728]{1,0:T(8,128)(2,1)S(1)} %get-tuple-element.151), channel_id=1, source_target_pairs={{0,7},{1,6},{2,5},{3,4},{4,3},{5,2},{6,1},{7,0},{8,15},{9,14},{10,... | collective-permute-start | bytes 331784 | tf_op jit(solution)/shard_map/ppermute | solution.py:415
  38.2 7.8 %collective-permute-start.10 = (bf16[32,1728]{1,0:T(8,128)(2,1)S(1)}, bf16[32,1728]{1,0:T(8,128)(2,1)S(1)}, u32[]{:S(2)}, u32[]{:S(2)}) collective-permute-start(bf16[32,1728]{1,0:T(8,128)(2,1)S(1)} %get-tuple-element.152), channel_id=1, source_target_pairs={{0,4},{1,5},{2,6},{3,7},{4,0},{5,1},{6,2},{7,3},{8,12},{9,13},{10,... | collective-permute-start | bytes 331784 | tf_op jit(solution)/shard_map/ppermute | solution.py:415
  38.3 7.7 %collective-permute-start.11 = (bf16[32,1728]{1,0:T(8,128)(2,1)S(1)}, bf16[32,1728]{1,0:T(8,128)(2,1)S(1)}, u32[]{:S(2)}, u32[]{:S(2)}) collective-permute-start(bf16[32,1728]{1,0:T(8,128)(2,1)S(1)} %get-tuple-element.153), channel_id=1, source_target_pairs={{0,2},{1,3},{2,0},{3,1},{4,6},{5,7},{6,4},{7,5},{8,10},{9,11},{10,... | collective-permute-start | bytes 331784 | tf_op jit(solution)/shard_map/ppermute | solution.py:415
  40.5 6.1 %collective-permute-start.12 = (bf16[32,1728]{1,0:T(8,128)(2,1)S(1)}, bf16[32,1728]{1,0:T(8,128)(2,1)S(1)}, u32[]{:S(2)}, u32[]{:S(2)}) collective-permute-start(bf16[32,1728]{1,0:T(8,128)(2,1)S(1)} %get-tuple-element.154), channel_id=1, source_target_pairs={{0,1},{1,0},{2,3},{3,2},{4,5},{5,4},{6,7},{7,6},{8,9},{9,8},{10,11... | collective-permute-start | bytes 331784 | tf_op jit(solution)/shard_map/ppermute | solution.py:415
  42.4 6.0 %collective-permute-start.13 = (bf16[32,1728]{1,0:T(8,128)(2,1)S(1)}, bf16[32,1728]{1,0:T(8,128)(2,1)S(1)}, u32[]{:S(2)}, u32[]{:S(2)}) collective-permute-start(bf16[32,1728]{1,0:T(8,128)(2,1)S(1)} %get-tuple-element.155), channel_id=1, source_target_pairs={{0,3},{1,2},{2,1},{3,0},{4,7},{5,6},{6,5},{7,4},{8,11},{9,10},{10,... | collective-permute-start | bytes 331784 | tf_op jit(solution)/shard_map/ppermute | solution.py:415
  48.5 6.6 %collective-permute-start.16 = (bf16[256,1792]{1,0:T(8,128)(2,1)S(1)}, bf16[256,1792]{1,0:T(8,128)(2,1)S(1)}, u32[]{:S(2)}, u32[]{:S(2)}) collective-permute-start(bf16[256,1792]{1,0:T(8,128)(2,1)S(1)} %get-tuple-element.179.refs_2_), channel_id=1, source_target_pairs={{0,8},{1,9},{2,10},{3,11},{4,12},{5,13},{6,14},{7,15},{8,0},{9,1},... | collective-permute-start | bytes 2752520 | tf_op jit(solution)/shard_map/ppermute | solution.py:401
  50.7 2.0 %collective-permute-start.14 = (bf16[576,256]{1,0:T(8,128)(2,1)S(1)}, bf16[576,256]{1,0:T(8,128)(2,1)S(1)}, u32[]{:S(2)}, u32[]{:S(2)}) collective-permute-start(bf16[576,256]{1,0:T(8,128)(2,1)S(1)} %get-tuple-element.177), channel_id=1, source_target_pairs={{0,8},{1,9},{2,10},{3,11},{4,12},{5,13},{6,14},{7,15},{8,0},{9,1},... | collective-permute-start | bytes 884744 | tf_op jit(solution)/shard_map/ppermute | solution.py:401
  51.5 3.6 %collective-permute-start.18 = (bf16[1152,256]{1,0:T(8,128)(2,1)S(1)}, bf16[1152,256]{1,0:T(8,128)(2,1)S(1)}, u32[]{:S(2)}, u32[]{:S(2)}) collective-permute-start(bf16[1152,256]{1,0:T(8,128)(2,1)S(1)} %get-tuple-element.181), channel_id=1, source_target_pairs={{0,8},{1,9},{2,10},{3,11},{4,12},{5,13},{6,14},{7,15},{8,0},{9,1},... | collective-permute-start | bytes 1769480 | tf_op jit(solution)/shard_map/ppermute | solution.py:401
  51.6 3.5 %collective-permute-start.17 = (bf16[256,640]{1,0:T(8,128)(2,1)S(1)}, bf16[256,640]{1,0:T(8,128)(2,1)S(1)}, u32[]{:S(2)}, u32[]{:S(2)}) collective-permute-start(bf16[256,640]{1,0:T(8,128)(2,1)S(1)} %get-tuple-element.207.refs_6_.att_t), channel_id=1, source_target_pairs={{0,8},{1,9},{2,10},{3,11},{4,12},{5,13},{6,14},{7,15},{8,0},{9,1},... | collective-permute-start | bytes 983048 | tf_op jit(solution)/shard_map/ppermute | solution.py:401
  52.0 3.1 %collective-permute-start.19 = (bf16[256,640]{1,0:T(8,128)(2,1)S(1)}, bf16[256,640]{1,0:T(8,128)(2,1)S(1)}, u32[]{:S(2)}, u32[]{:S(2)}) collective-permute-start(bf16[256,640]{1,0:T(8,128)(2,1)S(1)} %get-tuple-element.182.refs_10_), channel_id=1, source_target_pairs={{0,8},{1,9},{2,10},{3,11},{4,12},{5,13},{6,14},{7,15},{8,0},{9,1},... | collective-permute-start | bytes 983048 | tf_op jit(solution)/shard_map/ppermute | solution.py:401
  52.7 2.3 %collective-permute-start.15 = (bf16[576,256]{1,0:T(8,128)(2,1)S(1)}, bf16[576,256]{1,0:T(8,128)(2,1)S(1)}, u32[]{:S(2)}, u32[]{:S(2)}) collective-permute-start(bf16[576,256]{1,0:T(8,128)(2,1)S(1)} %get-tuple-element.178), channel_id=1, source_target_pairs={{0,8},{1,9},{2,10},{3,11},{4,12},{5,13},{6,14},{7,15},{8,0},{9,1},... | collective-permute-start | bytes 884744 | tf_op jit(solution)/shard_map/ppermute | solution.py:401
  55.1 2.9 %collective-permute-start.20 = (bf16[256,1792]{1,0:T(8,128)(2,1)S(1)}, bf16[256,1792]{1,0:T(8,128)(2,1)S(1)}, u32[]{:S(2)}, u32[]{:S(2)}) collective-permute-start(bf16[256,1792]{1,0:T(8,128)(2,1)S(1)} %shard_map.132.refs_2_.qkv_grad), channel_id=1, source_target_pairs={{0,8},{1,9},{2,10},{3,11},{4,12},{5,13},{6,14},{7,15},{8,0},{9,1},... | collective-permute-start | bytes 2752520 | tf_op jit(solution)/shard_map/ppermute | solution.py:401
  59.6 14.3 %collective-permute-start.21 = (bf16[96,4608]{1,0:T(8,128)(2,1)S(1)}, bf16[96,4608]{1,0:T(8,128)(2,1)S(1)}, u32[]{:S(2)}, u32[]{:S(2)}) collective-permute-start(bf16[96,4608]{1,0:T(8,128)(2,1)S(1)} %get-tuple-element.215), channel_id=1, source_target_pairs={{0,96},{1,97},{2,98},{3,99},{4,100},{5,101},{6,102},{7,103},{8,40}... | collective-permute-start | bytes 2654216 | tf_op jit(solution)/shard_map/ppermute | solution.py:410
  62.4 14.6 %collective-permute-start.23 = (bf16[96,4608]{1,0:T(8,128)(2,1)S(1)}, bf16[96,4608]{1,0:T(8,128)(2,1)S(1)}, u32[]{:S(2)}, u32[]{:S(2)}) collective-permute-start(bf16[96,4608]{1,0:T(8,128)(2,1)S(1)} %get-tuple-element.219), channel_id=1, source_target_pairs={{0,20},{1,21},{2,22},{3,23},{4,16},{5,17},{6,18},{7,19},{8,12},{9,... | collective-permute-start | bytes 2654216 | tf_op jit(solution)/shard_map/ppermute | solution.py:410
  65.3 14.3 %collective-permute-start.25 = (bf16[96,4608]{1,0:T(8,128)(2,1)S(1)}, bf16[96,4608]{1,0:T(8,128)(2,1)S(1)}, u32[]{:S(2)}, u32[]{:S(2)}) collective-permute-start(bf16[96,4608]{1,0:T(8,128)(2,1)S(1)} %get-tuple-element.223), channel_id=1, source_target_pairs={{0,3},{1,2},{2,1},{3,0},{4,7},{5,6},{6,5},{7,4},{8,9},{9,8},{10,11... | collective-permute-start | bytes 2654216 | tf_op jit(solution)/shard_map/ppermute | solution.py:410
  74.1 9.6 %collective-permute-start.22 = (bf16[48,4608]{1,0:T(8,128)(2,1)S(1)}, bf16[48,4608]{1,0:T(8,128)(2,1)S(1)}, u32[]{:S(2)}, u32[]{:S(2)}) collective-permute-start(bf16[48,4608]{1,0:T(8,128)(2,1)S(1)} %get-tuple-element.217), channel_id=1, source_target_pairs={{0,20},{1,21},{2,22},{3,23},{4,16},{5,17},{6,18},{7,19},{8,12},{9,... | collective-permute-start | bytes 1327112 | tf_op jit(solution)/shard_map/ppermute | solution.py:410
  77.1 9.6 %collective-permute-start.24 = (bf16[48,4608]{1,0:T(8,128)(2,1)S(1)}, bf16[48,4608]{1,0:T(8,128)(2,1)S(1)}, u32[]{:S(2)}, u32[]{:S(2)}) collective-permute-start(bf16[48,4608]{1,0:T(8,128)(2,1)S(1)} %get-tuple-element.221), channel_id=1, source_target_pairs={{0,3},{1,2},{2,1},{3,0},{4,7},{5,6},{6,5},{7,4},{8,9},{9,8},{10,11... | collective-permute-start | bytes 1327112 | tf_op jit(solution)/shard_map/ppermute | solution.py:410
  79.7 10.2 %collective-permute-start.26 = (bf16[48,4608]{1,0:T(8,128)(2,1)S(1)}, bf16[48,4608]{1,0:T(8,128)(2,1)S(1)}, u32[]{:S(2)}, u32[]{:S(2)}) collective-permute-start(bf16[48,4608]{1,0:T(8,128)(2,1)S(1)} %get-tuple-element.225), channel_id=1, source_target_pairs={{0,96},{1,97},{2,98},{3,99},{4,100},{5,101},{6,102},{7,103},{8,40}... | collective-permute-start | bytes 1327112 | tf_op jit(solution)/shard_map/ppermute | solution.py:410
  83.7 8.3 %collective-permute-start.27 = (bf16[24,4608]{1,0:T(8,128)(2,1)S(1)}, bf16[24,4608]{1,0:T(8,128)(2,1)S(1)}, u32[]{:S(2)}, u32[]{:S(2)}) collective-permute-start(bf16[24,4608]{1,0:T(8,128)(2,1)S(1)} %get-tuple-element.227), channel_id=1, source_target_pairs={{0,3},{1,2},{2,1},{3,0},{4,7},{5,6},{6,5},{7,4},{8,9},{9,8},{10,11... | collective-permute-start | bytes 663560 | tf_op jit(solution)/shard_map/ppermute | solution.py:410
  86.8 8.7 %collective-permute-start.28 = (bf16[24,4608]{1,0:T(8,128)(2,1)S(1)}, bf16[24,4608]{1,0:T(8,128)(2,1)S(1)}, u32[]{:S(2)}, u32[]{:S(2)}) collective-permute-start(bf16[24,4608]{1,0:T(8,128)(2,1)S(1)} %get-tuple-element.228), channel_id=1, source_target_pairs={{0,96},{1,97},{2,98},{3,99},{4,100},{5,101},{6,102},{7,103},{8,40}... | collective-permute-start | bytes 663560 | tf_op jit(solution)/shard_map/ppermute | solution.py:410
  90.0 7.7 %collective-permute-start.29 = (bf16[24,4608]{1,0:T(8,128)(2,1)S(1)}, bf16[24,4608]{1,0:T(8,128)(2,1)S(1)}, u32[]{:S(2)}, u32[]{:S(2)}) collective-permute-start(bf16[24,4608]{1,0:T(8,128)(2,1)S(1)} %get-tuple-element.229), channel_id=1, source_target_pairs={{0,20},{1,21},{2,22},{3,23},{4,16},{5,17},{6,18},{7,19},{8,12},{9,... | collective-permute-start | bytes 663560 | tf_op jit(solution)/shard_map/ppermute | solution.py:410
  98.1 5.1 %collective-permute-start.30 = (bf16[3,13824]{1,0:T(4,128)(2,1)S(1)}, bf16[3,13824]{1,0:T(4,128)(2,1)S(1)}, u32[]{:S(2)}, u32[]{:S(2)}) collective-permute-start(bf16[3,13824]{1,0:T(4,128)(2,1)S(1)} %get-tuple-element.231), channel_id=1, source_target_pairs={{0,32},{1,33},{2,34},{3,35},{4,36},{5,37},{6,38},{7,39},{8,104},{9... | collective-permute-start | bytes 248840 | tf_op jit(solution)/shard_map/ppermute | solution.py:426
  98.2 5.0 %collective-permute-start.31 = (bf16[3,13824]{1,0:T(4,128)(2,1)S(1)}, bf16[3,13824]{1,0:T(4,128)(2,1)S(1)}, u32[]{:S(2)}, u32[]{:S(2)}) collective-permute-start(bf16[3,13824]{1,0:T(4,128)(2,1)S(1)} %get-tuple-element.232), channel_id=1, source_target_pairs={{0,4},{1,5},{2,6},{3,7},{4,0},{5,1},{6,2},{7,3},{8,28},{9,29},{10,... | collective-permute-start | bytes 248840 | tf_op jit(solution)/shard_map/ppermute | solution.py:426
  98.3 9.2 %collective-permute-start.32 = (bf16[3,13824]{1,0:T(4,128)(2,1)S(1)}, bf16[3,13824]{1,0:T(4,128)(2,1)S(1)}, u32[]{:S(2)}, u32[]{:S(2)}) collective-permute-start(bf16[3,13824]{1,0:T(4,128)(2,1)S(1)} %get-tuple-element.233), channel_id=1, source_target_pairs={{0,1},{1,0},{2,3},{3,2},{4,5},{5,4},{6,7},{7,6},{8,11},{9,10},{10,... | collective-permute-start | bytes 248840 | tf_op jit(solution)/shard_map/ppermute | solution.py:426
  98.4 9.2 %collective-permute-start.33 = (bf16[3,13824]{1,0:T(4,128)(2,1)S(1)}, bf16[3,13824]{1,0:T(4,128)(2,1)S(1)}, u32[]{:S(2)}, u32[]{:S(2)}) collective-permute-start(bf16[3,13824]{1,0:T(4,128)(2,1)S(1)} %get-tuple-element.234), channel_id=1, source_target_pairs={{0,36},{1,37},{2,38},{3,39},{4,32},{5,33},{6,34},{7,35},{8,124},{9... | collective-permute-start | bytes 248840 | tf_op jit(solution)/shard_map/ppermute | solution.py:426
  101.6 5.9 %collective-permute-start.34 = (bf16[3,13824]{1,0:T(4,128)(2,1)S(1)}, bf16[3,13824]{1,0:T(4,128)(2,1)S(1)}, u32[]{:S(2)}, u32[]{:S(2)}) collective-permute-start(bf16[3,13824]{1,0:T(4,128)(2,1)S(1)} %get-tuple-element.235), channel_id=1, source_target_pairs={{0,33},{1,32},{2,35},{3,34},{4,37},{5,36},{6,39},{7,38},{8,107},{9... | collective-permute-start | bytes 248840 | tf_op jit(solution)/shard_map/ppermute | solution.py:426
  103.2 5.6 %collective-permute-start.35 = (bf16[3,13824]{1,0:T(4,128)(2,1)S(1)}, bf16[3,13824]{1,0:T(4,128)(2,1)S(1)}, u32[]{:S(2)}, u32[]{:S(2)}) collective-permute-start(bf16[3,13824]{1,0:T(4,128)(2,1)S(1)} %get-tuple-element.236), channel_id=1, source_target_pairs={{0,5},{1,4},{2,7},{3,6},{4,1},{5,0},{6,3},{7,2},{8,31},{9,30},{10,... | collective-permute-start | bytes 248840 | tf_op jit(solution)/shard_map/ppermute | solution.py:426
  103.2 7.0 %collective-permute-start.36 = (bf16[3,13824]{1,0:T(4,128)(2,1)S(1)}, bf16[3,13824]{1,0:T(4,128)(2,1)S(1)}, u32[]{:S(2)}, u32[]{:S(2)}) collective-permute-start(bf16[3,13824]{1,0:T(4,128)(2,1)S(1)} %get-tuple-element.237), channel_id=1, source_target_pairs={{0,37},{1,36},{2,39},{3,38},{4,33},{5,32},{6,35},{7,34},{8,127},{9... | collective-permute-start | bytes 248840 | tf_op jit(solution)/shard_map/ppermute | solution.py:426

commit v3 on v2

--- a/solution.py
+++ b/solution.py
@@ -333,8 +333,8 @@
             rights = [refs[k][:, column : column + width] for k in (right, right_in)]
             tall_left = jnp.concatenate(lefts, axis=1)
             tall_right = jnp.concatenate(rights, axis=0)
-            for at in range(0, width, 576):
-                size = min(576, width - at)
+            for at in range(0, width, 640):
+                size = min(640, width - at)
                 total = dot(tall_left, tall_right[:, at : at + size], 1, 0)
                 for p in range(3):
                     rows = total[192 * p : 192 * p + 192]

time: 112 us -> 112 us (level)
  no operation moved by 1% of the time
where the time goes in v3:
time: 112 us; the launch traced here: 111 us
  starting transfers between devices  56.9 us (51%)
  Pallas kernels  30.7 us (27%)
  waiting for transfers between devices  22.3 us (20%)
    pallas_call x18, Pallas kernels, call(): pl.pallas_call(body, out_shape=tuple(shapes), in_specs=[pl.BlockSpec(memo...  30.7 us
    ppermute x9, starting transfers between devices, along(): return lax.ppermute(value, MESH, pairs(change))  22.8 us
    ppermute x14, starting transfers between devices, step(): lax.ppermute(chunks[k], MESH, [(d, d ^ PEERS[k]) for d in range(128)])  22.7 us
    ppermute x9, waiting for transfers between devices, along(): return lax.ppermute(value, MESH, pairs(change))  10.5 us
    ppermute x7, starting transfers between devices, step(): return lax.ppermute(pieces[t - 1], MESH, pairs(change))  9.39 us
    ppermute x14, waiting for transfers between devices, step(): lax.ppermute(chunks[k], MESH, [(d, d ^ PEERS[k]) for d in range(128)])  8.42 us
    ppermute x7, waiting for transfers between devices, step(): return lax.ppermute(pieces[t - 1], MESH, pairs(change))  2.73 us
  transfers between devices with their start and end apart: 37, of which 18 were waited for; matrix products, arithmetic and copies ran while one was open for 0% of the time, Pallas kernels for 14%

profile of v3, /device:TPU:0, one launch (start us, length us, event | category | flops | bytes accessed | tf_op | source)
XLA Modules:
  0.0 110.7 jit_solution(1187577597538518205)
XLA Ops:
  0.6 7.7 %shard_map.127 = (bf16[256,1152]{1,0:T(8,128)(2,1)S(1)}, bf16[256,1152]{1,0:T(8,128)(2,1)S(1)}, f32[3,2,1152]{2,1,0:T(2,128)S(1)}, f32[2,2,72]{2,1,0:T(2,128)S(1...) custom-call(bf16[256,1152]{1,0:T(8,128)(2,1)} %bitcast.13, ...), custom_call_target="tpu_custom_call" | custom-call | flops 11000000512 | bytes 22536448 | tf_op jit(solution)/shard_map/pallas_call | solution.py:52
  8.3 5.0 %collective-permute-start = (bf16[32,1728]{1,0:T(8,128)(2,1)S(1)}, bf16[32,1728]{1,0:T(8,128)(2,1)S(1)}, u32[]{:S(2)}, u32[]{:S(2)}) collective-permute-start(bf16[32,1728]{1,0:T(8,128)(2,1)S(1)} %get-tuple-element.125), channel_id=1, source_target_pairs={{0,6},{1,7},{2,4},{3,5},{4,2},{5,3},{6,0},{7,1},{8,14},{9,15},{10,... | collective-permute-start | bytes 331784 | tf_op jit(solution)/shard_map/ppermute | solution.py:415
  13.4 0.9 collective-permute-start.1
  14.3 0.2 collective-permute-start.2
  14.5 1.4 %collective-permute-start.3 = (bf16[32,1728]{1,0:T(8,128)(2,1)S(1)}, bf16[32,1728]{1,0:T(8,128)(2,1)S(1)}, u32[]{:S(2)}, u32[]{:S(2)}) collective-permute-start(bf16[32,1728]{1,0:T(8,128)(2,1)S(1)} %get-tuple-element.128), channel_id=1, source_target_pairs={{0,4},{1,5},{2,6},{3,7},{4,0},{5,1},{6,2},{7,3},{8,12},{9,13},{10,... | collective-permute-start | bytes 331784 | tf_op jit(solution)/shard_map/ppermute | solution.py:415
  15.9 3.0 %collective-permute-start.4 = (bf16[32,1728]{1,0:T(8,128)(2,1)S(1)}, bf16[32,1728]{1,0:T(8,128)(2,1)S(1)}, u32[]{:S(2)}, u32[]{:S(2)}) collective-permute-start(bf16[32,1728]{1,0:T(8,128)(2,1)S(1)} %get-tuple-element.129), channel_id=1, source_target_pairs={{0,2},{1,3},{2,0},{3,1},{4,6},{5,7},{6,4},{7,5},{8,10},{9,11},{10,... | collective-permute-start | bytes 331784 | tf_op jit(solution)/shard_map/ppermute | solution.py:415
  18.8 1.0 collective-permute-start.5
  19.9 0.5 collective-permute-done.1.refs_2_
  20.4 0.6 collective-permute-start.6
  21.0 2.7 %shard_map.128 = (bf16[576,1152]{1,0:T(8,128)(2,1)S(1)}, bf16[576,1152]{1,0:T(8,128)(2,1)S(1)}, bf16[1152,256]{1,0:T(8,128)(2,1)S(1)}, bf16[1152,256]{1,0:T(8,128)(2,1)S(1)}, bf16[1728,1152]{1,0:T(8,128)(2,1)S(1)}) custom-call(bf16[256,1152]{1,0:T(8,128)(2,1)S(1)} %get-tuple-element.132.normed, bf16[256,1152]{1,0:T(8,128)(2,1)S(1)} %get-tuple-element.133.scaled, ...), custom_call_target="tpu_custom_call" | custom-call | flops 3080000000 | bytes 12976128 | tf_op jit(solution)/shard_map/pallas_call | solution.py:52
  23.7 0.4 collective-permute-done.3.refs_4_
  24.1 0.7 collective-permute-done.5.refs_6_
  24.8 1.6 %collective-permute-done.6.refs_7_ = bf16[32,1728]{1,0:T(8,128)(2,1)S(1)} collective-permute-done((bf16[32,1728]{1,0:T(8,128)(2,1)S(1)}, bf16[32,1728]{1,0:T(8,128)(2,1)S(1)}, u32[]{:S(2)}, u32[]{:S(2)}) %collective-permute-start.6) | collective-permute-done | bytes 110624 | tf_op jit(solution)/shard_map/ppermute | solution.py:415
  26.4 5.4 %shard_map.129 = (bf16[32,1728]{1,0:T(8,128)(2,1)S(1)}, bf16[32,1728]{1,0:T(8,128)(2,1)S(1)}, bf16[32,1728]{1,0:T(8,128)(2,1)S(1)}, bf16[32,1728]{1,0:T(8,128)(2...) custom-call(bf16[32,1728]{1,0:T(8,128)(2,1)S(1)} %get-tuple-element., ...), custom_call_target="tpu_custom_call" | custom-call | flops 11000000512 | bytes 7286912 | tf_op jit(solution)/shard_map/pallas_call | solution.py:52
  31.8 3.2 %collective-permute-start.7 = (bf16[32,1728]{1,0:T(8,128)(2,1)S(1)}, bf16[32,1728]{1,0:T(8,128)(2,1)S(1)}, u32[]{:S(2)}, u32[]{:S(2)}) collective-permute-start(bf16[32,1728]{1,0:T(8,128)(2,1)S(1)} %get-tuple-element.149), channel_id=1, source_target_pairs={{0,6},{1,7},{2,4},{3,5},{4,2},{5,3},{6,0},{7,1},{8,14},{9,15},{10,... | collective-permute-start | bytes 331784 | tf_op jit(solution)/shard_map/ppermute | solution.py:415
  34.9 1.1 collective-permute-start.8
  36.0 2.2 %collective-permute-start.9 = (bf16[32,1728]{1,0:T(8,128)(2,1)S(1)}, bf16[32,1728]{1,0:T(8,128)(2,1)S(1)}, u32[]{:S(2)}, u32[]{:S(2)}) collective-permute-start(bf16[32,1728]{1,0:T(8,128)(2,1)S(1)} %get-tuple-element.151), channel_id=1, source_target_pairs={{0,7},{1,6},{2,5},{3,4},{4,3},{5,2},{6,1},{7,0},{8,15},{9,14},{10,... | collective-permute-start | bytes 331784 | tf_op jit(solution)/shard_map/ppermute | solution.py:415
  38.3 2.2 %collective-permute-start.11 = (bf16[32,1728]{1,0:T(8,128)(2,1)S(1)}, bf16[32,1728]{1,0:T(8,128)(2,1)S(1)}, u32[]{:S(2)}, u32[]{:S(2)}) collective-permute-start(bf16[32,1728]{1,0:T(8,128)(2,1)S(1)} %get-tuple-element.153), channel_id=1, source_target_pairs={{0,2},{1,3},{2,0},{3,1},{4,6},{5,7},{6,4},{7,5},{8,10},{9,11},{10,... | collective-permute-start | bytes 331784 | tf_op jit(solution)/shard_map/ppermute | solution.py:415
  40.5 1.0 collective-permute-start.12
  41.6 0.9 collective-permute-done.8.refs_2_
  42.4 0.8 collective-permute-start.13
  43.2 0.9 shard_map.130
  44.2 0.4 collective-permute-done.9.refs_3_
  44.6 1.4 %collective-permute-done.10.refs_4_ = bf16[32,1728]{1,0:T(8,128)(2,1)S(1)} collective-permute-done((bf16[32,1728]{1,0:T(8,128)(2,1)S(1)}, bf16[32,1728]{1,0:T(8,128)(2,1)S(1)}, u32[]{:S(2)}, u32[]{:S(2)}) %collective-permute-start.10) | collective-permute-done | bytes 110624 | tf_op jit(solution)/shard_map/ppermute | solution.py:415
  46.0 0.7 collective-permute-done.12.refs_6_
  46.7 1.8 %collective-permute-done.13.refs_7_ = bf16[32,1728]{1,0:T(8,128)(2,1)S(1)} collective-permute-done((bf16[32,1728]{1,0:T(8,128)(2,1)S(1)}, bf16[32,1728]{1,0:T(8,128)(2,1)S(1)}, u32[]{:S(2)}, u32[]{:S(2)}) %collective-permute-start.13) | collective-permute-done | bytes 110624 | tf_op jit(solution)/shard_map/ppermute | solution.py:415
  48.5 2.2 %shard_map.131 = (bf16[256,1152]{1,0:T(8,128)(2,1)S(1)}, f32[256,640]{1,0:T(8,128)S(1)}, bf16[256,640]{1,0:T(8,128)(2,1)S(1)}, bf16[576,256]{1,0:T(8,128)(2,1)S(1)}, bf16[576,256]{1,0:T(8,128)(2,1)S(1)}) custom-call(bf16[32,1728]{1,0:T(8,128)(2,1)S(1)} %get-tuple-element.163.refs_0_, bf16[32,1728]{1,0:T(8,128)(2,1)S(1)} %collective-permute-done.7.refs_1_, ...), custom_call_target="tpu_custom_call" | custom-call | flops 2640000000 | bytes 8236032 | tf_op jit(solution)/shard_map/pallas_call | solution.py:52
  50.7 0.8 collective-permute-start.14
  51.6 0.4 collective-permute-start.17
  52.0 0.1 collective-permute-start.19
  52.1 0.6 collective-permute-done.14.refs_9_
  52.7 0.4 collective-permute-start.15
  53.1 2.0 %shard_map.132.refs_2_.qkv_grad = bf16[256,1792]{1,0:T(8,128)(2,1)S(1)} custom-call(f32[256,640]{1,0:T(8,128)S(1)} %get-tuple-element.174.att_grad, f32[1728,256]{1,0:T(8,128)S(1)} %get-tuple-element.175.qkv_t, f32[8,256,256]{2,1,0:T(8,128)S(1)} %get-tuple-element.176.probs_t, f32[2,2,72]{2,1,0:T(2,128)S(1)} %get-tuple-element.146.refs_9_.gains), custom_call_target="tpu_custom_call" | custom-call | flops 2200000000 | bytes 5440640 | tf_op jit(solution)/shard_map/pallas_call | solution.py:52
  55.1 0.3 collective-permute-start.20
  55.4 2.4 %shard_map.133 = (f32[3,96,4608]{2,1,0:T(8,128)S(1)}, bf16[96,4608]{1,0:T(8,128)(2,1)S(1)}, bf16[96,4608]{1,0:T(8,128)(2,1)S(1)}, bf16[96,4608]{1,0:T(8,128)(2,1)S(1)}) custom-call(bf16[576,256]{1,0:T(8,128)(2,1)S(1)} %get-tuple-element.185.refs_0_, bf16[576,256]{1,0:T(8,128)(2,1)S(1)} %collective-permute-done.15.refs_1_, ...), custom_call_target="tpu_custom_call" | custom-call | flops 2880000000 | bytes 13467648 | tf_op jit(solution)/shard_map/pallas_call | solution.py:52
  57.9 1.4 %shard_map.134 = (f32[3,96,4608]{2,1,0:T(8,128)S(1)}, bf16[96,4608]{1,0:T(8,128)(2,1)S(1)}, bf16[96,4608]{1,0:T(8,128)(2,1)S(1)}, bf16[96,4608]{1,0:T(8,128)(2,1)S(1)}) custom-call(bf16[1152,256]{1,0:T(8,128)(2,1)S(1)} %get-tuple-element.136.refs_4_.refs_0_, ...), custom_call_target="tpu_custom_call", output_to_operand_aliasing={{0}: (4, {}), {1}: (5, {}), {2}: (6, {}), {3}: (7, {})} | custom-call | flops 1728000000 | bytes 18939904 | tf_op jit(solution)/shard_map/pallas_call | solution.py:52
  59.3 2.8 %collective-permute-start.21 = (bf16[96,4608]{1,0:T(8,128)(2,1)S(1)}, bf16[96,4608]{1,0:T(8,128)(2,1)S(1)}, u32[]{:S(2)}, u32[]{:S(2)}) collective-permute-start(bf16[96,4608]{1,0:T(8,128)(2,1)S(1)} %get-tuple-element.215), channel_id=1, source_target_pairs={{0,96},{1,97},{2,98},{3,99},{4,100},{5,101},{6,102},{7,103},{8,40}... | collective-permute-start | bytes 2654216 | tf_op jit(solution)/shard_map/ppermute | solution.py:410
  62.1 2.8 %collective-permute-start.23 = (bf16[96,4608]{1,0:T(8,128)(2,1)S(1)}, bf16[96,4608]{1,0:T(8,128)(2,1)S(1)}, u32[]{:S(2)}, u32[]{:S(2)}) collective-permute-start(bf16[96,4608]{1,0:T(8,128)(2,1)S(1)} %get-tuple-element.219), channel_id=1, source_target_pairs={{0,20},{1,21},{2,22},{3,23},{4,16},{5,17},{6,18},{7,19},{8,12},{9,... | collective-permute-start | bytes 2654216 | tf_op jit(solution)/shard_map/ppermute | solution.py:410
  64.9 2.1 %collective-permute-start.25 = (bf16[96,4608]{1,0:T(8,128)(2,1)S(1)}, bf16[96,4608]{1,0:T(8,128)(2,1)S(1)}, u32[]{:S(2)}, u32[]{:S(2)}) collective-permute-start(bf16[96,4608]{1,0:T(8,128)(2,1)S(1)} %get-tuple-element.223), channel_id=1, source_target_pairs={{0,3},{1,2},{2,1},{3,0},{4,7},{5,6},{6,5},{7,4},{8,9},{9,8},{10,11... | collective-permute-start | bytes 2654216 | tf_op jit(solution)/shard_map/ppermute | solution.py:410
  67.0 1.5 %shard_map.135 = bf16[256,1152]{1,0:T(8,128)(2,1)} custom-call(bf16[256,1152]{1,0:T(8,128)(2,1)S(1)} %get-tuple-element.171.refs_8_.mid, bf16[256,640]{1,0:T(8,128)(2,1)S(1)} %get-tuple-element.207.refs_6_.att_t, f32[3,2,1152]{2,1,0:T(2,128)S(1)} %get-tuple-element.145.refs_8_.refs_10_.mod, bf16[576,1152]{1,0:T(8,128)(2,1)S(1)} %get-tuple-element.208.w_out), custom_call_target="tpu_custom_call" | custom-call | flops 1650000000 | bytes 2862080 | tf_op jit(solution)/shard_map/pallas_call | solution.py:52
  68.5 2.7 %shard_map.136 = bf16[256,1152]{1,0:T(8,128)(2,1)} custom-call(bf16[256,1152]{1,0:T(8,128)(2,1)S(1)} %get-tuple-element.209.mid_grad, bf16[256,1792]{1,0:T(8,128)(2,1)S(1)} %shard_map.132.refs_2_.qkv_grad, bf16[256,1152]{1,0:T(8,128)(2,1)S(1)} %get-tuple-element.210.latents, f32[3,2,1152]{2,1,0:T(2,128)S(1)} %get-tuple-element.145.refs_8_.refs_10_.mod, ...), custom_call_target="tpu_custom_call" | custom-call | flops 2969999872 | bytes 6695936 | tf_op jit(solution)/shard_map/pallas_call | solution.py:52
  71.1 2.5 %collective-permute-done.21.got = bf16[96,4608]{1,0:T(8,128)(2,1)S(1)} collective-permute-done((bf16[96,4608]{1,0:T(8,128)(2,1)S(1)}, bf16[96,4608]{1,0:T(8,128)(2,1)S(1)}, u32[]{:S(2)}, u32[]{:S(2)}) %collective-permute-start.21) | collective-permute-done | bytes 884768 | tf_op jit(solution)/shard_map/ppermute | solution.py:410
  73.6 0.1 shard_map.137
  73.7 2.9 %collective-permute-start.22 = (bf16[48,4608]{1,0:T(8,128)(2,1)S(1)}, bf16[48,4608]{1,0:T(8,128)(2,1)S(1)}, u32[]{:S(2)}, u32[]{:S(2)}) collective-permute-start(bf16[48,4608]{1,0:T(8,128)(2,1)S(1)} %get-tuple-element.217), channel_id=1, source_target_pairs={{0,20},{1,21},{2,22},{3,23},{4,16},{5,17},{6,18},{7,19},{8,12},{9,... | collective-permute-start | bytes 1327112 | tf_op jit(solution)/shard_map/ppermute | solution.py:410
  76.7 0.1 shard_map.139
  76.8 2.1 %collective-permute-start.24 = (bf16[48,4608]{1,0:T(8,128)(2,1)S(1)}, bf16[48,4608]{1,0:T(8,128)(2,1)S(1)}, u32[]{:S(2)}, u32[]{:S(2)}) collective-permute-start(bf16[48,4608]{1,0:T(8,128)(2,1)S(1)} %get-tuple-element.221), channel_id=1, source_target_pairs={{0,3},{1,2},{2,1},{3,0},{4,7},{5,6},{6,5},{7,4},{8,9},{9,8},{10,11... | collective-permute-start | bytes 1327112 | tf_op jit(solution)/shard_map/ppermute | solution.py:410
  78.9 0.2 collective-permute-done.25.got
  79.2 0.1 shard_map.141
  79.3 2.6 %collective-permute-start.26 = (bf16[48,4608]{1,0:T(8,128)(2,1)S(1)}, bf16[48,4608]{1,0:T(8,128)(2,1)S(1)}, u32[]{:S(2)}, u32[]{:S(2)}) collective-permute-start(bf16[48,4608]{1,0:T(8,128)(2,1)S(1)} %get-tuple-element.225), channel_id=1, source_target_pairs={{0,96},{1,97},{2,98},{3,99},{4,100},{5,101},{6,102},{7,103},{8,40}... | collective-permute-start | bytes 1327112 | tf_op jit(solution)/shard_map/ppermute | solution.py:410
  81.9 1.4 %collective-permute-done.22.got = bf16[48,4608]{1,0:T(8,128)(2,1)S(1)} collective-permute-done((bf16[48,4608]{1,0:T(8,128)(2,1)S(1)}, bf16[48,4608]{1,0:T(8,128)(2,1)S(1)}, u32[]{:S(2)}, u32[]{:S(2)}) %collective-permute-start.22) | collective-permute-done | bytes 442400 | tf_op jit(solution)/shard_map/ppermute | solution.py:410
  83.4 2.2 %collective-permute-start.27 = (bf16[24,4608]{1,0:T(8,128)(2,1)S(1)}, bf16[24,4608]{1,0:T(8,128)(2,1)S(1)}, u32[]{:S(2)}, u32[]{:S(2)}) collective-permute-start(bf16[24,4608]{1,0:T(8,128)(2,1)S(1)} %get-tuple-element.227), channel_id=1, source_target_pairs={{0,3},{1,2},{2,1},{3,0},{4,7},{5,6},{6,5},{7,4},{8,9},{9,8},{10,11... | collective-permute-start | bytes 663560 | tf_op jit(solution)/shard_map/ppermute | solution.py:410
  85.7 0.8 collective-permute-done.24.got
  86.5 2.8 %collective-permute-start.28 = (bf16[24,4608]{1,0:T(8,128)(2,1)S(1)}, bf16[24,4608]{1,0:T(8,128)(2,1)S(1)}, u32[]{:S(2)}, u32[]{:S(2)}) collective-permute-start(bf16[24,4608]{1,0:T(8,128)(2,1)S(1)} %get-tuple-element.228), channel_id=1, source_target_pairs={{0,96},{1,97},{2,98},{3,99},{4,100},{5,101},{6,102},{7,103},{8,40}... | collective-permute-start | bytes 663560 | tf_op jit(solution)/shard_map/ppermute | solution.py:410
  89.3 0.1 shard_map.142
  89.4 2.3 %collective-permute-start.29 = (bf16[24,4608]{1,0:T(8,128)(2,1)S(1)}, bf16[24,4608]{1,0:T(8,128)(2,1)S(1)}, u32[]{:S(2)}, u32[]{:S(2)}) collective-permute-start(bf16[24,4608]{1,0:T(8,128)(2,1)S(1)} %get-tuple-element.229), channel_id=1, source_target_pairs={{0,20},{1,21},{2,22},{3,23},{4,16},{5,17},{6,18},{7,19},{8,12},{9,... | collective-permute-start | bytes 663560 | tf_op jit(solution)/shard_map/ppermute | solution.py:410
  91.8 3.1 %collective-permute-done.28.refs_4_ = bf16[24,4608]{1,0:T(8,128)(2,1)S(1)} collective-permute-done((bf16[24,4608]{1,0:T(8,128)(2,1)S(1)}, bf16[24,4608]{1,0:T(8,128)(2,1)S(1)}, u32[]{:S(2)}, u32[]{:S(2)}) %collective-permute-start.28) | collective-permute-done | bytes 221216 | tf_op jit(solution)/shard_map/ppermute | solution.py:410
  94.9 2.5 %collective-permute-done.29.refs_5_ = bf16[24,4608]{1,0:T(8,128)(2,1)S(1)} collective-permute-done((bf16[24,4608]{1,0:T(8,128)(2,1)S(1)}, bf16[24,4608]{1,0:T(8,128)(2,1)S(1)}, u32[]{:S(2)}, u32[]{:S(2)}) %collective-permute-start.29) | collective-permute-done | bytes 221216 | tf_op jit(solution)/shard_map/ppermute | solution.py:410
  97.4 0.4 shard_map.143
  98.0 3.3 %collective-permute-start.33 = (bf16[3,13824]{1,0:T(4,128)(2,1)S(1)}, bf16[3,13824]{1,0:T(4,128)(2,1)S(1)}, u32[]{:S(2)}, u32[]{:S(2)}) collective-permute-start(bf16[3,13824]{1,0:T(4,128)(2,1)S(1)} %get-tuple-element.234), channel_id=1, source_target_pairs={{0,36},{1,37},{2,38},{3,39},{4,32},{5,33},{6,34},{7,35},{8,124},{9... | collective-permute-start | bytes 248840 | tf_op jit(solution)/shard_map/ppermute | solution.py:426
  101.3 1.6 %collective-permute-start.34 = (bf16[3,13824]{1,0:T(4,128)(2,1)S(1)}, bf16[3,13824]{1,0:T(4,128)(2,1)S(1)}, u32[]{:S(2)}, u32[]{:S(2)}) collective-permute-start(bf16[3,13824]{1,0:T(4,128)(2,1)S(1)} %get-tuple-element.235), channel_id=1, source_target_pairs={{0,33},{1,32},{2,35},{3,34},{4,37},{5,36},{6,39},{7,38},{8,107},{9... | collective-permute-start | bytes 248840 | tf_op jit(solution)/shard_map/ppermute | solution.py:426
  102.9 4.3 %collective-permute-start.36 = (bf16[3,13824]{1,0:T(4,128)(2,1)S(1)}, bf16[3,13824]{1,0:T(4,128)(2,1)S(1)}, u32[]{:S(2)}, u32[]{:S(2)}) collective-permute-start(bf16[3,13824]{1,0:T(4,128)(2,1)S(1)} %get-tuple-element.237), channel_id=1, source_target_pairs={{0,37},{1,36},{2,39},{3,38},{4,33},{5,32},{6,35},{7,34},{8,127},{9... | collective-permute-start | bytes 248840 | tf_op jit(solution)/shard_map/ppermute | solution.py:426
  107.2 1.3 %collective-permute-done.35.refs_6_ = bf16[3,13824]{1,0:T(4,128)(2,1)S(1)} collective-permute-done((bf16[3,13824]{1,0:T(4,128)(2,1)S(1)}, bf16[3,13824]{1,0:T(4,128)(2,1)S(1)}, u32[]{:S(2)}, u32[]{:S(2)}) %collective-permute-start.35) | collective-permute-done | bytes 82976 | tf_op jit(solution)/shard_map/ppermute | solution.py:426
  108.5 1.4 %collective-permute-done.36.refs_7_ = bf16[3,13824]{1,0:T(4,128)(2,1)S(1)} collective-permute-done((bf16[3,13824]{1,0:T(4,128)(2,1)S(1)}, bf16[3,13824]{1,0:T(4,128)(2,1)S(1)}, u32[]{:S(2)}, u32[]{:S(2)}) %collective-permute-start.36) | collective-permute-done | bytes 82976 | tf_op jit(solution)/shard_map/ppermute | solution.py:426
  109.9 0.8 shard_map.144
  (28 shorter events, 0.6 us)
Async XLA Ops:
  8.3 10.5 %collective-permute-start = (bf16[32,1728]{1,0:T(8,128)(2,1)S(1)}, bf16[32,1728]{1,0:T(8,128)(2,1)S(1)}, u32[]{:S(2)}, u32[]{:S(2)}) collective-permute-start(bf16[32,1728]{1,0:T(8,128)(2,1)S(1)} %get-tuple-element.125), channel_id=1, source_target_pairs={{0,6},{1,7},{2,4},{3,5},{4,2},{5,3},{6,0},{7,1},{8,14},{9,15},{10,... | collective-permute-start | bytes 331784 | tf_op jit(solution)/shard_map/ppermute | solution.py:415
  13.4 7.0 %collective-permute-start.1 = (bf16[32,1728]{1,0:T(8,128)(2,1)S(1)}, bf16[32,1728]{1,0:T(8,128)(2,1)S(1)}, u32[]{:S(2)}, u32[]{:S(2)}) collective-permute-start(bf16[32,1728]{1,0:T(8,128)(2,1)S(1)} %get-tuple-element.126), channel_id=1, source_target_pairs={{0,5},{1,4},{2,7},{3,6},{4,1},{5,0},{6,3},{7,2},{8,13},{9,12},{10,... | collective-permute-start | bytes 331784 | tf_op jit(solution)/shard_map/ppermute | solution.py:415
  14.3 9.4 %collective-permute-start.2 = (bf16[32,1728]{1,0:T(8,128)(2,1)S(1)}, bf16[32,1728]{1,0:T(8,128)(2,1)S(1)}, u32[]{:S(2)}, u32[]{:S(2)}) collective-permute-start(bf16[32,1728]{1,0:T(8,128)(2,1)S(1)} %get-tuple-element.127), channel_id=1, source_target_pairs={{0,7},{1,6},{2,5},{3,4},{4,3},{5,2},{6,1},{7,0},{8,15},{9,14},{10,... | collective-permute-start | bytes 331784 | tf_op jit(solution)/shard_map/ppermute | solution.py:415
  14.5 9.6 %collective-permute-start.3 = (bf16[32,1728]{1,0:T(8,128)(2,1)S(1)}, bf16[32,1728]{1,0:T(8,128)(2,1)S(1)}, u32[]{:S(2)}, u32[]{:S(2)}) collective-permute-start(bf16[32,1728]{1,0:T(8,128)(2,1)S(1)} %get-tuple-element.128), channel_id=1, source_target_pairs={{0,4},{1,5},{2,6},{3,7},{4,0},{5,1},{6,2},{7,3},{8,12},{9,13},{10,... | collective-permute-start | bytes 331784 | tf_op jit(solution)/shard_map/ppermute | solution.py:415
  15.9 8.2 %collective-permute-start.4 = (bf16[32,1728]{1,0:T(8,128)(2,1)S(1)}, bf16[32,1728]{1,0:T(8,128)(2,1)S(1)}, u32[]{:S(2)}, u32[]{:S(2)}) collective-permute-start(bf16[32,1728]{1,0:T(8,128)(2,1)S(1)} %get-tuple-element.129), channel_id=1, source_target_pairs={{0,2},{1,3},{2,0},{3,1},{4,6},{5,7},{6,4},{7,5},{8,10},{9,11},{10,... | collective-permute-start | bytes 331784 | tf_op jit(solution)/shard_map/ppermute | solution.py:415
  18.8 5.9 %collective-permute-start.5 = (bf16[32,1728]{1,0:T(8,128)(2,1)S(1)}, bf16[32,1728]{1,0:T(8,128)(2,1)S(1)}, u32[]{:S(2)}, u32[]{:S(2)}) collective-permute-start(bf16[32,1728]{1,0:T(8,128)(2,1)S(1)} %get-tuple-element.130), channel_id=1, source_target_pairs={{0,1},{1,0},{2,3},{3,2},{4,5},{5,4},{6,7},{7,6},{8,9},{9,8},{10,11... | collective-permute-start | bytes 331784 | tf_op jit(solution)/shard_map/ppermute | solution.py:415
  20.4 6.0 %collective-permute-start.6 = (bf16[32,1728]{1,0:T(8,128)(2,1)S(1)}, bf16[32,1728]{1,0:T(8,128)(2,1)S(1)}, u32[]{:S(2)}, u32[]{:S(2)}) collective-permute-start(bf16[32,1728]{1,0:T(8,128)(2,1)S(1)} %get-tuple-element.131), channel_id=1, source_target_pairs={{0,3},{1,2},{2,1},{3,0},{4,7},{5,6},{6,5},{7,4},{8,11},{9,10},{10,... | collective-permute-start | bytes 331784 | tf_op jit(solution)/shard_map/ppermute | solution.py:415
  31.8 8.8 %collective-permute-start.7 = (bf16[32,1728]{1,0:T(8,128)(2,1)S(1)}, bf16[32,1728]{1,0:T(8,128)(2,1)S(1)}, u32[]{:S(2)}, u32[]{:S(2)}) collective-permute-start(bf16[32,1728]{1,0:T(8,128)(2,1)S(1)} %get-tuple-element.149), channel_id=1, source_target_pairs={{0,6},{1,7},{2,4},{3,5},{4,2},{5,3},{6,0},{7,1},{8,14},{9,15},{10,... | collective-permute-start | bytes 331784 | tf_op jit(solution)/shard_map/ppermute | solution.py:415
  34.9 7.5 %collective-permute-start.8 = (bf16[32,1728]{1,0:T(8,128)(2,1)S(1)}, bf16[32,1728]{1,0:T(8,128)(2,1)S(1)}, u32[]{:S(2)}, u32[]{:S(2)}) collective-permute-start(bf16[32,1728]{1,0:T(8,128)(2,1)S(1)} %get-tuple-element.150), channel_id=1, source_target_pairs={{0,5},{1,4},{2,7},{3,6},{4,1},{5,0},{6,3},{7,2},{8,13},{9,12},{10,... | collective-permute-start | bytes 331784 | tf_op jit(solution)/shard_map/ppermute | solution.py:415
  36.0 8.5 %collective-permute-start.9 = (bf16[32,1728]{1,0:T(8,128)(2,1)S(1)}, bf16[32,1728]{1,0:T(8,128)(2,1)S(1)}, u32[]{:S(2)}, u32[]{:S(2)}) collective-permute-start(bf16[32,1728]{1,0:T(8,128)(2,1)S(1)} %get-tuple-element.151), channel_id=1, source_target_pairs={{0,7},{1,6},{2,5},{3,4},{4,3},{5,2},{6,1},{7,0},{8,15},{9,14},{10,... | collective-permute-start | bytes 331784 | tf_op jit(solution)/shard_map/ppermute | solution.py:415
  38.2 7.8 %collective-permute-start.10 = (bf16[32,1728]{1,0:T(8,128)(2,1)S(1)}, bf16[32,1728]{1,0:T(8,128)(2,1)S(1)}, u32[]{:S(2)}, u32[]{:S(2)}) collective-permute-start(bf16[32,1728]{1,0:T(8,128)(2,1)S(1)} %get-tuple-element.152), channel_id=1, source_target_pairs={{0,4},{1,5},{2,6},{3,7},{4,0},{5,1},{6,2},{7,3},{8,12},{9,13},{10,... | collective-permute-start | bytes 331784 | tf_op jit(solution)/shard_map/ppermute | solution.py:415
  38.3 7.7 %collective-permute-start.11 = (bf16[32,1728]{1,0:T(8,128)(2,1)S(1)}, bf16[32,1728]{1,0:T(8,128)(2,1)S(1)}, u32[]{:S(2)}, u32[]{:S(2)}) collective-permute-start(bf16[32,1728]{1,0:T(8,128)(2,1)S(1)} %get-tuple-element.153), channel_id=1, source_target_pairs={{0,2},{1,3},{2,0},{3,1},{4,6},{5,7},{6,4},{7,5},{8,10},{9,11},{10,... | collective-permute-start | bytes 331784 | tf_op jit(solution)/shard_map/ppermute | solution.py:415
  40.5 6.1 %collective-permute-start.12 = (bf16[32,1728]{1,0:T(8,128)(2,1)S(1)}, bf16[32,1728]{1,0:T(8,128)(2,1)S(1)}, u32[]{:S(2)}, u32[]{:S(2)}) collective-permute-start(bf16[32,1728]{1,0:T(8,128)(2,1)S(1)} %get-tuple-element.154), channel_id=1, source_target_pairs={{0,1},{1,0},{2,3},{3,2},{4,5},{5,4},{6,7},{7,6},{8,9},{9,8},{10,11... | collective-permute-start | bytes 331784 | tf_op jit(solution)/shard_map/ppermute | solution.py:415
  42.4 6.0 %collective-permute-start.13 = (bf16[32,1728]{1,0:T(8,128)(2,1)S(1)}, bf16[32,1728]{1,0:T(8,128)(2,1)S(1)}, u32[]{:S(2)}, u32[]{:S(2)}) collective-permute-start(bf16[32,1728]{1,0:T(8,128)(2,1)S(1)} %get-tuple-element.155), channel_id=1, source_target_pairs={{0,3},{1,2},{2,1},{3,0},{4,7},{5,6},{6,5},{7,4},{8,11},{9,10},{10,... | collective-permute-start | bytes 331784 | tf_op jit(solution)/shard_map/ppermute | solution.py:415
  48.5 6.6 %collective-permute-start.16 = (bf16[256,1792]{1,0:T(8,128)(2,1)S(1)}, bf16[256,1792]{1,0:T(8,128)(2,1)S(1)}, u32[]{:S(2)}, u32[]{:S(2)}) collective-permute-start(bf16[256,1792]{1,0:T(8,128)(2,1)S(1)} %get-tuple-element.179.refs_2_), channel_id=1, source_target_pairs={{0,8},{1,9},{2,10},{3,11},{4,12},{5,13},{6,14},{7,15},{8,0},{9,1},... | collective-permute-start | bytes 2752520 | tf_op jit(solution)/shard_map/ppermute | solution.py:401
  50.7 2.0 %collective-permute-start.14 = (bf16[576,256]{1,0:T(8,128)(2,1)S(1)}, bf16[576,256]{1,0:T(8,128)(2,1)S(1)}, u32[]{:S(2)}, u32[]{:S(2)}) collective-permute-start(bf16[576,256]{1,0:T(8,128)(2,1)S(1)} %get-tuple-element.177), channel_id=1, source_target_pairs={{0,8},{1,9},{2,10},{3,11},{4,12},{5,13},{6,14},{7,15},{8,0},{9,1},... | collective-permute-start | bytes 884744 | tf_op jit(solution)/shard_map/ppermute | solution.py:401
  51.5 3.6 %collective-permute-start.18 = (bf16[1152,256]{1,0:T(8,128)(2,1)S(1)}, bf16[1152,256]{1,0:T(8,128)(2,1)S(1)}, u32[]{:S(2)}, u32[]{:S(2)}) collective-permute-start(bf16[1152,256]{1,0:T(8,128)(2,1)S(1)} %get-tuple-element.181), channel_id=1, source_target_pairs={{0,8},{1,9},{2,10},{3,11},{4,12},{5,13},{6,14},{7,15},{8,0},{9,1},... | collective-permute-start | bytes 1769480 | tf_op jit(solution)/shard_map/ppermute | solution.py:401
  51.6 3.5 %collective-permute-start.17 = (bf16[256,640]{1,0:T(8,128)(2,1)S(1)}, bf16[256,640]{1,0:T(8,128)(2,1)S(1)}, u32[]{:S(2)}, u32[]{:S(2)}) collective-permute-start(bf16[256,640]{1,0:T(8,128)(2,1)S(1)} %get-tuple-element.207.refs_6_.att_t), channel_id=1, source_target_pairs={{0,8},{1,9},{2,10},{3,11},{4,12},{5,13},{6,14},{7,15},{8,0},{9,1},... | collective-permute-start | bytes 983048 | tf_op jit(solution)/shard_map/ppermute | solution.py:401
  52.0 3.1 %collective-permute-start.19 = (bf16[256,640]{1,0:T(8,128)(2,1)S(1)}, bf16[256,640]{1,0:T(8,128)(2,1)S(1)}, u32[]{:S(2)}, u32[]{:S(2)}) collective-permute-start(bf16[256,640]{1,0:T(8,128)(2,1)S(1)} %get-tuple-element.182.refs_10_), channel_id=1, source_target_pairs={{0,8},{1,9},{2,10},{3,11},{4,12},{5,13},{6,14},{7,15},{8,0},{9,1},... | collective-permute-start | bytes 983048 | tf_op jit(solution)/shard_map/ppermute | solution.py:401
  52.7 2.3 %collective-permute-start.15 = (bf16[576,256]{1,0:T(8,128)(2,1)S(1)}, bf16[576,256]{1,0:T(8,128)(2,1)S(1)}, u32[]{:S(2)}, u32[]{:S(2)}) collective-permute-start(bf16[576,256]{1,0:T(8,128)(2,1)S(1)} %get-tuple-element.178), channel_id=1, source_target_pairs={{0,8},{1,9},{2,10},{3,11},{4,12},{5,13},{6,14},{7,15},{8,0},{9,1},... | collective-permute-start | bytes 884744 | tf_op jit(solution)/shard_map/ppermute | solution.py:401
  55.1 2.7 %collective-permute-start.20 = (bf16[256,1792]{1,0:T(8,128)(2,1)S(1)}, bf16[256,1792]{1,0:T(8,128)(2,1)S(1)}, u32[]{:S(2)}, u32[]{:S(2)}) collective-permute-start(bf16[256,1792]{1,0:T(8,128)(2,1)S(1)} %shard_map.132.refs_2_.qkv_grad), channel_id=1, source_target_pairs={{0,8},{1,9},{2,10},{3,11},{4,12},{5,13},{6,14},{7,15},{8,0},{9,1},... | collective-permute-start | bytes 2752520 | tf_op jit(solution)/shard_map/ppermute | solution.py:401
  59.3 14.3 %collective-permute-start.21 = (bf16[96,4608]{1,0:T(8,128)(2,1)S(1)}, bf16[96,4608]{1,0:T(8,128)(2,1)S(1)}, u32[]{:S(2)}, u32[]{:S(2)}) collective-permute-start(bf16[96,4608]{1,0:T(8,128)(2,1)S(1)} %get-tuple-element.215), channel_id=1, source_target_pairs={{0,96},{1,97},{2,98},{3,99},{4,100},{5,101},{6,102},{7,103},{8,40}... | collective-permute-start | bytes 2654216 | tf_op jit(solution)/shard_map/ppermute | solution.py:410
  62.1 14.6 %collective-permute-start.23 = (bf16[96,4608]{1,0:T(8,128)(2,1)S(1)}, bf16[96,4608]{1,0:T(8,128)(2,1)S(1)}, u32[]{:S(2)}, u32[]{:S(2)}) collective-permute-start(bf16[96,4608]{1,0:T(8,128)(2,1)S(1)} %get-tuple-element.219), channel_id=1, source_target_pairs={{0,20},{1,21},{2,22},{3,23},{4,16},{5,17},{6,18},{7,19},{8,12},{9,... | collective-permute-start | bytes 2654216 | tf_op jit(solution)/shard_map/ppermute | solution.py:410
  64.9 14.3 %collective-permute-start.25 = (bf16[96,4608]{1,0:T(8,128)(2,1)S(1)}, bf16[96,4608]{1,0:T(8,128)(2,1)S(1)}, u32[]{:S(2)}, u32[]{:S(2)}) collective-permute-start(bf16[96,4608]{1,0:T(8,128)(2,1)S(1)} %get-tuple-element.223), channel_id=1, source_target_pairs={{0,3},{1,2},{2,1},{3,0},{4,7},{5,6},{6,5},{7,4},{8,9},{9,8},{10,11... | collective-permute-start | bytes 2654216 | tf_op jit(solution)/shard_map/ppermute | solution.py:410
  73.7 9.6 %collective-permute-start.22 = (bf16[48,4608]{1,0:T(8,128)(2,1)S(1)}, bf16[48,4608]{1,0:T(8,128)(2,1)S(1)}, u32[]{:S(2)}, u32[]{:S(2)}) collective-permute-start(bf16[48,4608]{1,0:T(8,128)(2,1)S(1)} %get-tuple-element.217), channel_id=1, source_target_pairs={{0,20},{1,21},{2,22},{3,23},{4,16},{5,17},{6,18},{7,19},{8,12},{9,... | collective-permute-start | bytes 1327112 | tf_op jit(solution)/shard_map/ppermute | solution.py:410
  76.8 9.6 %collective-permute-start.24 = (bf16[48,4608]{1,0:T(8,128)(2,1)S(1)}, bf16[48,4608]{1,0:T(8,128)(2,1)S(1)}, u32[]{:S(2)}, u32[]{:S(2)}) collective-permute-start(bf16[48,4608]{1,0:T(8,128)(2,1)S(1)} %get-tuple-element.221), channel_id=1, source_target_pairs={{0,3},{1,2},{2,1},{3,0},{4,7},{5,6},{6,5},{7,4},{8,9},{9,8},{10,11... | collective-permute-start | bytes 1327112 | tf_op jit(solution)/shard_map/ppermute | solution.py:410
  79.3 10.0 %collective-permute-start.26 = (bf16[48,4608]{1,0:T(8,128)(2,1)S(1)}, bf16[48,4608]{1,0:T(8,128)(2,1)S(1)}, u32[]{:S(2)}, u32[]{:S(2)}) collective-permute-start(bf16[48,4608]{1,0:T(8,128)(2,1)S(1)} %get-tuple-element.225), channel_id=1, source_target_pairs={{0,96},{1,97},{2,98},{3,99},{4,100},{5,101},{6,102},{7,103},{8,40}... | collective-permute-start | bytes 1327112 | tf_op jit(solution)/shard_map/ppermute | solution.py:410
  83.4 8.4 %collective-permute-start.27 = (bf16[24,4608]{1,0:T(8,128)(2,1)S(1)}, bf16[24,4608]{1,0:T(8,128)(2,1)S(1)}, u32[]{:S(2)}, u32[]{:S(2)}) collective-permute-start(bf16[24,4608]{1,0:T(8,128)(2,1)S(1)} %get-tuple-element.227), channel_id=1, source_target_pairs={{0,3},{1,2},{2,1},{3,0},{4,7},{5,6},{6,5},{7,4},{8,9},{9,8},{10,11... | collective-permute-start | bytes 663560 | tf_op jit(solution)/shard_map/ppermute | solution.py:410
  86.5 8.4 %collective-permute-start.28 = (bf16[24,4608]{1,0:T(8,128)(2,1)S(1)}, bf16[24,4608]{1,0:T(8,128)(2,1)S(1)}, u32[]{:S(2)}, u32[]{:S(2)}) collective-permute-start(bf16[24,4608]{1,0:T(8,128)(2,1)S(1)} %get-tuple-element.228), channel_id=1, source_target_pairs={{0,96},{1,97},{2,98},{3,99},{4,100},{5,101},{6,102},{7,103},{8,40}... | collective-permute-start | bytes 663560 | tf_op jit(solution)/shard_map/ppermute | solution.py:410
  89.4 7.9 %collective-permute-start.29 = (bf16[24,4608]{1,0:T(8,128)(2,1)S(1)}, bf16[24,4608]{1,0:T(8,128)(2,1)S(1)}, u32[]{:S(2)}, u32[]{:S(2)}) collective-permute-start(bf16[24,4608]{1,0:T(8,128)(2,1)S(1)} %get-tuple-element.229), channel_id=1, source_target_pairs={{0,20},{1,21},{2,22},{3,23},{4,16},{5,17},{6,18},{7,19},{8,12},{9,... | collective-permute-start | bytes 663560 | tf_op jit(solution)/shard_map/ppermute | solution.py:410
  97.8 5.1 %collective-permute-start.30 = (bf16[3,13824]{1,0:T(4,128)(2,1)S(1)}, bf16[3,13824]{1,0:T(4,128)(2,1)S(1)}, u32[]{:S(2)}, u32[]{:S(2)}) collective-permute-start(bf16[3,13824]{1,0:T(4,128)(2,1)S(1)} %get-tuple-element.231), channel_id=1, source_target_pairs={{0,32},{1,33},{2,34},{3,35},{4,36},{5,37},{6,38},{7,39},{8,104},{9... | collective-permute-start | bytes 248840 | tf_op jit(solution)/shard_map/ppermute | solution.py:426
  97.8 5.0 %collective-permute-start.31 = (bf16[3,13824]{1,0:T(4,128)(2,1)S(1)}, bf16[3,13824]{1,0:T(4,128)(2,1)S(1)}, u32[]{:S(2)}, u32[]{:S(2)}) collective-permute-start(bf16[3,13824]{1,0:T(4,128)(2,1)S(1)} %get-tuple-element.232), channel_id=1, source_target_pairs={{0,4},{1,5},{2,6},{3,7},{4,0},{5,1},{6,2},{7,3},{8,28},{9,29},{10,... | collective-permute-start | bytes 248840 | tf_op jit(solution)/shard_map/ppermute | solution.py:426
  97.9 9.2 %collective-permute-start.32 = (bf16[3,13824]{1,0:T(4,128)(2,1)S(1)}, bf16[3,13824]{1,0:T(4,128)(2,1)S(1)}, u32[]{:S(2)}, u32[]{:S(2)}) collective-permute-start(bf16[3,13824]{1,0:T(4,128)(2,1)S(1)} %get-tuple-element.233), channel_id=1, source_target_pairs={{0,1},{1,0},{2,3},{3,2},{4,5},{5,4},{6,7},{7,6},{8,11},{9,10},{10,... | collective-permute-start | bytes 248840 | tf_op jit(solution)/shard_map/ppermute | solution.py:426
  98.0 9.2 %collective-permute-start.33 = (bf16[3,13824]{1,0:T(4,128)(2,1)S(1)}, bf16[3,13824]{1,0:T(4,128)(2,1)S(1)}, u32[]{:S(2)}, u32[]{:S(2)}) collective-permute-start(bf16[3,13824]{1,0:T(4,128)(2,1)S(1)} %get-tuple-element.234), channel_id=1, source_target_pairs={{0,36},{1,37},{2,38},{3,39},{4,32},{5,33},{6,34},{7,35},{8,124},{9... | collective-permute-start | bytes 248840 | tf_op jit(solution)/shard_map/ppermute | solution.py:426
  101.3 5.9 %collective-permute-start.34 = (bf16[3,13824]{1,0:T(4,128)(2,1)S(1)}, bf16[3,13824]{1,0:T(4,128)(2,1)S(1)}, u32[]{:S(2)}, u32[]{:S(2)}) collective-permute-start(bf16[3,13824]{1,0:T(4,128)(2,1)S(1)} %get-tuple-element.235), channel_id=1, source_target_pairs={{0,33},{1,32},{2,35},{3,34},{4,37},{5,36},{6,39},{7,38},{8,107},{9... | collective-permute-start | bytes 248840 | tf_op jit(solution)/shard_map/ppermute | solution.py:426
  102.9 5.6 %collective-permute-start.35 = (bf16[3,13824]{1,0:T(4,128)(2,1)S(1)}, bf16[3,13824]{1,0:T(4,128)(2,1)S(1)}, u32[]{:S(2)}, u32[]{:S(2)}) collective-permute-start(bf16[3,13824]{1,0:T(4,128)(2,1)S(1)} %get-tuple-element.236), channel_id=1, source_target_pairs={{0,5},{1,4},{2,7},{3,6},{4,1},{5,0},{6,3},{7,2},{8,31},{9,30},{10,... | collective-permute-start | bytes 248840 | tf_op jit(solution)/shard_map/ppermute | solution.py:426
  102.9 7.0 %collective-permute-start.36 = (bf16[3,13824]{1,0:T(4,128)(2,1)S(1)}, bf16[3,13824]{1,0:T(4,128)(2,1)S(1)}, u32[]{:S(2)}, u32[]{:S(2)}) collective-permute-start(bf16[3,13824]{1,0:T(4,128)(2,1)S(1)} %get-tuple-element.237), channel_id=1, source_target_pairs={{0,37},{1,36},{2,39},{3,38},{4,33},{5,32},{6,35},{7,34},{8,127},{9... | collective-permute-start | bytes 248840 | tf_op jit(solution)/shard_map/ppermute | solution.py:426

commit v4 on v3

--- a/solution.py
+++ b/solution.py
@@ -19,6 +19,7 @@
 LOCAL = 32
 STRIP = 288
 EPS = 1e-06
+FACTOR = HEAD_DIM ** (-0.5) * math.log2(math.e)
 BF = jnp.bfloat16
 F32 = jnp.float32
 MESH = ("dp", "seq")
@@ -127,10 +128,10 @@
         keys = head_norm(qkv[head_rows(1, h), :], pair[1])[1]
         probs[h] = dot(keys, queries, 0, 0)
     for h in range(HEADS):
-        scores = probs[h] * HEAD_DIM ** (-0.5)
+        scores = probs[h]
         if mask is not None:
             scores = jnp.where(mask, scores, -1e30)
-        expo = jnp.exp(scores - jnp.max(scores, axis=0, keepdims=True))
+        expo = jnp.exp2((scores - jnp.max(scores, axis=0, keepdims=True)) * FACTOR)
         probs[h] = expo * (1.0 / jnp.sum(expo, axis=0, keepdims=True))
     for h in range(HEADS):
         values = qkv[head_rows(2, h), :].astype(BF)

time: 112 us -> 112 us (level)
  no operation moved by 1% of the time
where the time goes in v4:
time: 112 us; the launch traced here: 111 us
  starting transfers between devices  57.1 us (51%)
  Pallas kernels  30.5 us (27%)
  waiting for transfers between devices  22.1 us (20%)
    pallas_call x18, Pallas kernels, call(): pl.pallas_call(body, out_shape=tuple(shapes), in_specs=[pl.BlockSpec(memo...  30.5 us
    ppermute x9, starting transfers between devices, along(): return lax.ppermute(value, MESH, pairs(change))  22.8 us
    ppermute x14, starting transfers between devices, step(): lax.ppermute(chunks[k], MESH, [(d, d ^ PEERS[k]) for d in range(128)])  22.8 us
    ppermute x9, waiting for transfers between devices, along(): return lax.ppermute(value, MESH, pairs(change))  10.4 us
    ppermute x7, starting transfers between devices, step(): return lax.ppermute(pieces[t - 1], MESH, pairs(change))  9.39 us
    ppermute x14, waiting for transfers between devices, step(): lax.ppermute(chunks[k], MESH, [(d, d ^ PEERS[k]) for d in range(128)])  8.34 us
    ppermute x7, waiting for transfers between devices, step(): return lax.ppermute(pieces[t - 1], MESH, pairs(change))  2.73 us
  transfers between devices with their start and end apart: 37, of which 18 were waited for; matrix products, arithmetic and copies ran while one was open for 0% of the time, Pallas kernels for 14%

profile of v4, /device:TPU:0, one launch (start us, length us, event | category | flops | bytes accessed | tf_op | source)
XLA Modules:
  0.0 110.5 jit_solution(12168997534047604800)
XLA Ops:
  0.6 7.6 %shard_map.127 = (bf16[256,1152]{1,0:T(8,128)(2,1)S(1)}, bf16[256,1152]{1,0:T(8,128)(2,1)S(1)}, f32[3,2,1152]{2,1,0:T(2,128)S(1)}, f32[2,2,72]{2,1,0:T(2,128)S(1...) custom-call(bf16[256,1152]{1,0:T(8,128)(2,1)} %bitcast.13, ...), custom_call_target="tpu_custom_call" | custom-call | flops 11000000512 | bytes 22536448 | tf_op jit(solution)/shard_map/pallas_call | solution.py:53
  8.2 5.1 %collective-permute-start = (bf16[32,1728]{1,0:T(8,128)(2,1)S(1)}, bf16[32,1728]{1,0:T(8,128)(2,1)S(1)}, u32[]{:S(2)}, u32[]{:S(2)}) collective-permute-start(bf16[32,1728]{1,0:T(8,128)(2,1)S(1)} %get-tuple-element.125), channel_id=1, source_target_pairs={{0,6},{1,7},{2,4},{3,5},{4,2},{5,3},{6,0},{7,1},{8,14},{9,15},{10,... | collective-permute-start | bytes 331784 | tf_op jit(solution)/shard_map/ppermute | solution.py:416
  13.3 0.9 collective-permute-start.1
  14.2 0.2 collective-permute-start.2
  14.4 1.4 %collective-permute-start.3 = (bf16[32,1728]{1,0:T(8,128)(2,1)S(1)}, bf16[32,1728]{1,0:T(8,128)(2,1)S(1)}, u32[]{:S(2)}, u32[]{:S(2)}) collective-permute-start(bf16[32,1728]{1,0:T(8,128)(2,1)S(1)} %get-tuple-element.128), channel_id=1, source_target_pairs={{0,4},{1,5},{2,6},{3,7},{4,0},{5,1},{6,2},{7,3},{8,12},{9,13},{10,... | collective-permute-start | bytes 331784 | tf_op jit(solution)/shard_map/ppermute | solution.py:416
  15.8 3.0 %collective-permute-start.4 = (bf16[32,1728]{1,0:T(8,128)(2,1)S(1)}, bf16[32,1728]{1,0:T(8,128)(2,1)S(1)}, u32[]{:S(2)}, u32[]{:S(2)}) collective-permute-start(bf16[32,1728]{1,0:T(8,128)(2,1)S(1)} %get-tuple-element.129), channel_id=1, source_target_pairs={{0,2},{1,3},{2,0},{3,1},{4,6},{5,7},{6,4},{7,5},{8,10},{9,11},{10,... | collective-permute-start | bytes 331784 | tf_op jit(solution)/shard_map/ppermute | solution.py:416
  18.7 1.0 collective-permute-start.5
  19.8 0.5 collective-permute-done.1.refs_2_
  20.3 0.6 collective-permute-start.6
  20.9 2.7 %shard_map.128 = (bf16[576,1152]{1,0:T(8,128)(2,1)S(1)}, bf16[576,1152]{1,0:T(8,128)(2,1)S(1)}, bf16[1152,256]{1,0:T(8,128)(2,1)S(1)}, bf16[1152,256]{1,0:T(8,128)(2,1)S(1)}, bf16[1728,1152]{1,0:T(8,128)(2,1)S(1)}) custom-call(bf16[256,1152]{1,0:T(8,128)(2,1)S(1)} %get-tuple-element.132.normed, bf16[256,1152]{1,0:T(8,128)(2,1)S(1)} %get-tuple-element.133.scaled, ...), custom_call_target="tpu_custom_call" | custom-call | flops 3080000000 | bytes 12976128 | tf_op jit(solution)/shard_map/pallas_call | solution.py:53
  23.6 0.4 collective-permute-done.3.refs_4_
  24.0 0.7 collective-permute-done.5.refs_6_
  24.7 1.6 %collective-permute-done.6.refs_7_ = bf16[32,1728]{1,0:T(8,128)(2,1)S(1)} collective-permute-done((bf16[32,1728]{1,0:T(8,128)(2,1)S(1)}, bf16[32,1728]{1,0:T(8,128)(2,1)S(1)}, u32[]{:S(2)}, u32[]{:S(2)}) %collective-permute-start.6) | collective-permute-done | bytes 110624 | tf_op jit(solution)/shard_map/ppermute | solution.py:416
  26.3 5.3 %shard_map.129 = (bf16[32,1728]{1,0:T(8,128)(2,1)S(1)}, bf16[32,1728]{1,0:T(8,128)(2,1)S(1)}, bf16[32,1728]{1,0:T(8,128)(2,1)S(1)}, bf16[32,1728]{1,0:T(8,128)(2...) custom-call(bf16[32,1728]{1,0:T(8,128)(2,1)S(1)} %get-tuple-element., ...), custom_call_target="tpu_custom_call" | custom-call | flops 11000000512 | bytes 7286912 | tf_op jit(solution)/shard_map/pallas_call | solution.py:53
  31.6 3.2 %collective-permute-start.7 = (bf16[32,1728]{1,0:T(8,128)(2,1)S(1)}, bf16[32,1728]{1,0:T(8,128)(2,1)S(1)}, u32[]{:S(2)}, u32[]{:S(2)}) collective-permute-start(bf16[32,1728]{1,0:T(8,128)(2,1)S(1)} %get-tuple-element.149), channel_id=1, source_target_pairs={{0,6},{1,7},{2,4},{3,5},{4,2},{5,3},{6,0},{7,1},{8,14},{9,15},{10,... | collective-permute-start | bytes 331784 | tf_op jit(solution)/shard_map/ppermute | solution.py:416
  34.7 1.1 collective-permute-start.8
  35.8 2.2 %collective-permute-start.9 = (bf16[32,1728]{1,0:T(8,128)(2,1)S(1)}, bf16[32,1728]{1,0:T(8,128)(2,1)S(1)}, u32[]{:S(2)}, u32[]{:S(2)}) collective-permute-start(bf16[32,1728]{1,0:T(8,128)(2,1)S(1)} %get-tuple-element.151), channel_id=1, source_target_pairs={{0,7},{1,6},{2,5},{3,4},{4,3},{5,2},{6,1},{7,0},{8,15},{9,14},{10,... | collective-permute-start | bytes 331784 | tf_op jit(solution)/shard_map/ppermute | solution.py:416
  38.1 2.3 %collective-permute-start.11 = (bf16[32,1728]{1,0:T(8,128)(2,1)S(1)}, bf16[32,1728]{1,0:T(8,128)(2,1)S(1)}, u32[]{:S(2)}, u32[]{:S(2)}) collective-permute-start(bf16[32,1728]{1,0:T(8,128)(2,1)S(1)} %get-tuple-element.153), channel_id=1, source_target_pairs={{0,2},{1,3},{2,0},{3,1},{4,6},{5,7},{6,4},{7,5},{8,10},{9,11},{10,... | collective-permute-start | bytes 331784 | tf_op jit(solution)/shard_map/ppermute | solution.py:416
  40.4 1.0 collective-permute-start.12
  41.4 0.9 collective-permute-done.8.refs_2_
  42.3 0.8 collective-permute-start.13
  43.1 0.9 shard_map.130
  44.0 0.3 collective-permute-done.9.refs_3_
  44.4 1.4 %collective-permute-done.10.refs_4_ = bf16[32,1728]{1,0:T(8,128)(2,1)S(1)} collective-permute-done((bf16[32,1728]{1,0:T(8,128)(2,1)S(1)}, bf16[32,1728]{1,0:T(8,128)(2,1)S(1)}, u32[]{:S(2)}, u32[]{:S(2)}) %collective-permute-start.10) | collective-permute-done | bytes 110624 | tf_op jit(solution)/shard_map/ppermute | solution.py:416
  45.8 0.7 collective-permute-done.12.refs_6_
  46.5 1.8 %collective-permute-done.13.refs_7_ = bf16[32,1728]{1,0:T(8,128)(2,1)S(1)} collective-permute-done((bf16[32,1728]{1,0:T(8,128)(2,1)S(1)}, bf16[32,1728]{1,0:T(8,128)(2,1)S(1)}, u32[]{:S(2)}, u32[]{:S(2)}) %collective-permute-start.13) | collective-permute-done | bytes 110624 | tf_op jit(solution)/shard_map/ppermute | solution.py:416
  48.3 2.2 %shard_map.131 = (bf16[256,1152]{1,0:T(8,128)(2,1)S(1)}, f32[256,640]{1,0:T(8,128)S(1)}, bf16[256,640]{1,0:T(8,128)(2,1)S(1)}, bf16[576,256]{1,0:T(8,128)(2,1)S(1)}, bf16[576,256]{1,0:T(8,128)(2,1)S(1)}) custom-call(bf16[32,1728]{1,0:T(8,128)(2,1)S(1)} %get-tuple-element.163.refs_0_, bf16[32,1728]{1,0:T(8,128)(2,1)S(1)} %collective-permute-done.7.refs_1_, ...), custom_call_target="tpu_custom_call" | custom-call | flops 2640000000 | bytes 8236032 | tf_op jit(solution)/shard_map/pallas_call | solution.py:53
  50.5 0.8 collective-permute-start.14
  51.3 0.1 collective-permute-start.18
  51.4 0.4 collective-permute-start.17
  51.9 0.6 collective-permute-done.14.refs_9_
  52.5 0.4 collective-permute-start.15
  52.9 2.0 %shard_map.132.refs_2_.qkv_grad = bf16[256,1792]{1,0:T(8,128)(2,1)S(1)} custom-call(f32[256,640]{1,0:T(8,128)S(1)} %get-tuple-element.174.att_grad, f32[1728,256]{1,0:T(8,128)S(1)} %get-tuple-element.175.qkv_t, f32[8,256,256]{2,1,0:T(8,128)S(1)} %get-tuple-element.176.probs_t, f32[2,2,72]{2,1,0:T(2,128)S(1)} %get-tuple-element.146.refs_9_.gains), custom_call_target="tpu_custom_call" | custom-call | flops 2200000000 | bytes 5440640 | tf_op jit(solution)/shard_map/pallas_call | solution.py:53
  54.9 0.3 collective-permute-start.20
  55.2 2.4 %shard_map.133 = (f32[3,96,4608]{2,1,0:T(8,128)S(1)}, bf16[96,4608]{1,0:T(8,128)(2,1)S(1)}, bf16[96,4608]{1,0:T(8,128)(2,1)S(1)}, bf16[96,4608]{1,0:T(8,128)(2,1)S(1)}) custom-call(bf16[576,256]{1,0:T(8,128)(2,1)S(1)} %get-tuple-element.185.refs_0_, bf16[576,256]{1,0:T(8,128)(2,1)S(1)} %collective-permute-done.15.refs_1_, ...), custom_call_target="tpu_custom_call" | custom-call | flops 2880000000 | bytes 13467648 | tf_op jit(solution)/shard_map/pallas_call | solution.py:53
  57.7 1.4 %shard_map.134 = (f32[3,96,4608]{2,1,0:T(8,128)S(1)}, bf16[96,4608]{1,0:T(8,128)(2,1)S(1)}, bf16[96,4608]{1,0:T(8,128)(2,1)S(1)}, bf16[96,4608]{1,0:T(8,128)(2,1)S(1)}) custom-call(bf16[1152,256]{1,0:T(8,128)(2,1)S(1)} %get-tuple-element.136.refs_4_.refs_0_, ...), custom_call_target="tpu_custom_call", output_to_operand_aliasing={{0}: (4, {}), {1}: (5, {}), {2}: (6, {}), {3}: (7, {})} | custom-call | flops 1728000000 | bytes 18939904 | tf_op jit(solution)/shard_map/pallas_call | solution.py:53
  59.1 2.8 %collective-permute-start.21 = (bf16[96,4608]{1,0:T(8,128)(2,1)S(1)}, bf16[96,4608]{1,0:T(8,128)(2,1)S(1)}, u32[]{:S(2)}, u32[]{:S(2)}) collective-permute-start(bf16[96,4608]{1,0:T(8,128)(2,1)S(1)} %get-tuple-element.215), channel_id=1, source_target_pairs={{0,96},{1,97},{2,98},{3,99},{4,100},{5,101},{6,102},{7,103},{8,40}... | collective-permute-start | bytes 2654216 | tf_op jit(solution)/shard_map/ppermute | solution.py:411
  61.9 2.8 %collective-permute-start.23 = (bf16[96,4608]{1,0:T(8,128)(2,1)S(1)}, bf16[96,4608]{1,0:T(8,128)(2,1)S(1)}, u32[]{:S(2)}, u32[]{:S(2)}) collective-permute-start(bf16[96,4608]{1,0:T(8,128)(2,1)S(1)} %get-tuple-element.219), channel_id=1, source_target_pairs={{0,20},{1,21},{2,22},{3,23},{4,16},{5,17},{6,18},{7,19},{8,12},{9,... | collective-permute-start | bytes 2654216 | tf_op jit(solution)/shard_map/ppermute | solution.py:411
  64.7 2.1 %collective-permute-start.25 = (bf16[96,4608]{1,0:T(8,128)(2,1)S(1)}, bf16[96,4608]{1,0:T(8,128)(2,1)S(1)}, u32[]{:S(2)}, u32[]{:S(2)}) collective-permute-start(bf16[96,4608]{1,0:T(8,128)(2,1)S(1)} %get-tuple-element.223), channel_id=1, source_target_pairs={{0,3},{1,2},{2,1},{3,0},{4,7},{5,6},{6,5},{7,4},{8,9},{9,8},{10,11... | collective-permute-start | bytes 2654216 | tf_op jit(solution)/shard_map/ppermute | solution.py:411
  66.8 1.5 %shard_map.135 = bf16[256,1152]{1,0:T(8,128)(2,1)} custom-call(bf16[256,1152]{1,0:T(8,128)(2,1)S(1)} %get-tuple-element.171.refs_8_.mid, bf16[256,640]{1,0:T(8,128)(2,1)S(1)} %get-tuple-element.207.refs_6_.att_t, f32[3,2,1152]{2,1,0:T(2,128)S(1)} %get-tuple-element.145.refs_8_.refs_10_.mod, bf16[576,1152]{1,0:T(8,128)(2,1)S(1)} %get-tuple-element.208.w_out), custom_call_target="tpu_custom_call" | custom-call | flops 1650000000 | bytes 2862080 | tf_op jit(solution)/shard_map/pallas_call | solution.py:53
  68.3 2.7 %shard_map.136 = bf16[256,1152]{1,0:T(8,128)(2,1)} custom-call(bf16[256,1152]{1,0:T(8,128)(2,1)S(1)} %get-tuple-element.209.mid_grad, bf16[256,1792]{1,0:T(8,128)(2,1)S(1)} %shard_map.132.refs_2_.qkv_grad, bf16[256,1152]{1,0:T(8,128)(2,1)S(1)} %get-tuple-element.210.latents, f32[3,2,1152]{2,1,0:T(2,128)S(1)} %get-tuple-element.145.refs_8_.refs_10_.mod, ...), custom_call_target="tpu_custom_call" | custom-call | flops 2969999872 | bytes 6695936 | tf_op jit(solution)/shard_map/pallas_call | solution.py:53
  70.9 2.5 %collective-permute-done.21.got = bf16[96,4608]{1,0:T(8,128)(2,1)S(1)} collective-permute-done((bf16[96,4608]{1,0:T(8,128)(2,1)S(1)}, bf16[96,4608]{1,0:T(8,128)(2,1)S(1)}, u32[]{:S(2)}, u32[]{:S(2)}) %collective-permute-start.21) | collective-permute-done | bytes 884768 | tf_op jit(solution)/shard_map/ppermute | solution.py:411
  73.4 0.1 shard_map.137
  73.6 2.9 %collective-permute-start.22 = (bf16[48,4608]{1,0:T(8,128)(2,1)S(1)}, bf16[48,4608]{1,0:T(8,128)(2,1)S(1)}, u32[]{:S(2)}, u32[]{:S(2)}) collective-permute-start(bf16[48,4608]{1,0:T(8,128)(2,1)S(1)} %get-tuple-element.217), channel_id=1, source_target_pairs={{0,20},{1,21},{2,22},{3,23},{4,16},{5,17},{6,18},{7,19},{8,12},{9,... | collective-permute-start | bytes 1327112 | tf_op jit(solution)/shard_map/ppermute | solution.py:411
  76.5 0.1 shard_map.139
  76.6 2.1 %collective-permute-start.24 = (bf16[48,4608]{1,0:T(8,128)(2,1)S(1)}, bf16[48,4608]{1,0:T(8,128)(2,1)S(1)}, u32[]{:S(2)}, u32[]{:S(2)}) collective-permute-start(bf16[48,4608]{1,0:T(8,128)(2,1)S(1)} %get-tuple-element.221), channel_id=1, source_target_pairs={{0,3},{1,2},{2,1},{3,0},{4,7},{5,6},{6,5},{7,4},{8,9},{9,8},{10,11... | collective-permute-start | bytes 1327112 | tf_op jit(solution)/shard_map/ppermute | solution.py:411
  78.8 0.2 collective-permute-done.25.got
  79.0 0.1 shard_map.141
  79.1 2.6 %collective-permute-start.26 = (bf16[48,4608]{1,0:T(8,128)(2,1)S(1)}, bf16[48,4608]{1,0:T(8,128)(2,1)S(1)}, u32[]{:S(2)}, u32[]{:S(2)}) collective-permute-start(bf16[48,4608]{1,0:T(8,128)(2,1)S(1)} %get-tuple-element.225), channel_id=1, source_target_pairs={{0,96},{1,97},{2,98},{3,99},{4,100},{5,101},{6,102},{7,103},{8,40}... | collective-permute-start | bytes 1327112 | tf_op jit(solution)/shard_map/ppermute | solution.py:411
  81.8 1.4 %collective-permute-done.22.got = bf16[48,4608]{1,0:T(8,128)(2,1)S(1)} collective-permute-done((bf16[48,4608]{1,0:T(8,128)(2,1)S(1)}, bf16[48,4608]{1,0:T(8,128)(2,1)S(1)}, u32[]{:S(2)}, u32[]{:S(2)}) %collective-permute-start.22) | collective-permute-done | bytes 442400 | tf_op jit(solution)/shard_map/ppermute | solution.py:411
  83.2 2.2 %collective-permute-start.27 = (bf16[24,4608]{1,0:T(8,128)(2,1)S(1)}, bf16[24,4608]{1,0:T(8,128)(2,1)S(1)}, u32[]{:S(2)}, u32[]{:S(2)}) collective-permute-start(bf16[24,4608]{1,0:T(8,128)(2,1)S(1)} %get-tuple-element.227), channel_id=1, source_target_pairs={{0,3},{1,2},{2,1},{3,0},{4,7},{5,6},{6,5},{7,4},{8,9},{9,8},{10,11... | collective-permute-start | bytes 663560 | tf_op jit(solution)/shard_map/ppermute | solution.py:411
  85.5 0.7 collective-permute-done.24.got
  86.3 2.8 %collective-permute-start.28 = (bf16[24,4608]{1,0:T(8,128)(2,1)S(1)}, bf16[24,4608]{1,0:T(8,128)(2,1)S(1)}, u32[]{:S(2)}, u32[]{:S(2)}) collective-permute-start(bf16[24,4608]{1,0:T(8,128)(2,1)S(1)} %get-tuple-element.228), channel_id=1, source_target_pairs={{0,96},{1,97},{2,98},{3,99},{4,100},{5,101},{6,102},{7,103},{8,40}... | collective-permute-start | bytes 663560 | tf_op jit(solution)/shard_map/ppermute | solution.py:411
  89.1 0.1 shard_map.142
  89.2 2.3 %collective-permute-start.29 = (bf16[24,4608]{1,0:T(8,128)(2,1)S(1)}, bf16[24,4608]{1,0:T(8,128)(2,1)S(1)}, u32[]{:S(2)}, u32[]{:S(2)}) collective-permute-start(bf16[24,4608]{1,0:T(8,128)(2,1)S(1)} %get-tuple-element.229), channel_id=1, source_target_pairs={{0,20},{1,21},{2,22},{3,23},{4,16},{5,17},{6,18},{7,19},{8,12},{9,... | collective-permute-start | bytes 663560 | tf_op jit(solution)/shard_map/ppermute | solution.py:411
  91.6 3.1 %collective-permute-done.28.refs_4_ = bf16[24,4608]{1,0:T(8,128)(2,1)S(1)} collective-permute-done((bf16[24,4608]{1,0:T(8,128)(2,1)S(1)}, bf16[24,4608]{1,0:T(8,128)(2,1)S(1)}, u32[]{:S(2)}, u32[]{:S(2)}) %collective-permute-start.28) | collective-permute-done | bytes 221216 | tf_op jit(solution)/shard_map/ppermute | solution.py:411
  94.7 2.5 %collective-permute-done.29.refs_5_ = bf16[24,4608]{1,0:T(8,128)(2,1)S(1)} collective-permute-done((bf16[24,4608]{1,0:T(8,128)(2,1)S(1)}, bf16[24,4608]{1,0:T(8,128)(2,1)S(1)}, u32[]{:S(2)}, u32[]{:S(2)}) %collective-permute-start.29) | collective-permute-done | bytes 221216 | tf_op jit(solution)/shard_map/ppermute | solution.py:411
  97.2 0.4 shard_map.143
  97.9 3.3 %collective-permute-start.33 = (bf16[3,13824]{1,0:T(4,128)(2,1)S(1)}, bf16[3,13824]{1,0:T(4,128)(2,1)S(1)}, u32[]{:S(2)}, u32[]{:S(2)}) collective-permute-start(bf16[3,13824]{1,0:T(4,128)(2,1)S(1)} %get-tuple-element.234), channel_id=1, source_target_pairs={{0,36},{1,37},{2,38},{3,39},{4,32},{5,33},{6,34},{7,35},{8,124},{9... | collective-permute-start | bytes 248840 | tf_op jit(solution)/shard_map/ppermute | solution.py:427
  101.1 1.6 %collective-permute-start.34 = (bf16[3,13824]{1,0:T(4,128)(2,1)S(1)}, bf16[3,13824]{1,0:T(4,128)(2,1)S(1)}, u32[]{:S(2)}, u32[]{:S(2)}) collective-permute-start(bf16[3,13824]{1,0:T(4,128)(2,1)S(1)} %get-tuple-element.235), channel_id=1, source_target_pairs={{0,33},{1,32},{2,35},{3,34},{4,37},{5,36},{6,39},{7,38},{8,107},{9... | collective-permute-start | bytes 248840 | tf_op jit(solution)/shard_map/ppermute | solution.py:427
  102.7 4.3 %collective-permute-start.36 = (bf16[3,13824]{1,0:T(4,128)(2,1)S(1)}, bf16[3,13824]{1,0:T(4,128)(2,1)S(1)}, u32[]{:S(2)}, u32[]{:S(2)}) collective-permute-start(bf16[3,13824]{1,0:T(4,128)(2,1)S(1)} %get-tuple-element.237), channel_id=1, source_target_pairs={{0,37},{1,36},{2,39},{3,38},{4,33},{5,32},{6,35},{7,34},{8,127},{9... | collective-permute-start | bytes 248840 | tf_op jit(solution)/shard_map/ppermute | solution.py:427
  107.0 1.3 %collective-permute-done.35.refs_6_ = bf16[3,13824]{1,0:T(4,128)(2,1)S(1)} collective-permute-done((bf16[3,13824]{1,0:T(4,128)(2,1)S(1)}, bf16[3,13824]{1,0:T(4,128)(2,1)S(1)}, u32[]{:S(2)}, u32[]{:S(2)}) %collective-permute-start.35) | collective-permute-done | bytes 82976 | tf_op jit(solution)/shard_map/ppermute | solution.py:427
  108.3 1.4 %collective-permute-done.36.refs_7_ = bf16[3,13824]{1,0:T(4,128)(2,1)S(1)} collective-permute-done((bf16[3,13824]{1,0:T(4,128)(2,1)S(1)}, bf16[3,13824]{1,0:T(4,128)(2,1)S(1)}, u32[]{:S(2)}, u32[]{:S(2)}) %collective-permute-start.36) | collective-permute-done | bytes 82976 | tf_op jit(solution)/shard_map/ppermute | solution.py:427
  109.7 0.8 shard_map.144
  (28 shorter events, 0.6 us)
Async XLA Ops:
  8.2 10.5 %collective-permute-start = (bf16[32,1728]{1,0:T(8,128)(2,1)S(1)}, bf16[32,1728]{1,0:T(8,128)(2,1)S(1)}, u32[]{:S(2)}, u32[]{:S(2)}) collective-permute-start(bf16[32,1728]{1,0:T(8,128)(2,1)S(1)} %get-tuple-element.125), channel_id=1, source_target_pairs={{0,6},{1,7},{2,4},{3,5},{4,2},{5,3},{6,0},{7,1},{8,14},{9,15},{10,... | collective-permute-start | bytes 331784 | tf_op jit(solution)/shard_map/ppermute | solution.py:416
  13.3 7.0 %collective-permute-start.1 = (bf16[32,1728]{1,0:T(8,128)(2,1)S(1)}, bf16[32,1728]{1,0:T(8,128)(2,1)S(1)}, u32[]{:S(2)}, u32[]{:S(2)}) collective-permute-start(bf16[32,1728]{1,0:T(8,128)(2,1)S(1)} %get-tuple-element.126), channel_id=1, source_target_pairs={{0,5},{1,4},{2,7},{3,6},{4,1},{5,0},{6,3},{7,2},{8,13},{9,12},{10,... | collective-permute-start | bytes 331784 | tf_op jit(solution)/shard_map/ppermute | solution.py:416
  14.2 9.4 %collective-permute-start.2 = (bf16[32,1728]{1,0:T(8,128)(2,1)S(1)}, bf16[32,1728]{1,0:T(8,128)(2,1)S(1)}, u32[]{:S(2)}, u32[]{:S(2)}) collective-permute-start(bf16[32,1728]{1,0:T(8,128)(2,1)S(1)} %get-tuple-element.127), channel_id=1, source_target_pairs={{0,7},{1,6},{2,5},{3,4},{4,3},{5,2},{6,1},{7,0},{8,15},{9,14},{10,... | collective-permute-start | bytes 331784 | tf_op jit(solution)/shard_map/ppermute | solution.py:416
  14.4 9.6 %collective-permute-start.3 = (bf16[32,1728]{1,0:T(8,128)(2,1)S(1)}, bf16[32,1728]{1,0:T(8,128)(2,1)S(1)}, u32[]{:S(2)}, u32[]{:S(2)}) collective-permute-start(bf16[32,1728]{1,0:T(8,128)(2,1)S(1)} %get-tuple-element.128), channel_id=1, source_target_pairs={{0,4},{1,5},{2,6},{3,7},{4,0},{5,1},{6,2},{7,3},{8,12},{9,13},{10,... | collective-permute-start | bytes 331784 | tf_op jit(solution)/shard_map/ppermute | solution.py:416
  15.8 8.2 %collective-permute-start.4 = (bf16[32,1728]{1,0:T(8,128)(2,1)S(1)}, bf16[32,1728]{1,0:T(8,128)(2,1)S(1)}, u32[]{:S(2)}, u32[]{:S(2)}) collective-permute-start(bf16[32,1728]{1,0:T(8,128)(2,1)S(1)} %get-tuple-element.129), channel_id=1, source_target_pairs={{0,2},{1,3},{2,0},{3,1},{4,6},{5,7},{6,4},{7,5},{8,10},{9,11},{10,... | collective-permute-start | bytes 331784 | tf_op jit(solution)/shard_map/ppermute | solution.py:416
  18.7 5.9 %collective-permute-start.5 = (bf16[32,1728]{1,0:T(8,128)(2,1)S(1)}, bf16[32,1728]{1,0:T(8,128)(2,1)S(1)}, u32[]{:S(2)}, u32[]{:S(2)}) collective-permute-start(bf16[32,1728]{1,0:T(8,128)(2,1)S(1)} %get-tuple-element.130), channel_id=1, source_target_pairs={{0,1},{1,0},{2,3},{3,2},{4,5},{5,4},{6,7},{7,6},{8,9},{9,8},{10,11... | collective-permute-start | bytes 331784 | tf_op jit(solution)/shard_map/ppermute | solution.py:416
  20.3 6.0 %collective-permute-start.6 = (bf16[32,1728]{1,0:T(8,128)(2,1)S(1)}, bf16[32,1728]{1,0:T(8,128)(2,1)S(1)}, u32[]{:S(2)}, u32[]{:S(2)}) collective-permute-start(bf16[32,1728]{1,0:T(8,128)(2,1)S(1)} %get-tuple-element.131), channel_id=1, source_target_pairs={{0,3},{1,2},{2,1},{3,0},{4,7},{5,6},{6,5},{7,4},{8,11},{9,10},{10,... | collective-permute-start | bytes 331784 | tf_op jit(solution)/shard_map/ppermute | solution.py:416
  31.6 8.8 %collective-permute-start.7 = (bf16[32,1728]{1,0:T(8,128)(2,1)S(1)}, bf16[32,1728]{1,0:T(8,128)(2,1)S(1)}, u32[]{:S(2)}, u32[]{:S(2)}) collective-permute-start(bf16[32,1728]{1,0:T(8,128)(2,1)S(1)} %get-tuple-element.149), channel_id=1, source_target_pairs={{0,6},{1,7},{2,4},{3,5},{4,2},{5,3},{6,0},{7,1},{8,14},{9,15},{10,... | collective-permute-start | bytes 331784 | tf_op jit(solution)/shard_map/ppermute | solution.py:416
  34.7 7.5 %collective-permute-start.8 = (bf16[32,1728]{1,0:T(8,128)(2,1)S(1)}, bf16[32,1728]{1,0:T(8,128)(2,1)S(1)}, u32[]{:S(2)}, u32[]{:S(2)}) collective-permute-start(bf16[32,1728]{1,0:T(8,128)(2,1)S(1)} %get-tuple-element.150), channel_id=1, source_target_pairs={{0,5},{1,4},{2,7},{3,6},{4,1},{5,0},{6,3},{7,2},{8,13},{9,12},{10,... | collective-permute-start | bytes 331784 | tf_op jit(solution)/shard_map/ppermute | solution.py:416
  35.8 8.5 %collective-permute-start.9 = (bf16[32,1728]{1,0:T(8,128)(2,1)S(1)}, bf16[32,1728]{1,0:T(8,128)(2,1)S(1)}, u32[]{:S(2)}, u32[]{:S(2)}) collective-permute-start(bf16[32,1728]{1,0:T(8,128)(2,1)S(1)} %get-tuple-element.151), channel_id=1, source_target_pairs={{0,7},{1,6},{2,5},{3,4},{4,3},{5,2},{6,1},{7,0},{8,15},{9,14},{10,... | collective-permute-start | bytes 331784 | tf_op jit(solution)/shard_map/ppermute | solution.py:416
  38.0 7.8 %collective-permute-start.10 = (bf16[32,1728]{1,0:T(8,128)(2,1)S(1)}, bf16[32,1728]{1,0:T(8,128)(2,1)S(1)}, u32[]{:S(2)}, u32[]{:S(2)}) collective-permute-start(bf16[32,1728]{1,0:T(8,128)(2,1)S(1)} %get-tuple-element.152), channel_id=1, source_target_pairs={{0,4},{1,5},{2,6},{3,7},{4,0},{5,1},{6,2},{7,3},{8,12},{9,13},{10,... | collective-permute-start | bytes 331784 | tf_op jit(solution)/shard_map/ppermute | solution.py:416
  38.1 7.7 %collective-permute-start.11 = (bf16[32,1728]{1,0:T(8,128)(2,1)S(1)}, bf16[32,1728]{1,0:T(8,128)(2,1)S(1)}, u32[]{:S(2)}, u32[]{:S(2)}) collective-permute-start(bf16[32,1728]{1,0:T(8,128)(2,1)S(1)} %get-tuple-element.153), channel_id=1, source_target_pairs={{0,2},{1,3},{2,0},{3,1},{4,6},{5,7},{6,4},{7,5},{8,10},{9,11},{10,... | collective-permute-start | bytes 331784 | tf_op jit(solution)/shard_map/ppermute | solution.py:416
  40.4 6.1 %collective-permute-start.12 = (bf16[32,1728]{1,0:T(8,128)(2,1)S(1)}, bf16[32,1728]{1,0:T(8,128)(2,1)S(1)}, u32[]{:S(2)}, u32[]{:S(2)}) collective-permute-start(bf16[32,1728]{1,0:T(8,128)(2,1)S(1)} %get-tuple-element.154), channel_id=1, source_target_pairs={{0,1},{1,0},{2,3},{3,2},{4,5},{5,4},{6,7},{7,6},{8,9},{9,8},{10,11... | collective-permute-start | bytes 331784 | tf_op jit(solution)/shard_map/ppermute | solution.py:416
  42.3 6.0 %collective-permute-start.13 = (bf16[32,1728]{1,0:T(8,128)(2,1)S(1)}, bf16[32,1728]{1,0:T(8,128)(2,1)S(1)}, u32[]{:S(2)}, u32[]{:S(2)}) collective-permute-start(bf16[32,1728]{1,0:T(8,128)(2,1)S(1)} %get-tuple-element.155), channel_id=1, source_target_pairs={{0,3},{1,2},{2,1},{3,0},{4,7},{5,6},{6,5},{7,4},{8,11},{9,10},{10,... | collective-permute-start | bytes 331784 | tf_op jit(solution)/shard_map/ppermute | solution.py:416
  48.3 6.7 %collective-permute-start.16 = (bf16[256,1792]{1,0:T(8,128)(2,1)S(1)}, bf16[256,1792]{1,0:T(8,128)(2,1)S(1)}, u32[]{:S(2)}, u32[]{:S(2)}) collective-permute-start(bf16[256,1792]{1,0:T(8,128)(2,1)S(1)} %get-tuple-element.179.refs_2_), channel_id=1, source_target_pairs={{0,8},{1,9},{2,10},{3,11},{4,12},{5,13},{6,14},{7,15},{8,0},{9,1},... | collective-permute-start | bytes 2752520 | tf_op jit(solution)/shard_map/ppermute | solution.py:402
  50.5 2.0 %collective-permute-start.14 = (bf16[576,256]{1,0:T(8,128)(2,1)S(1)}, bf16[576,256]{1,0:T(8,128)(2,1)S(1)}, u32[]{:S(2)}, u32[]{:S(2)}) collective-permute-start(bf16[576,256]{1,0:T(8,128)(2,1)S(1)} %get-tuple-element.177), channel_id=1, source_target_pairs={{0,8},{1,9},{2,10},{3,11},{4,12},{5,13},{6,14},{7,15},{8,0},{9,1},... | collective-permute-start | bytes 884744 | tf_op jit(solution)/shard_map/ppermute | solution.py:402
  51.3 3.6 %collective-permute-start.18 = (bf16[1152,256]{1,0:T(8,128)(2,1)S(1)}, bf16[1152,256]{1,0:T(8,128)(2,1)S(1)}, u32[]{:S(2)}, u32[]{:S(2)}) collective-permute-start(bf16[1152,256]{1,0:T(8,128)(2,1)S(1)} %get-tuple-element.181), channel_id=1, source_target_pairs={{0,8},{1,9},{2,10},{3,11},{4,12},{5,13},{6,14},{7,15},{8,0},{9,1},... | collective-permute-start | bytes 1769480 | tf_op jit(solution)/shard_map/ppermute | solution.py:402
  51.4 3.5 %collective-permute-start.17 = (bf16[256,640]{1,0:T(8,128)(2,1)S(1)}, bf16[256,640]{1,0:T(8,128)(2,1)S(1)}, u32[]{:S(2)}, u32[]{:S(2)}) collective-permute-start(bf16[256,640]{1,0:T(8,128)(2,1)S(1)} %get-tuple-element.207.refs_6_.att_t), channel_id=1, source_target_pairs={{0,8},{1,9},{2,10},{3,11},{4,12},{5,13},{6,14},{7,15},{8,0},{9,1},... | collective-permute-start | bytes 983048 | tf_op jit(solution)/shard_map/ppermute | solution.py:402
  51.8 3.1 %collective-permute-start.19 = (bf16[256,640]{1,0:T(8,128)(2,1)S(1)}, bf16[256,640]{1,0:T(8,128)(2,1)S(1)}, u32[]{:S(2)}, u32[]{:S(2)}) collective-permute-start(bf16[256,640]{1,0:T(8,128)(2,1)S(1)} %get-tuple-element.182.refs_10_), channel_id=1, source_target_pairs={{0,8},{1,9},{2,10},{3,11},{4,12},{5,13},{6,14},{7,15},{8,0},{9,1},... | collective-permute-start | bytes 983048 | tf_op jit(solution)/shard_map/ppermute | solution.py:402
  52.5 2.3 %collective-permute-start.15 = (bf16[576,256]{1,0:T(8,128)(2,1)S(1)}, bf16[576,256]{1,0:T(8,128)(2,1)S(1)}, u32[]{:S(2)}, u32[]{:S(2)}) collective-permute-start(bf16[576,256]{1,0:T(8,128)(2,1)S(1)} %get-tuple-element.178), channel_id=1, source_target_pairs={{0,8},{1,9},{2,10},{3,11},{4,12},{5,13},{6,14},{7,15},{8,0},{9,1},... | collective-permute-start | bytes 884744 | tf_op jit(solution)/shard_map/ppermute | solution.py:402
  54.9 2.7 %collective-permute-start.20 = (bf16[256,1792]{1,0:T(8,128)(2,1)S(1)}, bf16[256,1792]{1,0:T(8,128)(2,1)S(1)}, u32[]{:S(2)}, u32[]{:S(2)}) collective-permute-start(bf16[256,1792]{1,0:T(8,128)(2,1)S(1)} %shard_map.132.refs_2_.qkv_grad), channel_id=1, source_target_pairs={{0,8},{1,9},{2,10},{3,11},{4,12},{5,13},{6,14},{7,15},{8,0},{9,1},... | collective-permute-start | bytes 2752520 | tf_op jit(solution)/shard_map/ppermute | solution.py:402
  59.1 14.3 %collective-permute-start.21 = (bf16[96,4608]{1,0:T(8,128)(2,1)S(1)}, bf16[96,4608]{1,0:T(8,128)(2,1)S(1)}, u32[]{:S(2)}, u32[]{:S(2)}) collective-permute-start(bf16[96,4608]{1,0:T(8,128)(2,1)S(1)} %get-tuple-element.215), channel_id=1, source_target_pairs={{0,96},{1,97},{2,98},{3,99},{4,100},{5,101},{6,102},{7,103},{8,40}... | collective-permute-start | bytes 2654216 | tf_op jit(solution)/shard_map/ppermute | solution.py:411
  61.9 14.5 %collective-permute-start.23 = (bf16[96,4608]{1,0:T(8,128)(2,1)S(1)}, bf16[96,4608]{1,0:T(8,128)(2,1)S(1)}, u32[]{:S(2)}, u32[]{:S(2)}) collective-permute-start(bf16[96,4608]{1,0:T(8,128)(2,1)S(1)} %get-tuple-element.219), channel_id=1, source_target_pairs={{0,20},{1,21},{2,22},{3,23},{4,16},{5,17},{6,18},{7,19},{8,12},{9,... | collective-permute-start | bytes 2654216 | tf_op jit(solution)/shard_map/ppermute | solution.py:411
  64.7 14.3 %collective-permute-start.25 = (bf16[96,4608]{1,0:T(8,128)(2,1)S(1)}, bf16[96,4608]{1,0:T(8,128)(2,1)S(1)}, u32[]{:S(2)}, u32[]{:S(2)}) collective-permute-start(bf16[96,4608]{1,0:T(8,128)(2,1)S(1)} %get-tuple-element.223), channel_id=1, source_target_pairs={{0,3},{1,2},{2,1},{3,0},{4,7},{5,6},{6,5},{7,4},{8,9},{9,8},{10,11... | collective-permute-start | bytes 2654216 | tf_op jit(solution)/shard_map/ppermute | solution.py:411
  73.6 9.6 %collective-permute-start.22 = (bf16[48,4608]{1,0:T(8,128)(2,1)S(1)}, bf16[48,4608]{1,0:T(8,128)(2,1)S(1)}, u32[]{:S(2)}, u32[]{:S(2)}) collective-permute-start(bf16[48,4608]{1,0:T(8,128)(2,1)S(1)} %get-tuple-element.217), channel_id=1, source_target_pairs={{0,20},{1,21},{2,22},{3,23},{4,16},{5,17},{6,18},{7,19},{8,12},{9,... | collective-permute-start | bytes 1327112 | tf_op jit(solution)/shard_map/ppermute | solution.py:411
  76.6 9.6 %collective-permute-start.24 = (bf16[48,4608]{1,0:T(8,128)(2,1)S(1)}, bf16[48,4608]{1,0:T(8,128)(2,1)S(1)}, u32[]{:S(2)}, u32[]{:S(2)}) collective-permute-start(bf16[48,4608]{1,0:T(8,128)(2,1)S(1)} %get-tuple-element.221), channel_id=1, source_target_pairs={{0,3},{1,2},{2,1},{3,0},{4,7},{5,6},{6,5},{7,4},{8,9},{9,8},{10,11... | collective-permute-start | bytes 1327112 | tf_op jit(solution)/shard_map/ppermute | solution.py:411
  79.1 10.0 %collective-permute-start.26 = (bf16[48,4608]{1,0:T(8,128)(2,1)S(1)}, bf16[48,4608]{1,0:T(8,128)(2,1)S(1)}, u32[]{:S(2)}, u32[]{:S(2)}) collective-permute-start(bf16[48,4608]{1,0:T(8,128)(2,1)S(1)} %get-tuple-element.225), channel_id=1, source_target_pairs={{0,96},{1,97},{2,98},{3,99},{4,100},{5,101},{6,102},{7,103},{8,40}... | collective-permute-start | bytes 1327112 | tf_op jit(solution)/shard_map/ppermute | solution.py:411
  83.2 8.4 %collective-permute-start.27 = (bf16[24,4608]{1,0:T(8,128)(2,1)S(1)}, bf16[24,4608]{1,0:T(8,128)(2,1)S(1)}, u32[]{:S(2)}, u32[]{:S(2)}) collective-permute-start(bf16[24,4608]{1,0:T(8,128)(2,1)S(1)} %get-tuple-element.227), channel_id=1, source_target_pairs={{0,3},{1,2},{2,1},{3,0},{4,7},{5,6},{6,5},{7,4},{8,9},{9,8},{10,11... | collective-permute-start | bytes 663560 | tf_op jit(solution)/shard_map/ppermute | solution.py:411
  86.3 8.4 %collective-permute-start.28 = (bf16[24,4608]{1,0:T(8,128)(2,1)S(1)}, bf16[24,4608]{1,0:T(8,128)(2,1)S(1)}, u32[]{:S(2)}, u32[]{:S(2)}) collective-permute-start(bf16[24,4608]{1,0:T(8,128)(2,1)S(1)} %get-tuple-element.228), channel_id=1, source_target_pairs={{0,96},{1,97},{2,98},{3,99},{4,100},{5,101},{6,102},{7,103},{8,40}... | collective-permute-start | bytes 663560 | tf_op jit(solution)/shard_map/ppermute | solution.py:411
  89.2 8.0 %collective-permute-start.29 = (bf16[24,4608]{1,0:T(8,128)(2,1)S(1)}, bf16[24,4608]{1,0:T(8,128)(2,1)S(1)}, u32[]{:S(2)}, u32[]{:S(2)}) collective-permute-start(bf16[24,4608]{1,0:T(8,128)(2,1)S(1)} %get-tuple-element.229), channel_id=1, source_target_pairs={{0,20},{1,21},{2,22},{3,23},{4,16},{5,17},{6,18},{7,19},{8,12},{9,... | collective-permute-start | bytes 663560 | tf_op jit(solution)/shard_map/ppermute | solution.py:411
  97.6 5.1 %collective-permute-start.30 = (bf16[3,13824]{1,0:T(4,128)(2,1)S(1)}, bf16[3,13824]{1,0:T(4,128)(2,1)S(1)}, u32[]{:S(2)}, u32[]{:S(2)}) collective-permute-start(bf16[3,13824]{1,0:T(4,128)(2,1)S(1)} %get-tuple-element.231), channel_id=1, source_target_pairs={{0,32},{1,33},{2,34},{3,35},{4,36},{5,37},{6,38},{7,39},{8,104},{9... | collective-permute-start | bytes 248840 | tf_op jit(solution)/shard_map/ppermute | solution.py:427
  97.7 5.0 %collective-permute-start.31 = (bf16[3,13824]{1,0:T(4,128)(2,1)S(1)}, bf16[3,13824]{1,0:T(4,128)(2,1)S(1)}, u32[]{:S(2)}, u32[]{:S(2)}) collective-permute-start(bf16[3,13824]{1,0:T(4,128)(2,1)S(1)} %get-tuple-element.232), channel_id=1, source_target_pairs={{0,4},{1,5},{2,6},{3,7},{4,0},{5,1},{6,2},{7,3},{8,28},{9,29},{10,... | collective-permute-start | bytes 248840 | tf_op jit(solution)/shard_map/ppermute | solution.py:427
  97.8 9.2 %collective-permute-start.32 = (bf16[3,13824]{1,0:T(4,128)(2,1)S(1)}, bf16[3,13824]{1,0:T(4,128)(2,1)S(1)}, u32[]{:S(2)}, u32[]{:S(2)}) collective-permute-start(bf16[3,13824]{1,0:T(4,128)(2,1)S(1)} %get-tuple-element.233), channel_id=1, source_target_pairs={{0,1},{1,0},{2,3},{3,2},{4,5},{5,4},{6,7},{7,6},{8,11},{9,10},{10,... | collective-permute-start | bytes 248840 | tf_op jit(solution)/shard_map/ppermute | solution.py:427
  97.9 9.2 %collective-permute-start.33 = (bf16[3,13824]{1,0:T(4,128)(2,1)S(1)}, bf16[3,13824]{1,0:T(4,128)(2,1)S(1)}, u32[]{:S(2)}, u32[]{:S(2)}) collective-permute-start(bf16[3,13824]{1,0:T(4,128)(2,1)S(1)} %get-tuple-element.234), channel_id=1, source_target_pairs={{0,36},{1,37},{2,38},{3,39},{4,32},{5,33},{6,34},{7,35},{8,124},{9... | collective-permute-start | bytes 248840 | tf_op jit(solution)/shard_map/ppermute | solution.py:427
  101.1 5.9 %collective-permute-start.34 = (bf16[3,13824]{1,0:T(4,128)(2,1)S(1)}, bf16[3,13824]{1,0:T(4,128)(2,1)S(1)}, u32[]{:S(2)}, u32[]{:S(2)}) collective-permute-start(bf16[3,13824]{1,0:T(4,128)(2,1)S(1)} %get-tuple-element.235), channel_id=1, source_target_pairs={{0,33},{1,32},{2,35},{3,34},{4,37},{5,36},{6,39},{7,38},{8,107},{9... | collective-permute-start | bytes 248840 | tf_op jit(solution)/shard_map/ppermute | solution.py:427
  102.7 5.6 %collective-permute-start.35 = (bf16[3,13824]{1,0:T(4,128)(2,1)S(1)}, bf16[3,13824]{1,0:T(4,128)(2,1)S(1)}, u32[]{:S(2)}, u32[]{:S(2)}) collective-permute-start(bf16[3,13824]{1,0:T(4,128)(2,1)S(1)} %get-tuple-element.236), channel_id=1, source_target_pairs={{0,5},{1,4},{2,7},{3,6},{4,1},{5,0},{6,3},{7,2},{8,31},{9,30},{10,... | collective-permute-start | bytes 248840 | tf_op jit(solution)/shard_map/ppermute | solution.py:427
  102.7 7.0 %collective-permute-start.36 = (bf16[3,13824]{1,0:T(4,128)(2,1)S(1)}, bf16[3,13824]{1,0:T(4,128)(2,1)S(1)}, u32[]{:S(2)}, u32[]{:S(2)}) collective-permute-start(bf16[3,13824]{1,0:T(4,128)(2,1)S(1)} %get-tuple-element.237), channel_id=1, source_target_pairs={{0,37},{1,36},{2,39},{3,38},{4,33},{5,32},{6,35},{7,34},{8,127},{9... | collective-permute-start | bytes 248840 | tf_op jit(solution)/shard_map/ppermute | solution.py:427
